TPU v7x, 32 devices: a whole 2x2x4 slice. The times are simulated.
32 devices in a mesh: dp: 8 (over z, core), mp: 4 (over y, x).
Axes of the slice: x: 2, y: 2, z: 4, core: 2. Of those that a mesh axis runs over, the one named last changes fastest.
Arguments:
- tokens: bfloat16 [7680, 2048], P('dp'), may hold values from -6 to 6
- segment_ids: int32 [8, 960], P('dp'), may hold values from 0 to 3, never falling along the last dimension, each value on 1 to 480 neighbouring positions
- cotangent: bfloat16 [7680, 2048], P(('dp', 'mp')), may hold values from -6 to 6
- gain_in: float32 [2048], replicated, may hold values from 0.5 to 1.5
- w_in: bfloat16 [2048, 2048], P('dp'), may hold values from -0.125 to 0.125
- w_forget: bfloat16 [2048, 2048], P('dp'), may hold values from -0.125 to 0.125
- w_outgate: bfloat16 [2048, 2048], P('dp'), may hold values from -0.125 to 0.125
- bound_logit: float32 [1024], replicated, may hold values from -1 to 3
- gain_mix: float32 [2048], replicated, may hold values from 0.5 to 1.5
- w_mix: bfloat16 [2048, 2048], P('dp'), may hold values from -0.125 to 0.125
- gain_ffn: float32 [2048], replicated, may hold values from 0.5 to 1.5
- w_gate: bfloat16 [2048, 5632], P('dp', 'mp'), may hold values from -0.125 to 0.125
- w_up: bfloat16 [2048, 5632], P('dp', 'mp'), may hold values from -0.125 to 0.125
- w_down: bfloat16 [5632, 2048], P('mp', 'dp'), may hold values from -0.078125 to 0.078125
Outputs:
- mixed: bfloat16 [7680, 2048], P(('dp', 'mp'))
- grad_tokens: float32 [7680, 2048], P(('dp', 'mp'))
- grad_gain_in: float32 [2048], P('dp')
- grad_w_in: float32 [2048, 2048], P('dp')
- grad_w_forget: float32 [2048, 2048], P('dp')
- grad_w_outgate: float32 [2048, 2048], P('dp')
- grad_bound: float32 [1024], P('dp')
- grad_gain_mix: float32 [2048], P('dp')
- grad_w_mix: float32 [2048, 2048], P('dp')
- grad_gain_ffn: float32 [2048], P('dp')
- grad_w_gate: float32 [2048, 5632], P('dp', 'mp')
- grad_w_up: float32 [2048, 5632], P('dp', 'mp')
- grad_w_down: float32 [5632, 2048], P('mp', 'dp')
Inputs may be any that keep to these rules, and one draw needn't show every extreme that they name: `segment_ids`: within each row ids never fall; 4 sequences, each 1 to 480 tokens, one exactly 480.
All inputs are finite; a program needn't handle non-finite values.
Results may differ from a plain program's by a relative error of at most 0.012.
The roundings to bfloat16 on the way count: a program that leaves them out, or rounds other values in their place, can miss the bound.
Values may be sent and summed in bfloat16 or wider, within the bound.
A program may use at most 384 MiB of HBM per device.

v0:
```python
import jax
import jax.numpy as jnp
from jax import lax
from jax.sharding import PartitionSpec as P

epsilon = 1e-06


def root_norm(values, gain):
    return values * lax.rsqrt(jnp.mean(values * values, axis=-1, keepdims=True) + epsilon) * gain


def combine(former, latter):
    decay_re = latter[0] * former[0] - latter[1] * former[1]
    decay_im = latter[0] * former[1] + latter[1] * former[0]
    state_re = latter[0] * former[2] - latter[1] * former[3] + latter[2]
    state_im = latter[0] * former[3] + latter[1] * former[2] + latter[3]
    return (decay_re, decay_im, state_re, state_im)


def recurrent_mix(proj_in, proj_forget, proj_gate, gain_mix, bound_logit, starts):
    half_width = proj_forget.shape[1] // 2
    low_bound = jax.nn.sigmoid(bound_logit)
    forget = low_bound + (1.0 - low_bound) * jax.nn.sigmoid(proj_forget[:, :half_width])
    phase_angle = proj_forget[:, half_width:]
    carry_on = (1.0 - starts)[:, None]
    decay_re = forget * jnp.cos(phase_angle) * carry_on
    decay_im = forget * jnp.sin(phase_angle) * carry_on
    inflow = 1.0 - forget
    input_re = jax.nn.silu(proj_in[:, :half_width]) * inflow
    input_im = jax.nn.silu(proj_in[:, half_width:]) * inflow
    scanned = lax.associative_scan(combine, (decay_re, decay_im, input_re, input_im), axis=0)
    states = jnp.concatenate([scanned[2], scanned[3]], axis=1)
    return root_norm(states, gain_mix) * jax.nn.silu(proj_gate)


def forward_dot(left, right):
    return jnp.dot(left, right, preferred_element_type=jnp.float32)


def dot_trans(left, right):
    return lax.dot_general(
        left, right, (((1,), (1,)), ((), ())), preferred_element_type=jnp.float32
    )


def dot_rows(left, right):
    return lax.dot_general(
        left, right, (((0,), (0,)), ((), ())), preferred_element_type=jnp.float32
    )


def per_device(
    tokens,
    segment_ids,
    cotangent,
    gain_in,
    w_in,
    w_forget,
    w_outgate,
    bound_logit,
    gain_mix,
    w_mix,
    gain_ffn,
    w_gate,
    w_up,
    w_down,
):
    gathered = (
        lax.all_gather(w_in, "dp", axis=0, tiled=True),
        lax.all_gather(w_forget, "dp", axis=0, tiled=True),
        lax.all_gather(w_outgate, "dp", axis=0, tiled=True),
        lax.all_gather(w_mix, "dp", axis=0, tiled=True),
        lax.all_gather(w_gate, "dp", axis=0, tiled=True),
        lax.all_gather(w_up, "dp", axis=0, tiled=True),
        lax.all_gather(w_down, "dp", axis=1, tiled=True),
    )
    stream = tokens.astype(jnp.float32)
    ident = segment_ids[0]
    previous = jnp.concatenate([ident[:1] - 1, ident[:-1]])
    starts = jnp.where(ident != previous, 1.0, 0.0).astype(jnp.float32)
    row_count = stream.shape[0] // lax.axis_size("mp")
    first_row = lax.axis_index("mp") * row_count
    normed_val, norm_in_back = jax.vjp(root_norm, stream, gain_in)
    normed = normed_val.astype(jnp.bfloat16)
    proj_in = forward_dot(normed, gathered[0])
    proj_forget = forward_dot(normed, gathered[1])
    proj_gate = forward_dot(normed, gathered[2])

    def mixer_fn(part_in, part_forget, part_gate, gain_part, bound_part):
        return recurrent_mix(part_in, part_forget, part_gate, gain_part, bound_part, starts)

    mixer_val, mixer_back = jax.vjp(
        mixer_fn, proj_in, proj_forget, proj_gate, gain_mix, bound_logit
    )
    mixer_out = mixer_val.astype(jnp.bfloat16)
    middle = stream + forward_dot(mixer_out, gathered[3])
    ffn_val, norm_ffn_back = jax.vjp(root_norm, middle, gain_ffn)
    ffn_in = ffn_val.astype(jnp.bfloat16)
    gate_val = forward_dot(ffn_in, gathered[4])
    up_val = forward_dot(ffn_in, gathered[5])
    hidden = (jax.nn.silu(gate_val) * up_val).astype(jnp.bfloat16)
    down_weight = gathered[6]
    down_share = lax.psum_scatter(
        forward_dot(hidden, down_weight), "mp", scatter_dimension=0, tiled=True
    )
    middle_share = lax.dynamic_slice_in_dim(middle, first_row, row_count, 0)
    mixed = (middle_share + down_share).astype(jnp.bfloat16)
    grad_out = lax.all_gather(cotangent, "mp", axis=0, tiled=True)
    grad_hidden = dot_trans(grad_out, gathered[6])
    grad_down = dot_rows(hidden, grad_out)
    sig_gate = jax.nn.sigmoid(gate_val)
    grad_gate = (grad_hidden * up_val * sig_gate * (1.0 + gate_val * (1.0 - sig_gate))).astype(
        jnp.bfloat16
    )
    grad_up = (grad_hidden * gate_val * sig_gate).astype(jnp.bfloat16)
    grad_wgate = dot_rows(ffn_in, grad_gate)
    grad_wup = dot_rows(ffn_in, grad_up)
    grad_ffn_part = dot_trans(grad_gate, gathered[4]) + dot_trans(grad_up, gathered[5])
    grad_ffn_in = lax.psum(grad_ffn_part, "mp")
    grad_middle_norm, grad_gain_ffn = norm_ffn_back(grad_ffn_in)
    grad_middle = grad_out.astype(jnp.float32) + grad_middle_norm
    grad_branch = grad_middle.astype(jnp.bfloat16)
    grad_mixer = dot_trans(grad_branch, gathered[3])
    grad_pin, grad_pforget, grad_pgate, grad_gain_mix, grad_bound = mixer_back(grad_mixer)
    grad_pin = grad_pin.astype(jnp.bfloat16)
    grad_pforget = grad_pforget.astype(jnp.bfloat16)
    grad_pgate = grad_pgate.astype(jnp.bfloat16)
    grad_win = dot_rows(normed, grad_pin)
    grad_wforget = dot_rows(normed, grad_pforget)
    grad_woutgate = dot_rows(normed, grad_pgate)
    grad_wmix = dot_rows(mixer_out, grad_branch)
    grad_normed = (
        dot_trans(grad_pin, gathered[0])
        + dot_trans(grad_pforget, gathered[1])
        + dot_trans(grad_pgate, gathered[2])
    )
    grad_stream_norm, grad_gain_in = norm_in_back(grad_normed)
    grad_stream = grad_middle + grad_stream_norm
    grad_tokens = lax.dynamic_slice_in_dim(grad_stream, first_row, row_count, 0)
    summed = (
        lax.psum_scatter(grad_win, "dp", scatter_dimension=0, tiled=True),
        lax.psum_scatter(grad_wforget, "dp", scatter_dimension=0, tiled=True),
        lax.psum_scatter(grad_woutgate, "dp", scatter_dimension=0, tiled=True),
        lax.psum_scatter(grad_wmix, "dp", scatter_dimension=0, tiled=True),
        lax.psum_scatter(grad_gain_in, "dp", scatter_dimension=0, tiled=True),
        lax.psum_scatter(grad_gain_mix, "dp", scatter_dimension=0, tiled=True),
        lax.psum_scatter(grad_bound, "dp", scatter_dimension=0, tiled=True),
        lax.psum_scatter(grad_wgate, "dp", scatter_dimension=0, tiled=True),
        lax.psum_scatter(grad_wup, "dp", scatter_dimension=0, tiled=True),
        lax.psum_scatter(grad_down, "dp", scatter_dimension=1, tiled=True),
        lax.psum_scatter(grad_gain_ffn, "dp", scatter_dimension=0, tiled=True),
    )
    (
        out_win,
        out_wforget,
        out_woutgate,
        out_wmix,
        out_gin,
        out_gmix,
        out_bound,
        out_wgate,
        out_wup,
        out_wdown,
        out_gffn,
    ) = summed
    return (
        mixed,
        grad_tokens,
        out_gin,
        out_win,
        out_wforget,
        out_woutgate,
        out_bound,
        out_gmix,
        out_wmix,
        out_gffn,
        out_wgate,
        out_wup,
        out_wdown,
    )


def solution(mesh):
    placed = (
        P("dp", None),
        P("dp", None),
        P(("dp", "mp"), None),
        P(),
        P("dp", None),
        P("dp", None),
        P("dp", None),
        P(),
        P(),
        P("dp", None),
        P(),
        P("dp", "mp"),
        P("dp", "mp"),
        P("mp", "dp"),
    )
    return jax.shard_map(
        per_device,
        mesh=mesh,
        in_specs=placed,
        out_specs=(
            P(("dp", "mp"), None),
            P(("dp", "mp"), None),
            P("dp"),
            P("dp", None),
            P("dp", None),
            P("dp", None),
            P("dp"),
            P("dp"),
            P("dp", None),
            P("dp"),
            P("dp", "mp"),
            P("dp", "mp"),
            P("mp", "dp"),
        ),
        check_vma=False,
    )
```

profile of v0, /device:TPU:8, one launch (start us, length us, event | category | flops | bytes accessed | tf_op | source)
XLA Modules:
  0.0 2182.9 jit_solution(14483882200202164905)
XLA Ops:
  17.0 73.2 %all-gather.11.cloned.1.call-done = bf16[2048,2048]{1,0:T(8,128)(2,1)} async-done(((bf16[256,2048]{1,0:T(8,128)(2,1)}), bf16[2048,2048]{1,0:T(8,128)(2,1)}) %all-gather.11.cloned.1.call-update) | async-done | bytes 8388624 | tf_op jit(solution)/shard_map/all_gather | solution.py:71
  90.2 14.1 fusion.40
  104.3 68.2 %all-gather.9.cloned.1.call-done = bf16[2048,2048]{1,0:T(8,128)(2,1)} async-done(((bf16[256,2048]{1,0:T(8,128)(2,1)}), bf16[2048,2048]{1,0:T(8,128)(2,1)}) %all-gather.9.cloned.1.call-update) | async-done | bytes 8388624 | tf_op jit(solution)/shard_map/all_gather | solution.py:70
  172.4 12.1 fusion.41
  184.6 18.9 multiply_multiply_fusion.1
  276.5 11.0 multiply_subtract_fusion
  478.6 9.6 slice.695
  631.4 10.3 pad.687
  665.3 10.5 pad.686
  675.8 10.4 pad.689
  707.2 17.9 multiply_convert_fusion.1
  725.1 12.7 multiply_reduce_fusion.6
  743.7 11.2 fusion.56
  754.9 11.2 fusion.57
  766.1 15.4 multiply_convert_fusion.3
  781.5 10.2 fusion.59
  800.2 10.2 fusion.58
  810.4 12.0 fusion.60
  822.5 11.8 fusion.61
  834.4 10.5 fusion.62
  845.0 120.8 %all-reduce.187.cloned.1.call-done = f32[960,2048]{1,0:T(8,128)} async-done(((f32[960,2048]{1,0:T(8,128)}), f32[960,2048]{1,0:T(8,128)}) %all-reduce.187.cloned.1.call-update) | async-done | bytes 7864336 | tf_op jit(solution)/shard_map/psum | solution.py:120
  984.4 22.9 %multiply_reduce_fusion.1 = (f32[2048]{0:T(1024)}, f32[960]{0:T(1024)S(1)}, bf16[960,2048]{1,0:T(8,128)(2,1)}, f32[960,2048]{1,0:T(8,128)}) fusion(f32[960]{0:T(1024)S(1)} %copy-done.221, f32[960,1024]{1,0:T(8,128)S(1)} %copy-done.6, f32[960,1024]{1,0:T(8,128)S(1)} %copy-done.4, f32[960,2048]{1,0:T(8,128)} %get-tuple-element.317, f32[2048]{0:T(1024)S(1)} %copy-done.226, ...), kind=kOutput, calls=%fused_computation.9 | convolution fusion | flops 8096314368 | bytes 43802112 | tf_op jit(solution)/shard_map/dot_general | solution.py:42
  1007.3 10.0 add_add_fusion
  1017.3 14.1 fusion.44
  1304.1 15.1 multiply_add_fusion.7
  1319.2 10.4 pad.794
  1329.6 10.6 pad.803
  1340.2 11.0 multiply_add_fusion.9
  1351.2 10.6 pad.799
  1361.8 10.5 pad.804
  1378.6 10.5 pad.856
  1395.4 10.5 pad.853
  1405.9 10.7 pad.692
  1423.0 10.7 pad.806
  1440.1 23.3 %multiply_reduce_fusion.9 = (f32[1024]{0:T(1024)S(1)}, f32[1024]{0:T(1024)S(1)}, f32[960,1024]{1,0:T(8,128)S(1)}, f32[960,1024]{1,0:T(8,128)S(1)}, f32[960,1024]...) fusion(f32[960,2048]{1,0:T(8,128)} %fusion.40, f32[960,2048]{1,0:T(8,128)} %copy-done.2, ...), kind=kLoop, calls=%fused_computation.43 | loop fusion | flops 33421312 | bytes 82595584 | tf_op jit(solution)/shard_map/transpose(jvp())/reduce_sum | solution.py:24
  1463.5 22.6 %fusion.6 = (f32[960,1024]{1,0:T(8,128)}, f32[960,1024]{1,0:T(8,128)}, f32[960,1024]{1,0:T(8,128)}, f32[960,1024]{1,0:T(8,128)}) fusion(f32[960,1024]{1,0:T(8,128)} %get-tuple-element.28, f32[960,2048]{1,0:T(8,128)} %copy-done.2, f32[1024]{0:T(1024)S(1)} %copy-done.207, f32[1024]{0:T(1024)S(1)} %copy-done.205, f32[960,2048]{1,0:T(8,128)} %fusion.40, ...), kind=kLoop, calls=%fused_computation.35 | loop fusion | flops 35389440 | bytes 51126272 | tf_op jit(solution)/shard_map/transpose(jvp(jit(silu)))/add_any | solution.py:31
  1486.1 15.6 fusion.23
  1501.7 16.8 fusion.21
  1518.6 15.7 fusion.16
  1534.3 15.7 fusion.38
  1558.3 15.2 fusion.24
  1573.5 13.0 fusion.22
  1586.6 19.9 multiply_reduce_fusion.2
  1606.5 26.8 %all-reduce.184 = (f32[2048]{0:T(1024)S(1)}, f32[1024]{0:T(1024)S(1)}, f32[2048]{0:T(1024)S(1)}, f32[2048]{0:T(1024)S(1)}) all-reduce(f32[2048]{0:T(1024)S(1)} %get-tuple-element.19, f32[1024]{0:T(1024)S(1)} %multiply_multiply_fusion.2, f32[2048]{0:T(1024)S(1)} %copy-done.227, ...), channel_id=3, replica_groups=mesh['dp'=8,'mp'=4] {'dp'}, use_global_device_ids=true, to_apply=%region_9.10.clone | all-reduce | flops 7168 | bytes 57344
  1643.8 23.9 %reduce-scatter.13.cloned.1.call-done = f32[256,2048]{1,0:T(8,128)} async-done(((f32[2048,2048]{1,0:T(8,128)}), f32[256,2048]{1,0:T(8,128)}) %reduce-scatter.13.cloned.1.call-update) | async-done | bytes 2097168 | tf_op jit(solution)/shard_map/reduce_scatter | solution.py:143
  1667.7 169.4 %reduce-scatter.11.cloned.1.call-done = f32[256,2048]{1,0:T(8,128)} async-done(((f32[2048,2048]{1,0:T(8,128)}), f32[256,2048]{1,0:T(8,128)}) %reduce-scatter.11.cloned.1.call-update) | async-done | bytes 2097168 | tf_op jit(solution)/shard_map/reduce_scatter | solution.py:142
  1837.1 169.4 %reduce-scatter.17.cloned.1.call-done = f32[256,2048]{1,0:T(8,128)} async-done(((f32[2048,2048]{1,0:T(8,128)}), f32[256,2048]{1,0:T(8,128)}) %reduce-scatter.17.cloned.1.call-update) | async-done | bytes 2097168 | tf_op jit(solution)/shard_map/reduce_scatter | solution.py:145
  2006.5 169.4 %reduce-scatter.15.cloned.1.call-done = f32[256,2048]{1,0:T(8,128)} async-done(((f32[2048,2048]{1,0:T(8,128)}), f32[256,2048]{1,0:T(8,128)}) %reduce-scatter.15.cloned.1.call-update) | async-done | bytes 2097168 | tf_op jit(solution)/shard_map/reduce_scatter | solution.py:144
  (945 shorter events, 806.9 us)
Async XLA Ops:
  7.2 83.0 %all-gather.11.cloned.1.call-start = ((), (), s32[]{:S(2)}) async-start(), calls=%async_computation.9 | async-start | bytes 9437184 | tf_op jit(solution)/shard_map/all_gather | solution.py:71
  7.9 164.5 %all-gather.9.cloned.1.call-start = ((), (), s32[]{:S(2)}) async-start(), calls=%async_computation.8 | async-start | bytes 9437184 | tf_op jit(solution)/shard_map/all_gather | solution.py:70
  8.7 698.5 %all-gather.13.cloned.1.call-start = ((), (), s32[]{:S(2)}) async-start(), calls=%async_computation.10 | async-start | bytes 9437184 | tf_op jit(solution)/shard_map/all_gather | solution.py:72
  9.4 80.8 %copy-start.232 = (f32[2048]{0:T(1024)S(1)}, f32[2048]{0:T(1024)}, u32[]{:S(2)}) copy-start(f32[2048]{0:T(1024)} %param.17) | copy-start | bytes 24580
  9.4 715.7 %all-gather.15.cloned.1.call-start = ((), (), s32[]{:S(2)}) async-start(), calls=%async_computation.11 | async-start | bytes 9437184 | tf_op jit(solution)/shard_map/all_gather | solution.py:73
  10.0 733.7 %all-gather.17.cloned.1.call-start = ((), (), s32[]{:S(2)}) async-start(), calls=%async_computation.12 | async-start | bytes 6488064 | tf_op jit(solution)/shard_map/all_gather | solution.py:74
  10.6 744.3 %all-gather.19.cloned.1.call-start = ((), (), s32[]{:S(2)}) async-start(), calls=%async_computation.13 | async-start | bytes 6488064 | tf_op jit(solution)/shard_map/all_gather | solution.py:75
  11.2 754.9 %all-gather.23.cloned.1.call-start = ((), (), s32[]{:S(2)}) async-start(), calls=%async_computation.16 | async-start | bytes 4915200 | tf_op jit(solution)/shard_map/all_gather | solution.py:109
  11.9 754.2 %all-gather.21.cloned.1.call-start = ((), (), s32[]{:S(2)}) async-start(), calls=%async_computation.14 | async-start | bytes 6488064 | tf_op jit(solution)/shard_map/all_gather | solution.py:76
  12.7 953.1 %all-reduce.187.cloned.1.call-start = ((), (), s32[]{:S(2)}) async-start(), calls=%async_computation.17 | async-start | bytes 15728640 | tf_op jit(solution)/shard_map/psum | solution.py:120
  15.7 156.7 %copy-start.228 = (f32[960]{0:T(1024)}, f32[960]{0:T(1024)S(1)}, u32[]{:S(2)}) copy-start(f32[960]{0:T(1024)S(1)} %fusion.31) | copy-start | bytes 11524
  15.7 168.8 %copy-start.204 = (f32[1024]{0:T(1024)}, f32[1024]{0:T(1024)S(1)}, u32[]{:S(2)}) copy-start(f32[1024]{0:T(1024)S(1)} %get-tuple-element.314) | copy-start | bytes 12292
  15.7 168.8 %copy-start.206 = (f32[1024]{0:T(1024)}, f32[1024]{0:T(1024)S(1)}, u32[]{:S(2)}) copy-start(f32[1024]{0:T(1024)S(1)} %get-tuple-element.315) | copy-start | bytes 12292
  17.0 167.6 %copy-start.200 = (f32[960]{0:T(1024)}, f32[960]{0:T(1024)S(1)}, u32[]{:S(2)}) copy-start(f32[960]{0:T(1024)S(1)} %select_subtract_fusion) | copy-start | bytes 11524
  211.5 65.0 %copy-start.7 = (f32[480,1024]{1,0:T(8,128)}, f32[480,1024]{1,0:T(8,128)S(1)}, u32[]{:S(2)}) copy-start(f32[480,1024]{1,0:T(8,128)S(1)} %slice.576) | copy-start | bytes 5898244
  364.1 64.6 %copy-start.104 = (f32[30,1024]{1,0:T(8,128)}, f32[30,1024]{1,0:T(8,128)S(1)}, u32[]{:S(2)}) copy-start(f32[30,1024]{1,0:T(8,128)S(1)} %slice.610) | copy-start | bytes 368644
  367.6 65.4 %copy-start.106 = (f32[30,1024]{1,0:T(8,128)}, f32[30,1024]{1,0:T(8,128)S(1)}, u32[]{:S(2)}) copy-start(f32[30,1024]{1,0:T(8,128)S(1)} %slice.616) | copy-start | bytes 368644
  367.7 67.0 %copy-start.108 = (f32[30,1024]{1,0:T(8,128)}, f32[30,1024]{1,0:T(8,128)S(1)}, u32[]{:S(2)}) copy-start(f32[30,1024]{1,0:T(8,128)S(1)} %slice.617) | copy-start | bytes 368644
  367.8 66.9 %copy-start.110 = (f32[30,1024]{1,0:T(8,128)}, f32[30,1024]{1,0:T(8,128)S(1)}, u32[]{:S(2)}) copy-start(f32[30,1024]{1,0:T(8,128)S(1)} %slice.613) | copy-start | bytes 368644
  367.8 66.9 %copy-start.92 = (f32[120,1024]{1,0:T(8,128)S(1)}, f32[120,1024]{1,0:T(8,128)}, u32[]{:S(2)}) copy-start(f32[120,1024]{1,0:T(8,128)} %get-tuple-element.193) | copy-start | bytes 1474564
  368.5 67.1 %copy-start.93 = (f32[120,1024]{1,0:T(8,128)S(1)}, f32[120,1024]{1,0:T(8,128)}, u32[]{:S(2)}) copy-start(f32[120,1024]{1,0:T(8,128)} %get-tuple-element.194) | copy-start | bytes 1474564
  370.5 58.2 %copy-start.121 = (f32[60,1024]{1,0:T(8,128)S(1)}, f32[60,1024]{1,0:T(8,128)}, u32[]{:S(2)}) copy-start(f32[60,1024]{1,0:T(8,128)} %copy-done.120) | copy-start | bytes 737284
  370.5 58.9 %copy-start.123 = (f32[60,1024]{1,0:T(8,128)S(1)}, f32[60,1024]{1,0:T(8,128)}, u32[]{:S(2)}) copy-start(f32[60,1024]{1,0:T(8,128)} %copy-done.122) | copy-start | bytes 737284
  371.5 65.5 %copy-start.142 = (f32[15,1024]{1,0:T(8,128)}, f32[15,1024]{1,0:T(8,128)S(1)}, u32[]{:S(2)}) copy-start(f32[15,1024]{1,0:T(8,128)S(1)} %slice.620) | copy-start | bytes 184324
  374.0 41.8 %copy-start.154 = (f32[15,1024]{1,0:T(8,128)}, f32[15,1024]{1,0:T(8,128)S(1)}, u32[]{:S(2)}) copy-start(f32[15,1024]{1,0:T(8,128)S(1)} %slice.619) | copy-start | bytes 184324
  375.0 62.0 %copy-start.144 = (f32[15,1024]{1,0:T(8,128)}, f32[15,1024]{1,0:T(8,128)S(1)}, u32[]{:S(2)}) copy-start(f32[15,1024]{1,0:T(8,128)S(1)} %slice.626) | copy-start | bytes 184324
  375.9 61.1 %copy-start.156 = (f32[15,1024]{1,0:T(8,128)}, f32[15,1024]{1,0:T(8,128)S(1)}, u32[]{:S(2)}) copy-start(f32[15,1024]{1,0:T(8,128)S(1)} %slice.621) | copy-start | bytes 184324
  376.9 60.1 %copy-start.146 = (f32[15,1024]{1,0:T(8,128)}, f32[15,1024]{1,0:T(8,128)S(1)}, u32[]{:S(2)}) copy-start(f32[15,1024]{1,0:T(8,128)S(1)} %slice.627) | copy-start | bytes 184324
  377.9 59.2 %copy-start.148 = (f32[15,1024]{1,0:T(8,128)}, f32[15,1024]{1,0:T(8,128)S(1)}, u32[]{:S(2)}) copy-start(f32[15,1024]{1,0:T(8,128)S(1)} %slice.623) | copy-start | bytes 184324
  381.0 56.0 %copy-start.167 = (f32[7,1024]{1,0:T(8,128)}, f32[7,1024]{1,0:T(8,128)S(1)}, u32[]{:S(2)}) copy-start(f32[7,1024]{1,0:T(8,128)S(1)} %slice.630) | copy-start | bytes 86020
  384.0 53.1 %copy-start.169 = (f32[7,1024]{1,0:T(8,128)}, f32[7,1024]{1,0:T(8,128)S(1)}, u32[]{:S(2)}) copy-start(f32[7,1024]{1,0:T(8,128)S(1)} %slice.636) | copy-start | bytes 86020
  386.3 50.8 %copy-start.171 = (f32[7,1024]{1,0:T(8,128)}, f32[7,1024]{1,0:T(8,128)S(1)}, u32[]{:S(2)}) copy-start(f32[7,1024]{1,0:T(8,128)S(1)} %slice.637) | copy-start | bytes 86020
  387.2 61.0 %copy-start.173 = (f32[7,1024]{1,0:T(8,128)}, f32[7,1024]{1,0:T(8,128)S(1)}, u32[]{:S(2)}) copy-start(f32[7,1024]{1,0:T(8,128)S(1)} %slice.633) | copy-start | bytes 86020
  401.8 115.9 %copy-start.183 = (f32[3,1024]{1,0:T(4,128)}, f32[3,1024]{1,0:T(4,128)S(1)}, u32[]{:S(2)}) copy-start(f32[3,1024]{1,0:T(4,128)S(1)} %slice.638) | copy-start | bytes 36868
  418.1 121.3 %copy-start.138 = (f32[14,1024]{1,0:T(8,128)}, f32[14,1024]{1,0:T(8,128)S(1)}, u32[]{:S(2)}) copy-start(f32[14,1024]{1,0:T(8,128)S(1)} %slice.618) | copy-start | bytes 172036
  440.0 154.1 %copy-start.51 = (f32[119,1024]{1,0:T(8,128)}, f32[119,1024]{1,0:T(8,128)S(1)}, u32[]{:S(2)}) copy-start(f32[119,1024]{1,0:T(8,128)S(1)} %slice.588) | copy-start | bytes 1462276
  454.4 161.8 %copy-start.25 = (f32[239,1024]{1,0:T(8,128)}, f32[239,1024]{1,0:T(8,128)S(1)}, u32[]{:S(2)}) copy-start(f32[239,1024]{1,0:T(8,128)S(1)} %slice.578) | copy-start | bytes 2936836
  478.6 207.6 %copy-start.10 = (f32[479,1024]{1,0:T(8,128)}, f32[479,1024]{1,0:T(8,128)S(1)}, u32[]{:S(2)}) copy-start(f32[479,1024]{1,0:T(8,128)S(1)} %slice.568) | copy-start | bytes 5885956
  523.9 43.6 %copy-start.160 = (f32[7,1024]{1,0:T(8,128)}, f32[7,1024]{1,0:T(8,128)S(1)}, u32[]{:S(2)}) copy-start(f32[7,1024]{1,0:T(8,128)S(1)} %get-tuple-element.88) | copy-start | bytes 86020
  800.1 840.3 %reduce-scatter.9.cloned.1.call-start = ((), (), s32[]{:S(2)}) async-start(), calls=%async_computation.15 | async-start | bytes 9830400 | tf_op jit(solution)/shard_map/reduce_scatter | solution.py:104
  810.4 833.4 %reduce-scatter.19.cloned.1.call-start = ((), (), s32[]{:S(2)}) async-start(), calls=%async_computation.22 | async-start | bytes 12976128 | tf_op jit(solution)/shard_map/reduce_scatter | solution.py:149
  822.5 821.3 %reduce-scatter.21.cloned.1.call-start = ((), (), s32[]{:S(2)}) async-start(), calls=%async_computation.23 | async-start | bytes 12976128 | tf_op jit(solution)/shard_map/reduce_scatter | solution.py:150
  834.3 809.5 %reduce-scatter.23.cloned.1.call-start = ((), (), s32[]{:S(2)}) async-start(), calls=%async_computation.24 | async-start | bytes 12976128 | tf_op jit(solution)/shard_map/reduce_scatter | solution.py:151
  844.9 822.8 %reduce-scatter.13.cloned.1.call-start = ((), (), s32[]{:S(2)}) async-start(), calls=%async_computation.19 | async-start | bytes 18874368 | tf_op jit(solution)/shard_map/reduce_scatter | solution.py:143
  1501.7 335.4 %reduce-scatter.11.cloned.1.call-start = ((), (), s32[]{:S(2)}) async-start(), calls=%async_computation.18 | async-start | bytes 18874368 | tf_op jit(solution)/shard_map/reduce_scatter | solution.py:142
  1518.5 488.0 %reduce-scatter.17.cloned.1.call-start = ((), (), s32[]{:S(2)}) async-start(), calls=%async_computation.21 | async-start | bytes 18874368 | tf_op jit(solution)/shard_map/reduce_scatter | solution.py:145
  1534.3 641.6 %reduce-scatter.15.cloned.1.call-start = ((), (), s32[]{:S(2)}) async-start(), calls=%async_computation.20 | async-start | bytes 18874368 | tf_op jit(solution)/shard_map/reduce_scatter | solution.py:144
  1586.6 48.7 %copy-start.203 = (f32[960]{0:T(1024)S(1)}, f32[960]{0:T(1024)}, u32[]{:S(2)}) copy-start(f32[960]{0:T(1024)} %copy-done.202) | copy-start | bytes 11524
  (217 other events, 2036.5 us)
Sparse Core Ops, SparseCore 0:
  9.6 80.5 all-gather.10
  91.8 80.5 all-gather.8
  174.0 80.5 all-gather.12
  256.1 80.5 all-gather.14
  338.2 59.5 all-gather.16
  399.3 59.0 all-gather.18
  460.3 51.2 all-gather.22
  513.2 57.8 all-gather.20
  800.3 165.5 all-reduce.186
  968.6 83.3 reduce-scatter.8
  1054.9 116.4 reduce-scatter.18
  1174.1 117.6 reduce-scatter.20
  1294.7 117.6 reduce-scatter.22
  1501.8 165.8 reduce-scatter.12
  1670.5 166.5 reduce-scatter.10
  1839.9 166.5 reduce-scatter.16
  2009.3 166.5 reduce-scatter.14
where the time goes:
time: 2210 us; the launch traced here: 2180 us
  waiting for transfers between devices  800 us (36%)
  local copies, waits for them, and re-layouts  741 us (34%)
  other arithmetic  303 us (14%)
  matrix products  292 us (13%)
  blocking collectives  26.8 us (1%)
    pad x145, local copies, waits for them, and re-layouts, recurrent_mix(): lax.associative_scan(combine, (decay_re, decay_im, input_re, input_im), a...  373 us
    slice x146, local copies, waits for them, and re-layouts, recurrent_mix(): lax.associative_scan(combine, (decay_re, decay_im, input_re, input_im), a...  350 us
    reduce_scatter x1, waiting for transfers between devices, per_device(): lax.psum_scatter(grad_wmix, 'dp', scatter_dimension=0, tiled=True)  169 us
    reduce_scatter x1, waiting for transfers between devices, per_device(): lax.psum_scatter(grad_win, 'dp', scatter_dimension=0, tiled=True)  169 us
    reduce_scatter x1, waiting for transfers between devices, per_device(): lax.psum_scatter(grad_woutgate, 'dp', scatter_dimension=0, tiled=True)  169 us
    psum x1, waiting for transfers between devices, per_device(): grad_ffn_in = lax.psum(grad_ffn_part, 'mp')  121 us
    dot_general x7, matrix products, dot_trans(): lax.dot_general(left, right, (((1,), (1,)), ((), ())), preferred_element_...  105 us
    dot_general x7, matrix products, dot_rows(): lax.dot_general(left, right, (((0,), (0,)), ((), ())), preferred_element_...  98.1 us
  transfers between devices with their start and end apart: 17, of which 7 were waited for; matrix products, arithmetic and copies ran while one was open for 59% of the time, Pallas kernels for 0%

commit v1 on v0

v1 whole, which is shorter than its diff:
```python
import functools

import jax
import jax.numpy as jnp
from jax import lax
from jax.experimental import pallas as pl
from jax.experimental.pallas import tpu as pltpu
from jax.sharding import PartitionSpec as P

EPS = 1e-06
F32, BF16 = jnp.float32, jnp.bfloat16
LANE = 128
CHUNKS = 8


def dot(left, right):
    return jnp.dot(left, right, preferred_element_type=F32)


def dot_trans(left, right):
    return lax.dot_general(left, right, (((1,), (1,)), ((), ())), preferred_element_type=F32)


def dot_rows(left, right):
    return lax.dot_general(left, right, (((0,), (0,)), ((), ())), preferred_element_type=F32)


def sigmoid(v):
    return 1.0 / (1.0 + jnp.exp(-v))


def scan_forward(pin, pf, starts, bl, st, phasor, rowsq, a_re, a_im, b_re, b_im):
    rows, half = pin.shape[0], pin.shape[1] // 2
    span = rows // CHUNKS
    lanes = half // LANE
    low = sigmoid(bl[...])
    step = 48

    def prepare(i, _):
        at = pl.ds(pl.multiple_of(i * step, 8), step)
        forget = low + (1.0 - low) * sigmoid(pf[at, :half])
        phase = pf[at, half:]
        keep = 1.0 - starts[at, :]
        cos, sin = jnp.cos(phase) * keep, jnp.sin(phase) * keep
        phasor[at, :half] = cos
        phasor[at, half:] = sin
        x_re, x_im = pin[at, :half], pin[at, half:]
        inflow = 1.0 - forget
        in_re, in_im = x_re * sigmoid(x_re) * inflow, x_im * sigmoid(x_im) * inflow
        d_re, d_im = forget * cos, forget * sin
        for j in range(lanes):
            cut = slice(j * LANE, (j + 1) * LANE)
            a_re[j, at, :] = d_re[:, cut]
            a_im[j, at, :] = d_im[:, cut]
            b_re[j, at, :] = in_re[:, cut]
            b_im[j, at, :] = in_im[:, cut]
        return 0

    lax.fori_loop(0, rows // step, prepare, 0)
    zero, one = jnp.zeros((CHUNKS, LANE), F32), jnp.ones((CHUNKS, LANE), F32)

    def local(s, carry):
        at = pl.ds(s, CHUNKS, stride=span)
        out = []
        for j in range(lanes):
            p_re, p_im, s_re, s_im = carry[4 * j : 4 * j + 4]
            d_re, d_im = a_re.at[j][at, :], a_im.at[j][at, :]
            i_re, i_im = b_re.at[j][at, :], b_im.at[j][at, :]
            p_re, p_im = d_re * p_re - d_im * p_im, d_re * p_im + d_im * p_re
            s_re, s_im = d_re * s_re - d_im * s_im + i_re, d_re * s_im + d_im * s_re + i_im
            a_re.at[j][at, :] = p_re
            a_im.at[j][at, :] = p_im
            b_re.at[j][at, :] = s_re
            b_im.at[j][at, :] = s_im
            out += [p_re, p_im, s_re, s_im]
        return tuple(out)

    last = lax.fori_loop(0, span, local, (one, zero, zero, zero) * lanes, unroll=2)
    carries = []
    for j in range(lanes):
        p_re, p_im, s_re, s_im = last[4 * j : 4 * j + 4]
        c_re = c_im = jnp.zeros((1, LANE), F32)
        held = []
        for k in range(CHUNKS):
            held.append((c_re, c_im))
            q_re, q_im = p_re[k : k + 1], p_im[k : k + 1]
            c_re, c_im = (
                q_re * c_re - q_im * c_im + s_re[k : k + 1],
                q_re * c_im + q_im * c_re + s_im[k : k + 1],
            )
        carries.append(held)
    fix = 40
    for k in range(CHUNKS):

        def finish(i, _):
            at = pl.ds(pl.multiple_of(k * span + i * fix, 8), fix)
            total = jnp.zeros((fix, LANE), F32)
            for j in range(lanes):
                c_re, c_im = carries[j][k]
                p_re, p_im = a_re[j, at, :], a_im[j, at, :]
                s_re = b_re[j, at, :] + p_re * c_re - p_im * c_im
                s_im = b_im[j, at, :] + p_re * c_im + p_im * c_re
                st[at, j * LANE : (j + 1) * LANE] = s_re
                st[at, half + j * LANE : half + (j + 1) * LANE] = s_im
                total = total + s_re * s_re + s_im * s_im
            rowsq[at, :] = jnp.sum(total, axis=1, keepdims=True)
            return 0

        lax.fori_loop(0, span // fix, finish, 0)


def scan_backward(
    gm, pin, pf, pg, st, phasor, r, rowdot, bl, gain, gin, gf, gg, dgain, dbound, a_re, a_im, b_re, b_im
):
    rows, half = pin.shape[0], pin.shape[1] // 2
    width = 2 * half
    span = rows // CHUNKS
    lanes = half // LANE
    low = sigmoid(bl[...])
    step = 48

    def prepare(i, total):
        at = pl.ds(pl.multiple_of(i * step, 16), step)
        g, gate = gm[at, :], pg[at, :]
        sig = sigmoid(gate)
        silu = gate * sig
        n = st[at, :] * r[at, :]
        gs = g * silu
        gg[at, :] = (g * n * gain[...] * (sig * (1.0 + gate * (1.0 - sig)))).astype(gg.dtype)
        total = total + jnp.sum((gs * n).reshape(step // 8, 8, width), axis=0)
        d_st = r[at, :] * (gs * gain[...] - n * rowdot[at, :])
        forget = low + (1.0 - low) * sigmoid(pf[at, :half])
        d_re, d_im = forget * phasor[at, :half], forget * phasor[at, half:]
        for j in range(lanes):
            a_re[j, at, :] = d_re[:, j * LANE : (j + 1) * LANE]
            a_im[j, at, :] = d_im[:, j * LANE : (j + 1) * LANE]
            b_re[j, at, :] = d_st[:, j * LANE : (j + 1) * LANE]
            b_im[j, at, :] = d_st[:, half + j * LANE : half + (j + 1) * LANE]
        return total

    total = lax.fori_loop(0, rows // step, prepare, jnp.zeros((8, width), F32))
    dgain[...] = jnp.sum(total, axis=0, keepdims=True)
    zero, one = jnp.zeros((CHUNKS, LANE), F32), jnp.ones((CHUNKS, LANE), F32)

    def local(i, carry):
        at = pl.ds(span - 1 - i, CHUNKS, stride=span)
        out = []
        for j in range(lanes):
            p_re, p_im, s_re, s_im = carry[4 * j : 4 * j + 4]
            d_re, d_im = a_re.at[j][at, :], a_im.at[j][at, :]
            s_re, s_im = s_re + b_re.at[j][at, :], s_im + b_im.at[j][at, :]
            a_re.at[j][at, :] = p_re
            a_im.at[j][at, :] = p_im
            b_re.at[j][at, :] = s_re
            b_im.at[j][at, :] = s_im
            p_re, p_im = d_re * p_re + d_im * p_im, d_re * p_im - d_im * p_re
            s_re, s_im = d_re * s_re + d_im * s_im, d_re * s_im - d_im * s_re
            out += [p_re, p_im, s_re, s_im]
        return tuple(out)

    last = lax.fori_loop(0, span, local, (one, zero, zero, zero) * lanes, unroll=2)
    carries = []
    for j in range(lanes):
        p_re, p_im, s_re, s_im = last[4 * j : 4 * j + 4]
        c_re = c_im = jnp.zeros((1, LANE), F32)
        held = [None] * CHUNKS
        for k in reversed(range(CHUNKS)):
            held[k] = (c_re, c_im)
            q_re, q_im = p_re[k : k + 1], p_im[k : k + 1]
            c_re, c_im = (
                q_re * c_re - q_im * c_im + s_re[k : k + 1],
                q_re * c_im + q_im * c_re + s_im[k : k + 1],
            )
        carries.append(held)
    fix = 40
    for k in range(CHUNKS):

        def carry_in(i, _):
            at = pl.ds(pl.multiple_of(k * span + i * fix, 8), fix)
            for j in range(lanes):
                c_re, c_im = carries[j][k]
                p_re, p_im = a_re[j, at, :], a_im[j, at, :]
                b_re[j, at, :] += p_re * c_re - p_im * c_im
                b_im[j, at, :] += p_re * c_im + p_im * c_re
            return 0

        lax.fori_loop(0, span // fix, carry_in, 0)

    def finish(i, carry):
        before, total = carry
        at = pl.ds(pl.multiple_of(i * step, 16), step)
        g_re = jnp.concatenate([b_re[j, at, :] for j in range(lanes)], axis=1)
        g_im = jnp.concatenate([b_im[j, at, :] for j in range(lanes)], axis=1)
        now = st[at, :]
        prev = jnp.concatenate([before, now[:-1]], axis=0)
        q_re, q_im = prev[:, :half], prev[:, half:]
        dd_re, dd_im = g_re * q_re + g_im * q_im, g_im * q_re - g_re * q_im
        mag = sigmoid(pf[at, :half])
        forget = low + (1.0 - low) * mag
        cos, sin = phasor[at, :half], phasor[at, half:]
        x_re, x_im = pin[at, :half], pin[at, half:]
        sig_re, sig_im = sigmoid(x_re), sigmoid(x_im)
        inflow = 1.0 - forget
        d_forget = dd_re * cos + dd_im * sin - g_re * x_re * sig_re - g_im * x_im * sig_im
        gf[at, :half] = (d_forget * (1.0 - low) * mag * (1.0 - mag)).astype(gf.dtype)
        gf[at, half:] = (forget * (dd_im * cos - dd_re * sin)).astype(gf.dtype)
        gin[at, :half] = (g_re * inflow * sig_re * (1.0 + x_re * (1.0 - sig_re))).astype(gin.dtype)
        gin[at, half:] = (g_im * inflow * sig_im * (1.0 + x_im * (1.0 - sig_im))).astype(gin.dtype)
        total = total + jnp.sum((d_forget * (1.0 - mag)).reshape(step // 8, 8, half), axis=0)
        return now[step - 1 :], total

    first = (jnp.zeros((1, width), F32), jnp.zeros((8, half), F32))
    total = lax.fori_loop(0, rows // step, finish, first)[1]
    dbound[...] = jnp.sum(total, axis=0, keepdims=True) * low * (1.0 - low)


def call_local(body, outs, scratch, *args, name):
    return pl.pallas_call(
        body,
        out_shape=outs,
        scratch_shapes=scratch,
        compiler_params=pltpu.CompilerParams(vmem_limit_bytes=48 * 2**20),
        name=name,
    )(*args)


def per_device(n_dp, n_mp, tokens, segment_ids, cotangent, gain_in, w_in, w_forget, w_outgate, bound_logit, gain_mix,
               w_mix, gain_ffn, w_gate, w_up, w_down):
    m, d = lax.axis_index("mp"), lax.axis_index("dp")
    rows, width = tokens.shape
    half = bound_logit.shape[0]
    ch = half // n_mp
    mine = 2 * ch
    own = rows // n_mp
    ffn = w_gate.shape[1]
    shard = w_in.shape[0]

    def from_peer(x, j):
        return lax.ppermute(x, "mp", [(q, q ^ j) for q in range(n_mp)])

    def cols(x, at, size):
        return lax.dynamic_slice_in_dim(x, at, size, 1)

    def own_channels(x):
        return jnp.concatenate([cols(x, m * ch, ch), cols(x, half + m * ch, ch)], axis=1)

    def gather_rows(x):
        out = jnp.zeros((x.shape[0] * n_mp, x.shape[1]), x.dtype)
        for j in range(n_mp):
            part = x if j == 0 else from_peer(x, j)
            out = lax.dynamic_update_slice_in_dim(out, part, (m ^ j) * x.shape[0], 0)
        return out

    def scatter_sum(x):
        total = lax.dynamic_slice_in_dim(x, m * own, own, 0)
        for j in range(1, n_mp):
            part = lax.dynamic_slice_in_dim(x, (m ^ j) * own, own, 0).astype(BF16)
            total = total + from_peer(part, j).astype(F32)
        return total

    mixer_cols = jnp.concatenate([own_channels(w_in), own_channels(w_forget), own_channels(w_outgate)], axis=1)
    w_cat = lax.all_gather(mixer_cols, "dp", axis=0, tiled=True)
    mix_cols = cols(w_mix, m * mine, mine)
    w_mix_q = lax.all_gather(mix_cols, "dp", axis=0, tiled=True)
    wg = lax.all_gather(w_gate, "dp", axis=0, tiled=True)
    wu = lax.all_gather(w_up, "dp", axis=0, tiled=True)
    wd = lax.all_gather(w_down, "dp", axis=1, tiled=True)

    core = lax.rem(d, 2)
    hw = width // 2
    part = lax.dynamic_slice_in_dim(w_mix_q, core * hw, hw, 0)
    half_mix = jnp.zeros((hw, width), BF16)
    for j in range(n_mp):
        piece = part if j == 0 else from_peer(part, j)
        half_mix = lax.dynamic_update_slice_in_dim(half_mix, piece, (m ^ j) * mine, 1)
    other_mix = lax.ppermute(half_mix, "dp", [(q, q ^ 1) for q in range(n_dp)])
    wm = jnp.zeros((width, width), BF16)
    wm = lax.dynamic_update_slice_in_dim(wm, half_mix, core * hw, 0)
    wm = lax.dynamic_update_slice_in_dim(wm, other_mix, (1 - core) * hw, 0)

    grad_out = gather_rows(cotangent)

    stream = tokens.astype(F32)
    ident = segment_ids[0]
    previous = jnp.concatenate([ident[:1] - 1, ident[:-1]])
    starts = jnp.where(ident != previous, 1.0, 0.0).astype(F32)[:, None]
    r_in = lax.rsqrt(jnp.mean(stream * stream, axis=-1, keepdims=True) + EPS)
    normed = (stream * r_in * gain_in).astype(BF16)
    pin = dot(normed, w_cat[:, :mine])
    pf = dot(normed, w_cat[:, mine : 2 * mine])
    pg = dot(normed, w_cat[:, 2 * mine :])
    bl = lax.dynamic_slice_in_dim(bound_logit, m * ch, ch, 0)[None]
    gain = own_channels(gain_mix[None])
    lanes = ch // LANE
    scratch = [pltpu.VMEM((lanes, rows, LANE), F32)] * 4
    st, phasor, rowsq = call_local(
        scan_forward,
        (
            jax.ShapeDtypeStruct((rows, mine), F32),
            jax.ShapeDtypeStruct((rows, mine), F32),
            jax.ShapeDtypeStruct((rows, 1), F32),
        ),
        scratch,
        pin, pf, starts, bl,
        name="scan_forward",
    )
    rowsq = lax.psum(rowsq[:, 0], "mp")[:, None]
    r_mix = lax.rsqrt(rowsq / width + EPS)
    mixer_mine = (st * r_mix * gain * (pg * jax.nn.sigmoid(pg))).astype(BF16)
    mixer_out = jnp.zeros((rows, width), BF16)
    for j in range(n_mp):
        piece = mixer_mine if j == 0 else from_peer(mixer_mine, j)
        mixer_out = lax.dynamic_update_slice_in_dim(mixer_out, piece[:, :ch], (m ^ j) * ch, 1)
        mixer_out = lax.dynamic_update_slice_in_dim(mixer_out, piece[:, ch:], half + (m ^ j) * ch, 1)
    branch = dot(mixer_out, wm)
    middle = stream + branch
    r_ffn = lax.rsqrt(jnp.mean(middle * middle, axis=-1, keepdims=True) + EPS)
    ffn_in = (middle * r_ffn * gain_ffn).astype(BF16)

    gate_val = dot(ffn_in, wg)
    up_val = dot(ffn_in, wu)
    sig = jax.nn.sigmoid(gate_val)
    hidden = (gate_val * sig * up_val).astype(BF16)
    grad_hidden = dot_trans(grad_out, wd)
    grad_gate = (grad_hidden * up_val * sig * (1.0 + gate_val * (1.0 - sig))).astype(BF16)
    grad_up = (grad_hidden * gate_val * sig).astype(BF16)
    grad_ffn = scatter_sum(dot_trans(grad_gate, wg) + dot_trans(grad_up, wu))
    g_down = lax.psum_scatter(dot_rows(grad_out, hidden).astype(BF16), "dp", scatter_dimension=0, tiled=True)
    g_gate_up = lax.psum_scatter(
        jnp.concatenate([dot_rows(ffn_in, grad_gate), dot_rows(ffn_in, grad_up)], axis=1).astype(BF16),
        "dp", scatter_dimension=0, tiled=True,
    )
    down = scatter_sum(dot(hidden, wd))
    row_at = m * own

    def own_rows(x):
        return lax.dynamic_slice_in_dim(x, row_at, own, 0)

    middle_own = own_rows(middle)
    mixed = (middle_own + down).astype(BF16)

    r_own = own_rows(r_ffn)
    n_own = middle_own * r_own
    gain_ffn_part = jnp.sum(grad_ffn * n_own, axis=0)
    gn = grad_ffn * gain_ffn
    grad_middle = cotangent.astype(F32) + r_own * (gn - n_own * jnp.mean(gn * n_own, axis=-1, keepdims=True))
    grad_branch = grad_middle.astype(BF16)
    rowdot_own = jnp.mean(grad_branch.astype(F32) * (middle_own - own_rows(stream)), axis=-1, keepdims=True)
    grad_mixer_own = dot_trans(grad_branch, wm)

    gm = jnp.zeros((rows, mine), F32)
    gb_cols = jnp.zeros((rows, mine), BF16)
    rowdot = jnp.zeros((rows, 1), F32)
    for j in range(n_mp):
        q = m ^ j
        piece = jnp.concatenate([cols(grad_mixer_own, q * ch, ch), cols(grad_mixer_own, half + q * ch, ch)], axis=1)
        gb = cols(grad_branch, q * mine, mine)
        rd = rowdot_own
        if j:
            piece, gb, rd = from_peer(piece, j), from_peer(gb, j), from_peer(rd, j)
        gm = lax.dynamic_update_slice_in_dim(gm, piece, q * own, 0)
        gb_cols = lax.dynamic_update_slice_in_dim(gb_cols, gb, q * own, 0)
        rowdot = lax.dynamic_update_slice_in_dim(rowdot, rd, q * own, 0)
    gin, gf, gg, dgain, dbound = call_local(
        scan_backward,
        (
            jax.ShapeDtypeStruct((rows, mine), BF16),
            jax.ShapeDtypeStruct((rows, mine), BF16),
            jax.ShapeDtypeStruct((rows, mine), BF16),
            jax.ShapeDtypeStruct((1, mine), F32),
            jax.ShapeDtypeStruct((1, ch), F32),
        ),
        scratch,
        gm, pin, pf, pg, st, phasor, r_mix, rowdot, bl, gain,
        name="scan_backward",
    )
    g_cat = jnp.concatenate([gin, gf, gg], axis=1)
    g_mix = lax.psum_scatter(
        jnp.concatenate([dot_rows(normed, g_cat), dot_rows(mixer_out, gb_cols)], axis=1).astype(BF16),
        "dp", scatter_dimension=0, tiled=True,
    )
    grad_normed = scatter_sum(dot_trans(g_cat, w_cat))
    s_own, ri_own = own_rows(stream), own_rows(r_in)
    n_in = s_own * ri_own
    gain_in_part = jnp.sum(grad_normed * n_in, axis=0)
    gn_in = grad_normed * gain_in
    grad_tokens = grad_middle + ri_own * (gn_in - n_in * jnp.mean(gn_in * n_in, axis=-1, keepdims=True))

    g_win = jnp.zeros((shard, width), F32)
    g_wf, g_wo, g_wm = g_win, g_win, g_win
    for j in range(n_mp):
        q = m ^ j
        piece = (g_mix if j == 0 else from_peer(g_mix, j)).astype(F32)

        def put(total, lo):
            total = lax.dynamic_update_slice_in_dim(total, piece[:, lo : lo + ch], q * ch, 1)
            return lax.dynamic_update_slice_in_dim(total, piece[:, lo + ch : lo + mine], half + q * ch, 1)

        g_win, g_wf, g_wo = put(g_win, 0), put(g_wf, mine), put(g_wo, 2 * mine)
        g_wm = lax.dynamic_update_slice_in_dim(g_wm, piece[:, 3 * mine :], q * mine, 1)

    gmix_full = jnp.zeros((width,), F32)
    gmix_full = lax.dynamic_update_slice_in_dim(gmix_full, dgain[0, :ch], m * ch, 0)
    gmix_full = lax.dynamic_update_slice_in_dim(gmix_full, dgain[0, ch:], half + m * ch, 0)
    gb_full = lax.dynamic_update_slice_in_dim(jnp.zeros((half,), F32), dbound[0], m * ch, 0)
    small = lax.psum(jnp.concatenate([gain_in_part, gain_ffn_part, gmix_full, gb_full]), ("dp", "mp"))

    def part_of(lo, size):
        return lax.dynamic_slice_in_dim(small, lo + d * (size // n_dp), size // n_dp, 0)

    return (
        mixed,
        grad_tokens,
        part_of(0, width),
        g_win,
        g_wf,
        g_wo,
        part_of(3 * width, half),
        part_of(2 * width, width),
        g_wm,
        part_of(width, width),
        g_gate_up[:, :ffn].astype(F32),
        g_gate_up[:, ffn:].astype(F32),
        g_down.astype(F32).T,
    )


def solution(mesh):
    both, split = P(("dp", "mp"), None), P("dp", "mp")
    row, vec = P("dp", None), P("dp")
    return jax.shard_map(
        functools.partial(per_device, mesh.shape["dp"], mesh.shape["mp"]),
        mesh=mesh,
        in_specs=(row, row, both, P(), row, row, row, P(), P(), row, P(), split, split, P("mp", "dp")),
        out_specs=(both, both, vec, row, row, row, vec, vec, row, vec, split, split, P("mp", "dp")),
        check_vma=False,
    )
```

time: 2210 us -> 760 us (0.34)
  local copies, waits for them, and re-layouts: 741 us -> 128 us
  waiting for transfers between devices: 800 us -> 263 us
  other arithmetic: 303 us -> 54.3 us
  matrix products: 292 us -> 150 us
  blocking collectives: 26.8 us -> 78.2 us
  starting transfers between devices: 0.68 us -> 39.1 us
    reduce_scatter x8 -> x3, waiting for transfers between devices: 532 us -> 0.01 us  [the longest x1 0.01 us: per_device(): lax.psum_scatter(jnp.concatenate([dot_rows(normed, g_cat), dot_rows(mixer...]
    pad x145 -> x0, local copies, waits for them, and re-layouts: 373 us -> none  [recurrent_mix(): lax.associative_scan(combine, (decay_re, decay_im, input_re, input_im), a...]
    slice x146 -> x37, local copies, waits for them, and re-layouts: 350 us -> 35.6 us  [the longest x16 17.8 us: put(): piece[:, lo + ch:lo + mine]]
    ppermute x0 -> x31, waiting for transfers between devices: none -> 228 us  [the longest x30 228 us: from_peer(): return lax.ppermute(x, 'mp', [(q, q ^ j) for q in range(n_mp)])]
    psum x1 -> x0, waiting for transfers between devices: 121 us -> none  [per_device(): grad_ffn_in = lax.psum(grad_ffn_part, 'mp')]
    add_any x43 -> x0, other arithmetic: 118 us -> none  [the longest x18 45.4 us: combine(): state_re = latter[0] * former[2] - latter[1] * former[3] + latter[2]]
    all_gather x8 -> x5, waiting for transfers between devices: 141 us -> 33.5 us  [the longest x1 23.4 us: per_device(): w_mix_q = lax.all_gather(mix_cols, 'dp', axis=0, tiled=True)]
    add x38 -> x1, other arithmetic: 85.6 us -> 7.21 us  [per_device(): grad_middle + ri_own * (gn_in - n_in * jnp.mean(gn_in * n_in, axis=-1, ke...]
  transfers between devices with their start and end apart: 17 -> 39, of which waited for: 7 -> 17; matrix products, arithmetic and copies ran while one was open for 59% -> 33% of each run, Pallas kernels for 0% -> 1%
where the time goes in v1:
time: 760 us; the launch traced here: 750 us
  waiting for transfers between devices  263 us (35%)
  matrix products  150 us (20%)
  local copies, waits for them, and re-layouts  128 us (17%)
  blocking collectives  78.2 us (10%)
  other arithmetic  54.3 us (7%)
  starting transfers between devices  39.1 us (5%)
  Pallas kernels  20.4 us (3%)
  between operations  16.3 us (2%)
    ppermute x30, waiting for transfers between devices, from_peer(): return lax.ppermute(x, 'mp', [(q, q ^ j) for q in range(n_mp)])  228 us
    psum x1, blocking collectives, per_device(): lax.psum(jnp.concatenate([gain_in_part, gain_ffn_part, gmix_full, gb_full...  68.3 us
    dot_general x7, matrix products, dot(): return jnp.dot(left, right, preferred_element_type=F32)  58.4 us
    dot_general x5, matrix products, dot_trans(): lax.dot_general(left, right, (((1,), (1,)), ((), ())), preferred_element_...  51.9 us
    dot_general x5, matrix products, dot_rows(): lax.dot_general(left, right, (((0,), (0,)), ((), ())), preferred_element_...  39.9 us
    ppermute x30, starting transfers between devices, from_peer(): return lax.ppermute(x, 'mp', [(q, q ^ j) for q in range(n_mp)])  38.8 us
    all_gather x1, waiting for transfers between devices, per_device(): w_mix_q = lax.all_gather(mix_cols, 'dp', axis=0, tiled=True)  23.4 us
    unnamed x102, local copies, waits for them, and re-layouts  22.4 us
  transfers between devices with their start and end apart: 39, of which 17 were waited for; matrix products, arithmetic and copies ran while one was open for 33% of the time, Pallas kernels for 1%

profile of v1, /device:TPU:8, one launch (start us, length us, event | category | flops | bytes accessed | tf_op | source)
XLA Modules:
  0.0 749.6 jit_solution(10240691897315520397)
XLA Ops:
  17.0 23.4 %all-gather.8.cloned.1.call-done = bf16[2048,512]{1,0:T(8,128)(2,1)} async-done(((bf16[256,512]{1,0:T(8,128)(2,1)}), bf16[2048,512]{1,0:T(8,128)(2,1)}) %all-gather.8.cloned.1.call-update) | async-done | bytes 2097168 | tf_op jit(solution)/shard_map/all_gather | solution.py:264
  55.4 15.4 %collective-permute-done.3 = bf16[1024,512]{1,0:T(8,128)(2,1)S(1)} collective-permute-done((bf16[1024,512]{1,0:T(8,128)(2,1)}, bf16[1024,512]{1,0:T(8,128)(2,1)S(1)}, u32[]{:S(2)}, u32[]{:S(2)}) %collective-permute-start.3) | collective-permute-done | bytes 1048608 | tf_op jit(solution)/shard_map/ppermute | solution.py:239
  74.2 61.8 %collective-permute-done.4 = bf16[1024,512]{1,0:T(8,128)(2,1)} collective-permute-done((bf16[1024,512]{1,0:T(8,128)(2,1)}, bf16[1024,512]{1,0:T(8,128)(2,1)}, u32[]{:S(2)}, u32[]{:S(2)}) %collective-permute-start.4) | collective-permute-done | bytes 1048608 | tf_op jit(solution)/shard_map/ppermute | solution.py:239
  148.5 6.6 fusion.2.pf
  155.0 5.1 fusion.4.pin
  160.2 10.3 %scan_forward.1 = (f32[960,512]{1,0:T(8,128)S(1)}, f32[960,512]{1,0:T(8,128)S(1)}, f32[960,1]{1,0:T(8,128)S(1)}) custom-call(f32[960,512]{1,0:T(8,128)} %fusion.4.pin, f32[960,512]{1,0:T(8,128)} %fusion.2.pf, f32[960,1]{1,0:T(8,128)S(1)} %compare_select_fusion.starts, f32[1,256]{1,0:T(1,128)S(1)} %bitcast.42), custom_call_target="tpu_custom_call" | custom-call | tf_op jit(solution)/shard_map/scan_forward/pallas_call | solution.py:218
  171.9 9.9 %psum.14 = f32[960]{0:T(1024)S(1)} all-reduce(f32[960]{0:T(1024)S(1)} %reduce), channel_id=1, replica_groups=mesh['dp'=8,'mp'=4] {'mp'}, use_global_device_ids=true, to_apply=%region_1.2 | all-reduce | flops 960 | bytes 7680 | tf_op jit(solution)/shard_map/psum | solution.py:307
  181.9 6.7 multiply_convert_fusion.5
  189.6 2.9 constant_dynamic-update-slice_fusion.43
  192.5 2.8 constant_dynamic-update-slice_fusion.42
  199.6 13.7 %collective-permute-done = bf16[960,512]{1,0:T(8,128)(2,1)S(1)} collective-permute-done((bf16[960,512]{1,0:T(8,128)(2,1)S(1)}, bf16[960,512]{1,0:T(8,128)(2,1)S(1)}, u32[]{:S(2)}, u32[]{:S(2)}) %collective-permute-start) | collective-permute-done | bytes 983072 | tf_op jit(solution)/shard_map/ppermute | solution.py:239
  213.4 25.5 %collective-permute-done.1 = bf16[960,512]{1,0:T(8,128)(2,1)S(1)} collective-permute-done((bf16[960,512]{1,0:T(8,128)(2,1)S(1)}, bf16[960,512]{1,0:T(8,128)(2,1)S(1)}, u32[]{:S(2)}, u32[]{:S(2)}) %collective-permute-start.1) | collective-permute-done | bytes 983072 | tf_op jit(solution)/shard_map/ppermute | solution.py:239
  239.2 8.6 %multiply_reduce_fusion = (f32[960]{0:T(1024)S(1)}, f32[960,2048]{1,0:T(8,128)S(1)}) fusion(bf16[960,2048]{1,0:T(8,128)(2,1)S(1)} %slice_dynamic-update-slice_fusion, bf16[2048,2048]{1,0:T(8,128)(2,1)S(1)} %constant_dynamic-update-slice_fusion.42, bf16[960,2048]{1,0:T(8,128)(2,1)S(1)} %copy-done.7), kind=kOutput, calls=%fused_computation.3 | convolution fusion | flops 8060926976 | bytes 24121088 | tf_op jit(solution)/shard_map/dot_general | solution.py:17
  247.9 3.1 copy-done.4
  251.0 2.6 multiply_convert_fusion
  253.5 11.6 %fusion.15 = f32[960,1408]{1,0:T(8,128)} fusion(bf16[960,2048]{1,0:T(8,128)(2,1)} %multiply_convert_fusion, bf16[2048,1408]{1,0:T(8,128)(2,1)} %all-gather.10.cloned.1.call-done), kind=kOutput, calls=%fused_computation.149 | convolution fusion | flops 5536481280 | bytes 15106048 | tf_op jit(solution)/shard_map/dot_general | solution.py:17
  265.1 11.3 %fusion.16 = f32[960,1408]{1,0:T(8,128)} fusion(bf16[960,2048]{1,0:T(8,128)(2,1)} %multiply_convert_fusion, bf16[2048,1408]{1,0:T(8,128)(2,1)} %all-gather.12.cloned.1.call-done), kind=kOutput, calls=%fused_computation.150 | convolution fusion | flops 5536481280 | bytes 15106048 | tf_op jit(solution)/shard_map/dot_general | solution.py:17
  276.4 10.0 %all-gather.14.cloned.1.call-done = bf16[1408,2048]{1,0:T(8,128)(2,1)} async-done(((bf16[1408,256]{1,0:T(8,128)(2,1)}), bf16[1408,2048]{1,0:T(8,128)(2,1)}) %all-gather.14.cloned.1.call-update) | async-done | bytes 5767184 | tf_op jit(solution)/shard_map/all_gather | solution.py:267
  286.5 15.0 %multiply_convert_fusion.2 = (bf16[960,1408]{1,0:T(8,128)(2,1)S(1)}, bf16[960,1408]{1,0:T(8,128)(2,1)S(1)}, bf16[960,1408]{1,0:T(8,128)(2,1)}) fusion(f32[960,1408]{1,0:T(8,128)} %fusion.15, f32[960,1408]{1,0:T(8,128)} %fusion.16, bf16[960,2048]{1,0:T(8,128)(2,1)} %constant_dynamic-update-slice_fusion.38, bf16[1408,2048]{1,0:T(8,128)(2,1)} %all-gather.14.cloned.1.call-done), kind=kOutput, calls=%fused_computation.11 | convolution fusion | flops 5558108160 | bytes 28622848 | tf_op jit(solution)/shard_map/dot_general | solution.py:21
  301.4 12.3 %fusion.18 = f32[960,2048]{1,0:T(8,128)} fusion(bf16[960,1408]{1,0:T(8,128)(2,1)S(1)} %get-tuple-element.79, bf16[2048,1408]{1,0:T(8,128)(2,1)} %all-gather.10.cloned.1.call-done), kind=kOutput, calls=%fused_computation.152 | convolution fusion | flops 5536481280 | bytes 16334848 | tf_op jit(solution)/shard_map/dot_general | solution.py:21
  313.8 9.1 %convolution_add_fusion = f32[960,2048]{1,0:T(8,128)S(1)} fusion(f32[960,2048]{1,0:T(8,128)} %fusion.18, bf16[960,1408]{1,0:T(8,128)(2,1)S(1)} %get-tuple-element.78, bf16[2048,1408]{1,0:T(8,128)(2,1)S(1)} %copy-done.41), kind=kOutput, calls=%fused_computation.15 | convolution fusion | flops 5538447360 | bytes 24199168 | tf_op jit(solution)/shard_map/dot_general | solution.py:21
  327.9 4.1 convert_element_type.111
  332.3 16.8 %collective-permute-done.13 = bf16[240,2048]{1,0:T(8,128)(2,1)} collective-permute-done((bf16[240,2048]{1,0:T(8,128)(2,1)}, bf16[240,2048]{1,0:T(8,128)(2,1)}, u32[]{:S(2)}, u32[]{:S(2)}) %collective-permute-start.13) | collective-permute-done | bytes 983072 | tf_op jit(solution)/shard_map/ppermute | solution.py:239
  349.2 20.5 %collective-permute-done.14 = bf16[240,2048]{1,0:T(8,128)(2,1)} collective-permute-done((bf16[240,2048]{1,0:T(8,128)(2,1)S(1)}, bf16[240,2048]{1,0:T(8,128)(2,1)}, u32[]{:S(2)}, u32[]{:S(2)}) %collective-permute-start.14) | collective-permute-done | bytes 983072 | tf_op jit(solution)/shard_map/ppermute | solution.py:239
  370.8 3.9 multiply_reduce_fusion.2
  374.8 3.8 multiply_reduce_fusion.5
  382.3 6.1 fusion.19
  399.0 15.5 %collective-permute-done.26 = bf16[240,512]{1,0:T(8,128)(2,1)S(1)} collective-permute-done((bf16[240,512]{1,0:T(8,128)(2,1)S(1)}, bf16[240,512]{1,0:T(8,128)(2,1)S(1)}, u32[]{:S(2)}, u32[]{:S(2)}) %collective-permute-start.26) | collective-permute-done | bytes 245792 | tf_op jit(solution)/shard_map/ppermute | solution.py:239
  414.6 3.7 convolution_convert_fusion.4
  418.3 3.2 collective-permute-done.16
  422.8 10.1 %scan_backward.1 = (bf16[960,512]{1,0:T(8,128)(2,1)S(1)}, bf16[960,512]{1,0:T(8,128)(2,1)S(1)}, bf16[960,512]{1,0:T(8,128)(2,1)S(1)}, f32[1,512]{1,0:T(1,128)S(1)}, f32[1,256]{1,0:T(1,128)S(1)}) custom-call(f32[960,512]{1,0:T(8,128)S(1)} %constant_dynamic-update-slice_fusion.35.gm, f32[960,512]{1,0:T(8,128)} %fusion.4.pin, f32[960,512]{1,0:T(8,128)} %fusion.2.pf, ...), custom_call_target="tpu_custom_call" | custom-call | tf_op jit(solution)/shard_map/scan_backward/pallas_call | solution.py:218
  436.0 9.6 %convolution_convert_fusion.3 = bf16[2048,1536]{0,1:T(8,128)(2,1)} fusion(bf16[960,1536]{1,0:T(8,128)(2,1)S(1)} %constant_dynamic-update-slice_fusion.48, bf16[960,2048]{1,0:T(8,128)(2,1)S(1)} %copy-done.9, f32[2048]{0:T(1024)S(1)} %copy-done.39, f32[960]{0:T(1024)S(1)} %add_rsqrt_fusion.2), kind=kOutput, calls=%fused_computation.9 | convolution fusion | flops 6050807808 | bytes 13184768 | tf_op jit(solution)/shard_map/dot_general | solution.py:25
  445.6 8.3 %pad_maximum_fusion.1 = bf16[2048,2048]{0,1:T(8,128)(2,1)} fusion(bf16[2048,512]{0,1:T(8,128)(2,1)} %convolution_convert_fusion.4, bf16[2048,1536]{0,1:T(8,128)(2,1)} %convolution_convert_fusion.3), kind=kLoop, calls=%fused_computation.1 | loop fusion | flops 16777216 | bytes 16777216 | tf_op jit(solution)/shard_map/concatenate | solution.py:379
  453.9 10.9 %convolution_convert_fusion = bf16[2048,1408]{1,0:T(8,128)(2,1)} fusion(bf16[960,2048]{1,0:T(8,128)(2,1)} %constant_dynamic-update-slice_fusion.38, bf16[960,1408]{1,0:T(8,128)(2,1)} %get-tuple-element.80), kind=kOutput, calls=%fused_computation.6 | convolution fusion | flops 5539364864 | bytes 12402688 | tf_op jit(solution)/shard_map/dot_general | solution.py:25
  464.9 9.2 %convolution_convert_fusion.1 = bf16[2048,1408]{0,1:T(8,128)(2,1)S(1)} fusion(bf16[960,2048]{1,0:T(8,128)(2,1)} %multiply_convert_fusion, bf16[960,1408]{1,0:T(8,128)(2,1)} %copy-done.43), kind=kOutput, calls=%fused_computation.7 | convolution fusion | flops 5539364864 | bytes 12402688 | tf_op jit(solution)/shard_map/dot_general | solution.py:25
  474.1 6.6 convolution_convert_fusion.2
  480.7 13.9 %pad_maximum_fusion = bf16[2048,2816]{0,1:T(8,128)(2,1)} fusion(bf16[2048,1408]{0,1:T(8,128)(2,1)S(1)} %convolution_convert_fusion.1, bf16[2048,1408]{0,1:T(8,128)(2,1)S(1)} %convolution_convert_fusion.2), kind=kLoop, calls=%fused_computation | loop fusion | flops 23068672 | bytes 23068672 | tf_op jit(solution)/shard_map/concatenate | solution.py:330
  494.6 9.4 %fusion.20 = f32[960,2048]{1,0:T(8,128)S(1)} fusion(bf16[960,1536]{1,0:T(8,128)(2,1)} %copy-done.37, bf16[2048,1536]{1,0:T(8,128)(2,1)} %all-gather.6.cloned.1.call-done), kind=kOutput, calls=%fused_computation.154 | convolution fusion | flops 6039797760 | bytes 17104896 | tf_op jit(solution)/shard_map/dot_general | solution.py:21
  509.7 8.6 %fusion.17 = f32[960,2048]{1,0:T(8,128)S(1)} fusion(bf16[960,1408]{1,0:T(8,128)(2,1)S(1)} %copy-done.42, bf16[1408,2048]{1,0:T(8,128)(2,1)} %all-gather.14.cloned.1.call-done), kind=kOutput, calls=%fused_computation.151 | convolution fusion | flops 5536481280 | bytes 16334848 | tf_op jit(solution)/shard_map/dot_general | solution.py:17
  522.3 8.1 %collective-permute-done.22 = bf16[240,2048]{1,0:T(8,128)(2,1)S(1)} collective-permute-done((bf16[240,2048]{1,0:T(8,128)(2,1)S(1)}, bf16[240,2048]{1,0:T(8,128)(2,1)S(1)}, u32[]{:S(2)}, u32[]{:S(2)}) %collective-permute-start.22) | collective-permute-done | bytes 983072 | tf_op jit(solution)/shard_map/ppermute | solution.py:239
  532.6 19.8 %collective-permute-done.23 = bf16[240,2048]{1,0:T(8,128)(2,1)} collective-permute-done((bf16[240,2048]{1,0:T(8,128)(2,1)}, bf16[240,2048]{1,0:T(8,128)(2,1)}, u32[]{:S(2)}, u32[]{:S(2)}) %collective-permute-start.23) | collective-permute-done | bytes 983072 | tf_op jit(solution)/shard_map/ppermute | solution.py:239
  552.4 5.1 multiply_reduce_fusion.3
  557.5 68.3 %psum.15 = f32[7168]{0:T(1024)S(1)} all-reduce(f32[7168]{0:T(1024)S(1)} %pad_maximum_fusion.5), channel_id=1, replica_groups=mesh['dp'=8,'mp'=4] {'dp','mp'}, use_global_device_ids=true, to_apply=%region_8.9 | all-reduce | flops 7168 | bytes 57344 | tf_op jit(solution)/shard_map/psum | solution.py:406
  627.0 7.2 multiply_add_fusion
  656.5 4.4 collective-permute-done.28
  662.1 20.0 %collective-permute-done.29 = bf16[256,2048]{0,1:T(8,128)(2,1)} collective-permute-done((bf16[256,2048]{0,1:T(8,128)(2,1)}, bf16[256,2048]{0,1:T(8,128)(2,1)}, u32[]{:S(2)}, u32[]{:S(2)}) %collective-permute-start.29) | collective-permute-done | bytes 1048608 | tf_op jit(solution)/shard_map/ppermute | solution.py:239
  735.1 2.7 slice_convert_fusion
  737.9 2.9 copy.132
  (315 shorter events, 163.0 us)
Async XLA Ops:
  7.2 33.3 %all-gather.8.cloned.1.call-start = ((), (), s32[]{:S(2)}) async-start(), calls=%async_computation.4 | async-start | bytes 2359296 | tf_op jit(solution)/shard_map/all_gather | solution.py:264
  9.2 139.3 %all-gather.6.cloned.1.call-start = ((), (), s32[]{:S(2)}) async-start(), calls=%async_computation.3 | async-start | bytes 7077888 | tf_op jit(solution)/shard_map/all_gather | solution.py:262
  15.7 237.9 %all-gather.10.cloned.1.call-start = ((), (), s32[]{:S(2)}) async-start(), calls=%async_computation.5 | async-start | bytes 6488064 | tf_op jit(solution)/shard_map/all_gather | solution.py:265
  16.4 248.7 %all-gather.12.cloned.1.call-start = ((), (), s32[]{:S(2)}) async-start(), calls=%async_computation.6 | async-start | bytes 6488064 | tf_op jit(solution)/shard_map/all_gather | solution.py:266
  17.0 269.5 %all-gather.14.cloned.1.call-start = ((), (), s32[]{:S(2)}) async-start(), calls=%async_computation.7 | async-start | bytes 6488064 | tf_op jit(solution)/shard_map/all_gather | solution.py:267
  17.0 29.0 %copy-start.10 = (bf16[240,2048]{1,0:T(8,128)(2,1)S(1)}, bf16[240,2048]{1,0:T(8,128)(2,1)}, u32[]{:S(2)}) copy-start(bf16[240,2048]{1,0:T(8,128)(2,1)} %param.16) | copy-start | bytes 2949124
  44.5 26.2 %collective-permute-start.3 = (bf16[1024,512]{1,0:T(8,128)(2,1)}, bf16[1024,512]{1,0:T(8,128)(2,1)S(1)}, u32[]{:S(2)}, u32[]{:S(2)}) collective-permute-start(bf16[1024,512]{1,0:T(8,128)(2,1)} %get-tuple-element.77), channel_id=1, source_target_pairs={{0,1},{1,0},{2,3},{3,2},{4,5},{5,4},{6,7},{7,6},{8,9},{9,8},{10,11... | collective-permute-start | bytes 3145736 | tf_op jit(solution)/shard_map/ppermute | solution.py:239
  46.0 95.6 %collective-permute-start.10 = (bf16[240,2048]{1,0:T(8,128)(2,1)S(1)}, bf16[240,2048]{1,0:T(8,128)(2,1)}, u32[]{:S(2)}, u32[]{:S(2)}) collective-permute-start(bf16[240,2048]{1,0:T(8,128)(2,1)S(1)} %copy-done.10), channel_id=1, source_target_pairs={{0,1},{1,0},{2,3},{3,2},{4,5},{5,4},{6,7},{7,6},{8,9},{9,8},{10,11... | collective-permute-start | bytes 2949128 | tf_op jit(solution)/shard_map/ppermute | solution.py:239
  46.6 97.3 %collective-permute-start.11 = (bf16[240,2048]{1,0:T(8,128)(2,1)S(1)}, bf16[240,2048]{1,0:T(8,128)(2,1)}, u32[]{:S(2)}, u32[]{:S(2)}) collective-permute-start(bf16[240,2048]{1,0:T(8,128)(2,1)S(1)} %copy-done.10), channel_id=1, source_target_pairs={{0,2},{1,3},{2,0},{3,1},{4,6},{5,7},{6,4},{7,5},{8,10},{9,11},{10,... | collective-permute-start | bytes 2949128 | tf_op jit(solution)/shard_map/ppermute | solution.py:239
  48.1 586.1 %reduce-scatter.4.cloned.1.call-start = ((), (), s32[]{:S(2)}) async-start(), calls=%async_computation.8 | async-start | bytes 9437184 | tf_op jit(solution)/shard_map/reduce_scatter | solution.py:378
  48.2 87.9 %collective-permute-start.4 = (bf16[1024,512]{1,0:T(8,128)(2,1)}, bf16[1024,512]{1,0:T(8,128)(2,1)}, u32[]{:S(2)}, u32[]{:S(2)}) collective-permute-start(bf16[1024,512]{1,0:T(8,128)(2,1)} %get-tuple-element.77), channel_id=1, source_target_pairs={{0,2},{1,3},{2,0},{3,1},{4,6},{5,7},{6,4},{7,5},{8,10},{9,11},{10,... | collective-permute-start | bytes 3145736 | tf_op jit(solution)/shard_map/ppermute | solution.py:239
  48.7 89.6 %collective-permute-start.5 = (bf16[1024,512]{1,0:T(8,128)(2,1)}, bf16[1024,512]{1,0:T(8,128)(2,1)S(1)}, u32[]{:S(2)}, u32[]{:S(2)}) collective-permute-start(bf16[1024,512]{1,0:T(8,128)(2,1)} %get-tuple-element.77), channel_id=1, source_target_pairs={{0,3},{1,2},{2,1},{3,0},{4,7},{5,6},{6,5},{7,4},{8,11},{9,10},{10,... | collective-permute-start | bytes 3145736 | tf_op jit(solution)/shard_map/ppermute | solution.py:239
  54.5 19.7 %copy-start.17 = (bf16[960,2048]{1,0:T(8,128)(2,1)}, bf16[960,2048]{1,0:T(8,128)(2,1)S(1)}, u32[]{:S(2)}) copy-start(bf16[960,2048]{1,0:T(8,128)(2,1)S(1)} %constant_dynamic-update-slice_fusion.41) | copy-start | bytes 11796484
  70.7 75.4 %collective-permute-start.12 = (bf16[240,2048]{1,0:T(8,128)(2,1)S(1)}, bf16[240,2048]{1,0:T(8,128)(2,1)}, u32[]{:S(2)}, u32[]{:S(2)}) collective-permute-start(bf16[240,2048]{1,0:T(8,128)(2,1)S(1)} %copy-done.10), channel_id=1, source_target_pairs={{0,3},{1,2},{2,1},{3,0},{4,7},{5,6},{6,5},{7,4},{8,11},{9,10},{10,... | collective-permute-start | bytes 2949128 | tf_op jit(solution)/shard_map/ppermute | solution.py:239
  139.5 53.0 %collective-permute-start.6 = (bf16[1024,2048]{1,0:T(8,128)(2,1)}, bf16[1024,2048]{1,0:T(8,128)(2,1)}, u32[]{:S(2)}, u32[]{:S(2)}) collective-permute-start(bf16[1024,2048]{1,0:T(8,128)(2,1)} %constant_dynamic-update-slice_fusion.44), channel_id=1, source_target_pairs={{0,4},{4,0},{8,12},{12,8},{16,20},{20,16},{24,28},{28,24},{1,5},{5... | collective-permute-start | bytes 12582920 | tf_op jit(solution)/shard_map/ppermute | solution.py:276
  171.7 16.8 %copy-start.2 = (f32[960,512]{1,0:T(8,128)}, f32[960,512]{1,0:T(8,128)S(1)}, u32[]{:S(2)}) copy-start(f32[960,512]{1,0:T(8,128)S(1)} %get-tuple-element.21.st) | copy-start | bytes 5898244
  188.6 24.7 %collective-permute-start = (bf16[960,512]{1,0:T(8,128)(2,1)S(1)}, bf16[960,512]{1,0:T(8,128)(2,1)S(1)}, u32[]{:S(2)}, u32[]{:S(2)}) collective-permute-start(bf16[960,512]{1,0:T(8,128)(2,1)S(1)} %get-tuple-element.137), channel_id=1, source_target_pairs={{0,1},{1,0},{2,3},{3,2},{4,5},{5,4},{6,7},{7,6},{8,9},{9,8},{10,11... | collective-permute-start | bytes 2949128 | tf_op jit(solution)/shard_map/ppermute | solution.py:239
  195.3 43.9 %copy-start.13 = (bf16[2048,2048]{1,0:T(8,128)(2,1)}, bf16[2048,2048]{1,0:T(8,128)(2,1)S(1)}, u32[]{:S(2)}) copy-start(bf16[2048,2048]{1,0:T(8,128)(2,1)S(1)} %constant_dynamic-update-slice_fusion.42) | copy-start | bytes 25165828
  195.3 43.5 %collective-permute-start.1 = (bf16[960,512]{1,0:T(8,128)(2,1)S(1)}, bf16[960,512]{1,0:T(8,128)(2,1)S(1)}, u32[]{:S(2)}, u32[]{:S(2)}) collective-permute-start(bf16[960,512]{1,0:T(8,128)(2,1)S(1)} %get-tuple-element.137), channel_id=1, source_target_pairs={{0,2},{1,3},{2,0},{3,1},{4,6},{5,7},{6,4},{7,5},{8,10},{9,11},{10,... | collective-permute-start | bytes 2949128 | tf_op jit(solution)/shard_map/ppermute | solution.py:239
  196.4 42.7 %collective-permute-start.2 = (bf16[960,512]{1,0:T(8,128)(2,1)S(1)}, bf16[960,512]{1,0:T(8,128)(2,1)S(1)}, u32[]{:S(2)}, u32[]{:S(2)}) collective-permute-start(bf16[960,512]{1,0:T(8,128)(2,1)S(1)} %get-tuple-element.137), channel_id=1, source_target_pairs={{0,3},{1,2},{2,1},{3,0},{4,7},{5,6},{6,5},{7,4},{8,11},{9,10},{10,... | collective-permute-start | bytes 2949128 | tf_op jit(solution)/shard_map/ppermute | solution.py:239
  199.5 39.7 %copy-start.7 = (bf16[960,2048]{1,0:T(8,128)(2,1)S(1)}, bf16[960,2048]{1,0:T(8,128)(2,1)}, u32[]{:S(2)}) copy-start(bf16[960,2048]{1,0:T(8,128)(2,1)} %param.14) | copy-start | bytes 11796484
  324.3 24.9 %collective-permute-start.13 = (bf16[240,2048]{1,0:T(8,128)(2,1)}, bf16[240,2048]{1,0:T(8,128)(2,1)}, u32[]{:S(2)}, u32[]{:S(2)}) collective-permute-start(bf16[240,2048]{1,0:T(8,128)(2,1)} %get-tuple-element.86), channel_id=1, source_target_pairs={{0,1},{1,0},{2,3},{3,2},{4,5},{5,4},{6,7},{7,6},{8,9},{9,8},{10,11... | collective-permute-start | bytes 2949128 | tf_op jit(solution)/shard_map/ppermute | solution.py:239
  326.0 43.7 %collective-permute-start.14 = (bf16[240,2048]{1,0:T(8,128)(2,1)S(1)}, bf16[240,2048]{1,0:T(8,128)(2,1)}, u32[]{:S(2)}, u32[]{:S(2)}) collective-permute-start(bf16[240,2048]{1,0:T(8,128)(2,1)S(1)} %get-tuple-element.88), channel_id=1, source_target_pairs={{0,2},{1,3},{2,0},{3,1},{4,6},{5,7},{6,4},{7,5},{8,10},{9,11},{10,... | collective-permute-start | bytes 2949128 | tf_op jit(solution)/shard_map/ppermute | solution.py:239
  327.5 43.3 %collective-permute-start.15 = (bf16[240,2048]{1,0:T(8,128)(2,1)S(1)}, bf16[240,2048]{1,0:T(8,128)(2,1)}, u32[]{:S(2)}, u32[]{:S(2)}) collective-permute-start(bf16[240,2048]{1,0:T(8,128)(2,1)S(1)} %get-tuple-element.87), channel_id=1, source_target_pairs={{0,3},{1,2},{2,1},{3,0},{4,7},{5,6},{6,5},{7,4},{8,11},{9,10},{10,... | collective-permute-start | bytes 2949128 | tf_op jit(solution)/shard_map/ppermute | solution.py:239
  332.3 42.4 %copy-start.11 = (bf16[240,2048]{1,0:T(8,128)(2,1)S(1)}, bf16[240,2048]{1,0:T(8,128)(2,1)}, u32[]{:S(2)}) copy-start(bf16[240,2048]{1,0:T(8,128)(2,1)} %param.16) | copy-start | bytes 2949124
  378.7 12.8 %collective-permute-start.19 = (f32[240,1]{1,0:T(8,128)S(1)}, f32[240,1]{1,0:T(8,128)S(1)}, u32[]{:S(2)}, u32[]{:S(2)}) collective-permute-start(f32[240,1]{1,0:T(8,128)S(1)} %copy.99), channel_id=1, source_target_pairs={{0,1},{1,0},{2,3},{3,2},{4,5},{5,4},{6,7},{7,6},{8,9},{9,8},{10,11... | collective-permute-start | bytes 2888 | tf_op jit(solution)/shard_map/ppermute | solution.py:239
  380.2 12.9 %collective-permute-start.20 = (f32[240,1]{1,0:T(8,128)S(1)}, f32[240,1]{1,0:T(8,128)S(1)}, u32[]{:S(2)}, u32[]{:S(2)}) collective-permute-start(f32[240,1]{1,0:T(8,128)S(1)} %copy.99), channel_id=1, source_target_pairs={{0,2},{1,3},{2,0},{3,1},{4,6},{5,7},{6,4},{7,5},{8,10},{9,11},{10,... | collective-permute-start | bytes 2888 | tf_op jit(solution)/shard_map/ppermute | solution.py:239
  380.8 13.8 %collective-permute-start.21 = (f32[240,1]{1,0:T(8,128)S(1)}, f32[240,1]{1,0:T(8,128)S(1)}, u32[]{:S(2)}, u32[]{:S(2)}) collective-permute-start(f32[240,1]{1,0:T(8,128)S(1)} %copy.99), channel_id=1, source_target_pairs={{0,3},{1,2},{2,1},{3,0},{4,7},{5,6},{6,5},{7,4},{8,11},{9,10},{10,... | collective-permute-start | bytes 2888 | tf_op jit(solution)/shard_map/ppermute | solution.py:239
  388.6 8.5 %collective-permute-start.25 = (bf16[240,512]{1,0:T(8,128)(2,1)S(1)}, bf16[240,512]{1,0:T(8,128)(2,1)S(1)}, u32[]{:S(2)}, u32[]{:S(2)}) collective-permute-start(bf16[240,512]{1,0:T(8,128)(2,1)S(1)} %get-tuple-element.128), channel_id=1, source_target_pairs={{0,1},{1,0},{2,3},{3,2},{4,5},{5,4},{6,7},{7,6},{8,9},{9,8},{10,11... | collective-permute-start | bytes 737288 | tf_op jit(solution)/shard_map/ppermute | solution.py:239
  390.1 24.4 %collective-permute-start.26 = (bf16[240,512]{1,0:T(8,128)(2,1)S(1)}, bf16[240,512]{1,0:T(8,128)(2,1)S(1)}, u32[]{:S(2)}, u32[]{:S(2)}) collective-permute-start(bf16[240,512]{1,0:T(8,128)(2,1)S(1)} %get-tuple-element.127), channel_id=1, source_target_pairs={{0,2},{1,3},{2,0},{3,1},{4,6},{5,7},{6,4},{7,5},{8,10},{9,11},{10,... | collective-permute-start | bytes 737288 | tf_op jit(solution)/shard_map/ppermute | solution.py:239
  391.1 23.4 %copy-start.19 = (bf16[960,2048]{1,0:T(8,128)(2,1)S(1)}, bf16[960,2048]{1,0:T(8,128)(2,1)}, u32[]{:S(2)}) copy-start(bf16[960,2048]{1,0:T(8,128)(2,1)} %copy-done.18) | copy-start | bytes 11796484
  391.5 23.0 %collective-permute-start.27 = (bf16[240,512]{1,0:T(8,128)(2,1)S(1)}, bf16[240,512]{1,0:T(8,128)(2,1)S(1)}, u32[]{:S(2)}, u32[]{:S(2)}) collective-permute-start(bf16[240,512]{1,0:T(8,128)(2,1)S(1)} %get-tuple-element.126), channel_id=1, source_target_pairs={{0,3},{1,2},{2,1},{3,0},{4,7},{5,6},{6,5},{7,4},{8,11},{9,10},{10,... | collective-permute-start | bytes 737288 | tf_op jit(solution)/shard_map/ppermute | solution.py:239
  393.1 29.6 %collective-permute-start.18 = (f32[240,512]{1,0:T(8,128)S(1)}, f32[240,512]{1,0:T(8,128)S(1)}, u32[]{:S(2)}, u32[]{:S(2)}) collective-permute-start(f32[240,512]{1,0:T(8,128)S(1)} %pad_maximum_fusion.4), channel_id=1, source_target_pairs={{0,3},{1,2},{2,1},{3,0},{4,7},{5,6},{6,5},{7,4},{8,11},{9,10},{10,... | collective-permute-start | bytes 1474568 | tf_op jit(solution)/shard_map/ppermute | solution.py:239
  394.6 28.0 %collective-permute-start.17 = (f32[240,512]{1,0:T(8,128)S(1)}, f32[240,512]{1,0:T(8,128)S(1)}, u32[]{:S(2)}, u32[]{:S(2)}) collective-permute-start(f32[240,512]{1,0:T(8,128)S(1)} %pad_maximum_fusion.3), channel_id=1, source_target_pairs={{0,2},{1,3},{2,0},{3,1},{4,6},{5,7},{6,4},{7,5},{8,10},{9,11},{10,... | collective-permute-start | bytes 1474568 | tf_op jit(solution)/shard_map/ppermute | solution.py:239
  397.1 24.3 %collective-permute-start.16 = (f32[240,512]{1,0:T(8,128)S(1)}, f32[240,512]{1,0:T(8,128)S(1)}, u32[]{:S(2)}, u32[]{:S(2)}) collective-permute-start(f32[240,512]{1,0:T(8,128)S(1)} %pad_maximum_fusion.2), channel_id=1, source_target_pairs={{0,1},{1,0},{2,3},{3,2},{4,5},{5,4},{6,7},{7,6},{8,9},{9,8},{10,11... | collective-permute-start | bytes 1474568 | tf_op jit(solution)/shard_map/ppermute | solution.py:239
  453.9 184.2 %reduce-scatter.8.cloned.1.call-start = ((), (), s32[]{:S(2)}) async-start(), calls=%async_computation.10 | async-start | bytes 6488064 | tf_op jit(solution)/shard_map/reduce_scatter | solution.py:328
  464.8 270.3 %reduce-scatter.6.cloned.1.call-start = ((), (), s32[]{:S(2)}) async-start(), calls=%async_computation.9 | async-start | bytes 12976128 | tf_op jit(solution)/shard_map/reduce_scatter | solution.py:329
  505.7 24.7 %collective-permute-start.22 = (bf16[240,2048]{1,0:T(8,128)(2,1)S(1)}, bf16[240,2048]{1,0:T(8,128)(2,1)S(1)}, u32[]{:S(2)}, u32[]{:S(2)}) collective-permute-start(bf16[240,2048]{1,0:T(8,128)(2,1)S(1)} %get-tuple-element.83), channel_id=1, source_target_pairs={{0,1},{1,0},{2,3},{3,2},{4,5},{5,4},{6,7},{7,6},{8,9},{9,8},{10,11... | collective-permute-start | bytes 2949128 | tf_op jit(solution)/shard_map/ppermute | solution.py:239
  506.3 46.1 %collective-permute-start.23 = (bf16[240,2048]{1,0:T(8,128)(2,1)}, bf16[240,2048]{1,0:T(8,128)(2,1)}, u32[]{:S(2)}, u32[]{:S(2)}) collective-permute-start(bf16[240,2048]{1,0:T(8,128)(2,1)} %get-tuple-element.85), channel_id=1, source_target_pairs={{0,2},{1,3},{2,0},{3,1},{4,6},{5,7},{6,4},{7,5},{8,10},{9,11},{10,... | collective-permute-start | bytes 2949128 | tf_op jit(solution)/shard_map/ppermute | solution.py:239
  508.3 44.1 %collective-permute-start.24 = (bf16[240,2048]{1,0:T(8,128)(2,1)}, bf16[240,2048]{1,0:T(8,128)(2,1)}, u32[]{:S(2)}, u32[]{:S(2)}) collective-permute-start(bf16[240,2048]{1,0:T(8,128)(2,1)} %get-tuple-element.84), channel_id=1, source_target_pairs={{0,3},{1,2},{2,1},{3,0},{4,7},{5,6},{6,5},{7,4},{8,11},{9,10},{10,... | collective-permute-start | bytes 2949128 | tf_op jit(solution)/shard_map/ppermute | solution.py:239
  520.3 106.8 %collective-permute-start.7 = (bf16[240,2048]{1,0:T(8,128)(2,1)}, bf16[240,2048]{1,0:T(8,128)(2,1)}, u32[]{:S(2)}, u32[]{:S(2)}) collective-permute-start(bf16[240,2048]{1,0:T(8,128)(2,1)} %get-tuple-element.89), channel_id=1, source_target_pairs={{0,1},{1,0},{2,3},{3,2},{4,5},{5,4},{6,7},{7,6},{8,9},{9,8},{10,11... | collective-permute-start | bytes 2949128 | tf_op jit(solution)/shard_map/ppermute | solution.py:239
  520.8 106.2 %collective-permute-start.8 = (bf16[240,2048]{1,0:T(8,128)(2,1)}, bf16[240,2048]{1,0:T(8,128)(2,1)}, u32[]{:S(2)}, u32[]{:S(2)}) collective-permute-start(bf16[240,2048]{1,0:T(8,128)(2,1)} %get-tuple-element.91), channel_id=1, source_target_pairs={{0,2},{1,3},{2,0},{3,1},{4,6},{5,7},{6,4},{7,5},{8,10},{9,11},{10,... | collective-permute-start | bytes 2949128 | tf_op jit(solution)/shard_map/ppermute | solution.py:239
  530.4 96.6 %collective-permute-start.9 = (bf16[240,2048]{1,0:T(8,128)(2,1)}, bf16[240,2048]{1,0:T(8,128)(2,1)}, u32[]{:S(2)}, u32[]{:S(2)}) collective-permute-start(bf16[240,2048]{1,0:T(8,128)(2,1)} %get-tuple-element.90), channel_id=1, source_target_pairs={{0,3},{1,2},{2,1},{3,0},{4,7},{5,6},{6,5},{7,4},{8,11},{9,10},{10,... | collective-permute-start | bytes 2949128 | tf_op jit(solution)/shard_map/ppermute | solution.py:239
  532.6 94.4 %copy-start.12 = (bf16[240,2048]{1,0:T(8,128)(2,1)S(1)}, bf16[240,2048]{1,0:T(8,128)(2,1)}, u32[]{:S(2)}) copy-start(bf16[240,2048]{1,0:T(8,128)(2,1)} %param.16) | copy-start | bytes 2949124
  634.2 26.7 %collective-permute-start.28 = (bf16[256,2048]{0,1:T(8,128)(2,1)}, bf16[256,2048]{0,1:T(8,128)(2,1)}, u32[]{:S(2)}, u32[]{:S(2)}) collective-permute-start(bf16[256,2048]{0,1:T(8,128)(2,1)} %reduce-scatter.4.cloned.1.call-done), channel_id=1, source_target_pairs={{0,1},{1,0},{2,3},{3,2},{4,5},{5,4},{6,7},{7,6},{8,9},{9,8},{10,11... | collective-permute-start | bytes 3145736 | tf_op jit(solution)/shard_map/ppermute | solution.py:239
  636.6 45.6 %collective-permute-start.29 = (bf16[256,2048]{0,1:T(8,128)(2,1)}, bf16[256,2048]{0,1:T(8,128)(2,1)}, u32[]{:S(2)}, u32[]{:S(2)}) collective-permute-start(bf16[256,2048]{0,1:T(8,128)(2,1)} %reduce-scatter.4.cloned.1.call-done), channel_id=1, source_target_pairs={{0,2},{1,3},{2,0},{3,1},{4,6},{5,7},{6,4},{7,5},{8,10},{9,11},{10,... | collective-permute-start | bytes 3145736 | tf_op jit(solution)/shard_map/ppermute | solution.py:239
  636.7 46.6 %collective-permute-start.30 = (bf16[256,2048]{0,1:T(8,128)(2,1)}, bf16[256,2048]{0,1:T(8,128)(2,1)S(1)}, u32[]{:S(2)}, u32[]{:S(2)}) collective-permute-start(bf16[256,2048]{0,1:T(8,128)(2,1)} %reduce-scatter.4.cloned.1.call-done), channel_id=1, source_target_pairs={{0,3},{1,2},{2,1},{3,0},{4,7},{5,6},{6,5},{7,4},{8,11},{9,10},{10,... | collective-permute-start | bytes 3145736 | tf_op jit(solution)/shard_map/ppermute | solution.py:239
  711.9 15.7 %copy-start.32 = (f32[256,256]{1,0:T(8,128)S(1)}, f32[256,256]{1,0:T(8,128)}, u32[]{:S(2)}) copy-start(f32[256,256]{1,0:T(8,128)} %copy.119) | copy-start | bytes 786436
  (37 other events, 299.0 us)
Sparse Core Ops, SparseCore 0:
  10.2 30.2 all-gather.7
  42.7 62.0 all-gather.5
  106.4 59.2 all-gather.9
  167.2 59.1 all-gather.11
  227.9 58.5 all-gather.13
  454.0 86.7 reduce-scatter.3
  543.1 63.4 reduce-scatter.7
  608.8 117.9 reduce-scatter.5

commit v2 on v1

--- a/solution.py
+++ b/solution.py
@@ -224,6 +224,975 @@
     )(*args)
 
 
+MESH_ID = pl.DeviceIdType.MESH
+VMEM_LIMIT = 62 * 2**20
+ANY = pl.BlockSpec(memory_space=pl.ANY)
+VMEM = pl.BlockSpec(memory_space=pltpu.VMEM)
+
+
+def remote(src, dst, send, recv, device):
+    return pltpu.make_async_remote_copy(
+        src_ref=src, dst_ref=dst, send_sem=send, recv_sem=recv, device_id=device, device_id_type=MESH_ID
+    )
+
+
+def load(src, dst, sem):
+    copy = pltpu.make_async_copy(src, dst, sem)
+    copy.start()
+    return copy
+
+
+def bounds(total, parts, unit):
+    ends = [i * (total // unit) // parts * unit for i in range(parts)] + [total]
+    return [(ends[i], ends[i + 1] - ends[i]) for i in range(parts)]
+
+
+def subsets(masks):
+    out = [0]
+    for mask in masks:
+        out += [sub | mask for sub in out]
+    return out
+
+
+class Place:
+    def __init__(self, n_dp, n_mp):
+        self.n_dp, self.n_mp = n_dp, n_mp
+        self.d, self.m = lax.axis_index("dp"), lax.axis_index("mp")
+        self.chips, self.bits = n_dp // 2, n_mp.bit_length() - 1
+        self.k, self.c = lax.div(self.d, 2), lax.rem(self.d, 2)
+
+    def twin(self):
+        return (2 * self.k + 1 - self.c, self.m)
+
+    def chip(self, step):
+        return (self.d + 2 * step, self.m)
+
+    def peer(self, mask):
+        return (self.d, self.m ^ mask)
+
+    def along(self, s):
+        return (2 * lax.rem(self.k + s, self.chips) + self.c, self.m)
+
+    def barrier(self, line=True, twin=True, far=False):
+        sem = pltpu.get_barrier_semaphore()
+
+        def greet(device):
+            pl.semaphore_signal(sem, inc=1, device_id=device, device_id_type=MESH_ID)
+
+        for mask in range(1, self.n_mp):
+            greet(self.peer(mask))
+        count = self.n_mp - 1
+        if twin:
+            greet(self.twin())
+            count += 1
+        if far:
+            for s in range(1, self.chips):
+                greet(self.along(s))
+            count += self.chips - 1
+        elif line:
+
+            @pl.when(self.k > 0)
+            def _():
+                greet(self.chip(-1))
+
+            @pl.when(self.k < self.chips - 1)
+            def _():
+                greet(self.chip(1))
+
+            count += jnp.where(self.k > 0, 1, 0) + jnp.where(self.k < self.chips - 1, 1, 0)
+        pl.semaphore_wait(sem, count)
+
+
+class RowSum:
+    @staticmethod
+    def scratch(n_dp, blocks, rows, width):
+        chips = n_dp // 2
+        return [
+            pltpu.VMEM((2, 2, rows, width), BF16),
+            pltpu.VMEM((blocks, chips, rows, width), BF16),
+            pltpu.VMEM((blocks, chips + 1, rows, width), BF16),
+            pltpu.VMEM((rows, width), F32),
+            pltpu.SemaphoreType.DMA((4, blocks, chips + 1)),
+        ]
+
+    def __init__(self, place, refs, piece, finish, skew):
+        self.p = place
+        self.out, self.summed, self.inbox, self.acc, self.sem = refs
+        self.piece, self.finish = piece, finish
+        self.blocks, self.skew = self.summed.shape[0], skew
+        chips = place.chips
+        self.steps = (self.blocks + chips - 1) * chips if skew else self.blocks * chips
+
+    def order(self, i):
+        chips = self.p.chips
+        ok = (i >= 0) & (i < self.steps)
+        i = jnp.clip(i, 0, self.steps - 1)
+        if self.skew:
+            t = lax.rem(i, chips)
+            b = lax.div(i, chips) - t
+            return t, jnp.clip(b, 0, self.blocks - 1), (b >= 0) & (b < self.blocks) & ok
+        return lax.div(i, self.blocks), lax.rem(i, self.blocks), ok
+
+    def targets(self, i):
+        p = self.p
+        t, b, ok = self.order(i)
+        up, down = p.chips - 1 - t + p.k, p.k - (p.chips - 1) + t
+        return b, up, ok & (up <= p.chips - 1), down, ok & (down >= 0) & (t < p.chips - 1), t == p.chips - 1
+
+    def swap(self, b, e, ring):
+        return remote(
+            self.out.at[ring[0], ring[1]], self.summed.at[b, e], self.sem.at[0, b, e], self.sem.at[1, b, e],
+            self.p.twin(),
+        )
+
+    def move(self, b, e, up):
+        slot = e + 1 if up else e
+        return remote(
+            self.summed.at[b, e], self.inbox.at[b, slot], self.sem.at[2, b, e], self.sem.at[3, b, slot],
+            self.p.chip(1 if up else -1),
+        )
+
+    def given(self, i):
+        b, up, up_ok, down, down_ok, _ = self.targets(i)
+        for side, e, ok in ((0, up, up_ok), (1, down, down_ok)):
+
+            @pl.when(ok)
+            def _():
+                self.swap(b, e, (lax.rem(i + 2, 2), side)).wait_send()
+
+    def give(self, i):
+        self.given(i - 2)
+        b, up, up_ok, down, down_ok, _ = self.targets(i)
+        for side, e, ok in ((0, up, up_ok), (1, down, down_ok)):
+
+            @pl.when(ok)
+            def _():
+                ring = (lax.rem(i, 2), side)
+                self.out[ring[0], side] = self.piece(b, 2 * e + 1 - self.p.c).astype(BF16)
+                self.swap(b, e, ring).start()
+
+    def take(self, b, slot, up):
+        e = slot - 1 if up else slot
+        self.move(b, e, up).wait_recv()
+        self.acc[...] += self.inbox[b, slot].astype(F32)
+
+    def send(self, b, e, up):
+        self.summed[b, e] = self.acc[...].astype(BF16)
+        self.move(b, e, up).start()
+
+    def work(self, i):
+        p = self.p
+        b, up, up_ok, down, down_ok, last = self.targets(i)
+
+        def begin(e):
+            own = self.piece(b, 2 * e + p.c)
+            self.swap(b, e, (0, 0)).wait_recv()
+            self.acc[...] = own + self.summed[b, e].astype(F32)
+
+        @pl.when(up_ok)
+        def _():
+            begin(up)
+
+            @pl.when(p.k > 0)
+            def _():
+                self.take(b, up + 1, True)
+
+            @pl.when(jnp.logical_not(last))
+            def _():
+                self.send(b, up, True)
+
+            @pl.when(last)
+            def _():
+                @pl.when(p.k < p.chips - 1)
+                def _():
+                    self.take(b, up, False)
+
+                self.finish(b, self.acc)
+
+        @pl.when(down_ok)
+        def _():
+            begin(down)
+
+            @pl.when(p.k < p.chips - 1)
+            def _():
+                self.take(b, down, False)
+
+            self.send(b, down, False)
+
+    def run(self, lo, hi):
+        if lo == 0:
+            self.give(0)
+
+        def body(i, _):
+            self.give(i + 1)
+            self.work(i)
+            return 0
+
+        lax.fori_loop(lo, hi, body, 0)
+        if hi == self.steps:
+            self.given(hi - 1)
+
+    def drain(self):
+        p = self.p
+
+        def body(e, _):
+            for b in range(self.blocks):
+
+                @pl.when(e > p.k)
+                def _():
+                    self.move(b, e, True).wait_send()
+
+                @pl.when(e < p.k)
+                def _():
+                    self.move(b, e, False).wait_send()
+
+            return 0
+
+        lax.fori_loop(0, p.chips, body, 0)
+
+
+class CubeSum:
+    @staticmethod
+    def scratch(n_mp, rows, width):
+        bits = n_mp.bit_length() - 1
+        most = max(size for _, size in bounds(width, bits, LANE))
+        return [
+            pltpu.VMEM((bits, n_mp - 1, rows, most), BF16),
+            pltpu.VMEM((bits, n_mp - 1, rows, most), BF16),
+            pltpu.SemaphoreType.DMA((2, bits, n_mp - 1)),
+        ]
+
+    def __init__(self, place, refs, partial, width):
+        self.p = place
+        self.out, self.inbox, self.sem = refs
+        self.partial = partial
+        bits = place.bits
+        self.cols = bounds(width, bits, LANE)
+        self.slots, self.masks = {}, {}
+        for part in range(bits):
+            used = 0
+            for s in range(bits):
+                subs = subsets([1 << ((part + r) % bits) for r in range(s + 1, bits)])
+                self.masks[part, s] = (1 << ((part + s) % bits), subs)
+                for sub in subs:
+                    self.slots[part, s, sub] = used
+                    used += 1
+
+    def copy(self, part, s, sub):
+        slot, size = self.slots[part, s, sub], self.cols[part][1]
+        return remote(
+            self.out.at[part, slot, :, :size], self.inbox.at[part, slot, :, :size],
+            self.sem.at[0, part, slot], self.sem.at[1, part, slot],
+            self.p.peer(self.masks[part, s][0]),
+        )
+
+    def arrived(self, part, s, sub):
+        self.copy(part, s, sub).wait_recv()
+        return self.inbox[part, self.slots[part, s, sub], :, : self.cols[part][1]].astype(F32)
+
+    def stage(self, s):
+        for part in range(self.p.bits):
+            bit, subs = self.masks[part, s]
+            for sub in subs:
+                value = self.partial(self.p.m ^ (bit | sub), part)
+                for r in range(s):
+                    value = value + self.arrived(part, r, bit | sub)
+                self.out[part, self.slots[part, s, sub], :, : self.cols[part][1]] = value.astype(BF16)
+                self.copy(part, s, sub).start()
+
+    def result(self, part):
+        value = self.partial(self.p.m, part)
+        for s in range(self.p.bits):
+            value = value + self.arrived(part, s, 0)
+        return value
+
+    def drain(self):
+        for part, s, sub in self.slots:
+            self.copy(part, s, sub).wait_send()
+
+
+class CubeGather:
+    @staticmethod
+    def scratch(n_mp):
+        bits = n_mp.bit_length() - 1
+        return [pltpu.SemaphoreType.DMA((bits, n_mp)), pltpu.SemaphoreType.DMA((bits, n_mp))]
+
+    def __init__(self, place, refs, view):
+        self.p, self.view = place, view
+        self.send, self.recv = refs
+        bits = place.bits
+        self.sends = {}
+        for part in range(bits):
+            for s in range(bits):
+                earlier = [1 << ((part + r) % bits) for r in range(s)]
+                for sub in subsets(earlier):
+                    self.sends[part, s, sub] = (1 << ((part + s) % bits), sub)
+
+    def copy(self, part, bit, sub):
+        p = self.p
+        ref = self.view(p.m ^ sub, part)
+        return remote(ref, ref, self.send.at[part, bit | sub], self.recv.at[part, p.m ^ sub], p.peer(bit))
+
+    def arrived(self, part, sub):
+        p = self.p
+        ref = self.view(p.m ^ sub, part)
+        remote(ref, ref, self.send.at[part, sub], self.recv.at[part, p.m ^ sub], p.peer(sub)).wait_recv()
+
+    def stage(self, s):
+        for (part, at, sub), (bit, _) in self.sends.items():
+            if at == s:
+                if sub:
+                    self.arrived(part, sub)
+                self.copy(part, bit, sub).start()
+
+    def last(self):
+        p = self.p
+        for part in range(p.bits):
+            final = 1 << ((part + p.bits - 1) % p.bits)
+            for sub in range(1, p.n_mp):
+                if sub & final:
+                    self.arrived(part, sub)
+
+    def drain(self):
+        for (part, _, sub), (bit, _) in self.sends.items():
+            self.copy(part, bit, sub).wait_send()
+
+
+class SmallSum:
+    @staticmethod
+    def scratch(n_dp, n_mp, shape):
+        slots = 3 + n_mp + n_dp // 2
+        return [pltpu.VMEM((slots, *shape), F32), pltpu.SemaphoreType.DMA((2, slots))]
+
+    def __init__(self, place, refs):
+        self.p = place
+        self.buf, self.sem = refs
+
+    def start(self, src, dst, device):
+        remote(self.buf.at[src], self.buf.at[dst], self.sem.at[0, dst], self.sem.at[1, dst], device).start()
+
+    def wait(self, dst):
+        copy = remote(self.buf.at[dst], self.buf.at[dst], self.sem.at[0, dst], self.sem.at[1, dst], self.p.twin())
+        copy.wait_recv()
+
+    def sent(self, dst):
+        copy = remote(self.buf.at[dst], self.buf.at[dst], self.sem.at[0, dst], self.sem.at[1, dst], self.p.twin())
+        copy.wait_send()
+
+    def twins(self):
+        self.start(0, 1, self.p.twin())
+
+    def cube(self):
+        p = self.p
+        self.wait(1)
+        self.buf[2] = self.buf[0] + self.buf[1]
+        for mask in range(1, p.n_mp):
+            self.start(2, 3 + mask, p.peer(mask))
+
+    def line(self):
+        p = self.p
+        for mask in range(1, p.n_mp):
+            self.wait(3 + mask)
+        total = 0.0
+        for q in range(p.n_mp):
+            mask = p.m ^ q
+            total = total + self.buf[jnp.where(mask == 0, 2, 3 + mask)]
+        self.buf[3] = total
+        for s in range(1, p.chips):
+            self.start(3, 3 + p.n_mp + s, p.along(s))
+
+    def result(self):
+        p = self.p
+        total = self.buf[3]
+        for s in range(1, p.chips):
+            self.wait(3 + p.n_mp + s)
+            total = total + self.buf[3 + p.n_mp + s]
+        for dst in [1, *range(4, 3 + p.n_mp), *range(4 + p.n_mp, 3 + p.n_mp + p.chips)]:
+            self.sent(dst)
+        return total
+
+
+def gather_kernel(n_dp, n_mp, mine, whole, lsem, send, recv):
+    p = Place(n_dp, n_mp)
+    p.barrier(line=False, twin=False)
+    own = load(mine, whole.at[p.m], lsem)
+    for mask in range(1, n_mp):
+        remote(mine, whole.at[p.m], send.at[mask], recv.at[p.m], p.peer(mask)).start()
+    own.wait()
+    for mask in range(1, n_mp):
+        remote(mine, whole.at[p.m ^ mask], send.at[mask], recv.at[p.m ^ mask], p.peer(mask)).wait()
+
+
+def gather_mp(n_dp, n_mp, cid, x):
+    return pl.pallas_call(
+        functools.partial(gather_kernel, n_dp, n_mp),
+        out_shape=jax.ShapeDtypeStruct((n_mp, *x.shape), x.dtype),
+        in_specs=[ANY],
+        out_specs=ANY,
+        scratch_shapes=[
+            pltpu.SemaphoreType.DMA,
+            pltpu.SemaphoreType.DMA((n_mp,)),
+            pltpu.SemaphoreType.DMA((n_mp,)),
+        ],
+        compiler_params=pltpu.CompilerParams(collective_id=cid, has_side_effects=True),
+        name="gather_mp",
+    )(x)
+
+
+def mixer_kernel(
+    n_dp, n_mp, normed, w, tokens, starts, bl, gain, gain_ffn,
+    pin_o, pf_o, pg_o, st_o, phasor_o, r_o, mix_o, ffn_o, mid_o, rmid_o, wm_o,
+    x, wv, pin, pf, pg, st, phasor, rowsq, a_re, a_im, b_re, b_im, mix, wm, tok, ffn_v, mid_v, rs_out, rs_in,
+    lsem, osem, rs_sem, wtwin, *gsems,
+):
+    p = Place(n_dp, n_mp)
+    rows, width = normed.shape
+    mine = pin.shape[1]
+    half, ch = width // 2, mine // 2
+    own = rows // n_mp
+    hw = width // 2
+    row_parts = bounds(hw, p.bits, 16)
+
+    def mix_view(q, part):
+        lo, size = row_parts[part]
+        return wm.at[pl.ds(pl.multiple_of(p.c * hw + lo, 16), size), pl.ds(pl.multiple_of(q * mine, LANE), mine)]
+
+    loads = [load(normed, x, lsem.at[0])]
+    loads += [load(w.at[:, i * mine : (i + 1) * mine], wv.at[i], lsem.at[1 + i]) for i in range(3)]
+    own_mix = load(
+        w.at[pl.ds(pl.multiple_of(p.c * hw, 16), hw), 3 * mine : 4 * mine],
+        wm.at[pl.ds(pl.multiple_of(p.c * hw, 16), hw), pl.ds(pl.multiple_of(p.m * mine, LANE), mine)],
+        lsem.at[4],
+    )
+    tok_load = load(tokens, tok, lsem.at[5])
+    p.barrier(line=False)
+    gw = CubeGather(p, gsems[0:2], mix_view)
+
+    def to_twin(part, sub):
+        ref = mix_view(p.m ^ sub, part)
+        return remote(ref, ref, wtwin.at[0, part, sub], wtwin.at[1, part, sub], p.twin())
+
+    def from_twin(part, sub):
+        lo, size = row_parts[part]
+        ref = wm.at[
+            pl.ds(pl.multiple_of((1 - p.c) * hw + lo, 16), size),
+            pl.ds(pl.multiple_of((p.m ^ sub) * mine, LANE), mine),
+        ]
+        return remote(ref, ref, wtwin.at[0, part, sub], wtwin.at[1, part, sub], p.twin())
+
+    own_mix.wait()
+    gw.stage(0)
+    for part in range(p.bits):
+        to_twin(part, 0).start()
+    for copy in loads:
+        copy.wait()
+    step = 240
+
+    def project(i, _):
+        at = pl.ds(pl.multiple_of(i * step, 16), step)
+        pin[at, :] = dot(x[at, :], wv[0])
+        pf[at, :] = dot(x[at, :], wv[1])
+        pg[at, :] = dot(x[at, :], wv[2])
+        return 0
+
+    lax.fori_loop(0, rows // step, project, 0)
+    for s in range(1, p.bits):
+        gw.stage(s)
+    scan_forward(pin, pf, starts, bl, st, phasor, rowsq, a_re, a_im, b_re, b_im)
+    outs = [
+        load(src, dst, osem.at[i])
+        for i, (src, dst) in enumerate(((pin, pin_o), (pf, pf_o), (pg, pg_o), (st, st_o), (phasor, phasor_o)))
+    ]
+    ones = jnp.ones((8, mine), F32)
+    rs_out[...] = lax.dot_general(
+        ones, st[...] * st[...], (((1,), (1,)), ((), ())), precision=lax.Precision.HIGHEST, preferred_element_type=F32
+    )
+
+    def rs_copy(mask):
+        return remote(rs_out, rs_in.at[mask], rs_sem.at[0, mask], rs_sem.at[1, mask], p.peer(mask))
+
+    for mask in range(1, n_mp):
+        rs_copy(mask).start()
+    total = rs_out[...]
+    for mask in range(1, n_mp):
+        rs_copy(mask).wait_recv()
+        total = total + rs_in[mask]
+    inv = lax.rsqrt(total / width + EPS)
+    eighth = jnp.full((8, LANE), 0.125, F32)
+    rowsq[...] = lax.dot_general(
+        inv, eighth, (((0,), (0,)), ((), ())), precision=lax.Precision.HIGHEST, preferred_element_type=F32
+    )[:, :1]
+    outs.append(load(rowsq, r_o, osem.at[5]))
+    fine = 48
+    re_at = pl.ds(pl.multiple_of(p.m * ch, LANE), ch)
+    im_at = pl.ds(pl.multiple_of(half + p.m * ch, LANE), ch)
+
+    def gate_out(i, _):
+        at = pl.ds(pl.multiple_of(i * fine, 16), fine)
+        gate = pg[at, :]
+        value = (st[at, :] * rowsq[at, :] * gain[...] * (gate * sigmoid(gate))).astype(BF16)
+        mix[at, re_at] = value[:, :ch]
+        mix[at, im_at] = value[:, ch:]
+        return 0
+
+    spans = 2
+    span = rows // spans
+    gathers = []
+    for n in range(spans):
+        lax.fori_loop(n * span // fine, (n + 1) * span // fine, gate_out, 0)
+        for side in range(2):
+
+            def view(q, part, n=n, side=side):
+                lo, size = bounds(span, p.bits, 16)[part]
+                return mix.at[n * span + lo : n * span + lo + size, pl.ds(pl.multiple_of(side * half + q * ch, LANE), ch)]
+
+            at = 2 + 2 * (2 * n + side)
+            gathers.append(CubeGather(p, gsems[at : at + 2], view))
+            gathers[-1].stage(0)
+    gw.last()
+    for part in range(p.bits):
+        for sub in range(1, n_mp):
+            to_twin(part, sub).start()
+    for s in range(1, p.bits):
+        for g in gathers:
+            g.stage(s)
+    tok_load.wait()
+    for part in range(p.bits):
+        for sub in range(n_mp):
+            from_twin(part, sub).wait_recv()
+    outs.append(load(wm, wm_o, osem.at[6]))
+    for n in range(spans):
+        gathers[2 * n].last()
+        gathers[2 * n + 1].last()
+
+        def mix_rows(i, _):
+            at = pl.ds(pl.multiple_of(i * step, 16), step)
+            middle = tok[at, :].astype(F32) + dot(mix[at, :], wm[...])
+            r = lax.rsqrt(jnp.mean(middle * middle, axis=-1, keepdims=True) + EPS)
+            ffn_v[at, :] = (middle * r * gain_ffn[...]).astype(BF16)
+            for j in range(step // own):
+
+                @pl.when(p.m == i * (step // own) + j)
+                def _():
+                    mid_v[...] = middle[j * own : (j + 1) * own]
+                    rmid_o[...] = r[j * own : (j + 1) * own]
+
+            return 0
+
+        lax.fori_loop(n * span // step, (n + 1) * span // step, mix_rows, 0)
+        rows_at = slice(n * span, (n + 1) * span)
+        outs.append(load(ffn_v.at[rows_at], ffn_o.at[rows_at], osem.at[7 + 2 * n]))
+        outs.append(load(mix.at[rows_at], mix_o.at[rows_at], osem.at[8 + 2 * n]))
+    outs.append(load(mid_v, mid_o, osem.at[7 + 2 * spans]))
+    for copy in outs:
+        copy.wait()
+    gw.drain()
+    for g in gathers:
+        g.drain()
+    for part in range(p.bits):
+        for sub in range(n_mp):
+            to_twin(part, sub).wait_send()
+    for mask in range(1, n_mp):
+        rs_copy(mask).wait_send()
+
+
+def mixer_forward(n_dp, n_mp, cid, normed, w, tokens, starts, bl, gain, gain_ffn):
+    rows, width = normed.shape
+    mine = w.shape[1] // 4
+    own, lanes = rows // n_mp, mine // 2 // LANE
+    bits = n_mp.bit_length() - 1
+    full, part, lane = (rows, width), (rows, mine), (lanes, rows, LANE)
+    return pl.pallas_call(
+        functools.partial(mixer_kernel, n_dp, n_mp),
+        out_shape=(
+            *(jax.ShapeDtypeStruct(part, F32),) * 5,
+            jax.ShapeDtypeStruct((rows, 1), F32),
+            jax.ShapeDtypeStruct(full, BF16),
+            jax.ShapeDtypeStruct(full, BF16),
+            jax.ShapeDtypeStruct((own, width), F32),
+            jax.ShapeDtypeStruct((own, 1), F32),
+            jax.ShapeDtypeStruct((width, width), BF16),
+        ),
+        in_specs=[ANY] * 3 + [VMEM] * 4,
+        out_specs=(ANY,) * 9 + (VMEM, ANY),
+        scratch_shapes=[
+            pltpu.VMEM(full, BF16),
+            pltpu.VMEM((3, width, mine), BF16),
+            *[pltpu.VMEM(part, F32)] * 5,
+            pltpu.VMEM((rows, 1), F32),
+            *[pltpu.VMEM(lane, F32)] * 4,
+            pltpu.VMEM(full, BF16),
+            pltpu.VMEM((width, width), BF16),
+            pltpu.VMEM(full, BF16),
+            pltpu.VMEM(full, BF16),
+            pltpu.VMEM((own, width), F32),
+            pltpu.VMEM((8, rows), F32),
+            pltpu.VMEM((n_mp, 8, rows), F32),
+            pltpu.SemaphoreType.DMA((6,)),
+            pltpu.SemaphoreType.DMA((12,)),
+            pltpu.SemaphoreType.DMA((2, n_mp)),
+            pltpu.SemaphoreType.DMA((2, bits, n_mp)),
+            *CubeGather.scratch(n_mp) * 5,
+        ],
+        compiler_params=pltpu.CompilerParams(collective_id=cid, has_side_effects=True, vmem_limit_bytes=VMEM_LIMIT),
+        name="mixer_forward",
+    )(normed, w, tokens, starts, bl, gain, gain_ffn)
+
+
+def ffn_kernel(n_dp, n_mp, final, ffn_in, grad_out, w, *refs):
+    p = Place(n_dp, n_mp)
+    rows, width = ffn_in.shape
+    own = rows // n_mp
+    if final:
+        gffn1, down1, middle, r_mid, cot, tok, gain_ffn, w_mix, gsum, mixed, gmid, gain_part, gm, gb, rowdot = refs[:15]
+        refs = refs[15:]
+    else:
+        gsum, gffn, down = refs[:3]
+        refs = refs[3:]
+    a, wv, bv, bq, lsem, gsem = refs[:6]
+    sums, cube_g = refs[6:11], refs[11:14]
+    cube_d = (cube_g[0], *refs[14:16])
+    refs = refs[16:]
+    h = bv.shape[2]
+    shard = gsum.shape[1]
+    loads = [load(ffn_in, a.at[0], lsem.at[0])]
+    loads += [load(w.at[:, b * h : (b + 1) * h], wv.at[b], lsem.at[1 + b]) for b in range(3)]
+    loads += [load(grad_out, a.at[1], lsem.at[4])]
+    if final:
+        gffn, mid_v, cot_v, tok_v, wmb, gbr, gm_out, gm_in, gb_in, rd_out, rd_in, wsem, ssem, rsem = refs
+        late = [load(src, dst, lsem.at[5 + i]) for i, (src, dst) in enumerate(((middle, mid_v), (cot, cot_v), (tok, tok_v), (gffn1, gffn)))]
+        mine = gm.shape[2]
+        half, ch = width // 2, mine // 2
+
+        def mix_load(j, s):
+            q = p.m ^ j
+            return pltpu.make_async_copy(
+                w_mix.at[pl.ds(pl.multiple_of(s * half + q * ch, LANE), ch)], wmb.at[s], wsem.at[s]
+            )
+
+    p.barrier()
+    for copy in loads:
+        copy.wait()
+    step = 240
+
+    def forward(i, _):
+        at = pl.ds(pl.multiple_of(i * step, 16), step)
+        gate = dot(a[0, at, :], wv[0])
+        up = dot(a[0, at, :], wv[1])
+        sig = sigmoid(gate)
+        silu = gate * sig
+        grad = dot(a[1, at, :], wv[2])
+        values = (grad * up * sig * (1.0 + gate * (1.0 - sig)), grad * silu, silu * up)
+        for b in range(3):
+            bv[b, at, :] = values[b].astype(BF16)
+            if own % 16:
+                for j in range(step // own):
+                    bq[b, i * (step // own) + j] = values[b][j * own : (j + 1) * own].astype(BF16)
+        return 0
+
+    lax.fori_loop(0, rows // step, forward, 0)
+    cols = bounds(width, p.bits, LANE)
+
+    def rows_of(b, q):
+        return bq[b, q] if own % 16 else bv[b, pl.ds(pl.multiple_of(q * own, 16), own), :]
+
+    def part_g(q, part):
+        lo, size = cols[part]
+        at = slice(lo, lo + size)
+        return dot_trans(rows_of(0, q), wv[0, at, :]) + dot_trans(rows_of(1, q), wv[1, at, :])
+
+    def part_d(q, part):
+        lo, size = cols[part]
+        return dot_trans(rows_of(2, q), wv[2, lo : lo + size, :])
+
+    def piece(b, e):
+        left = jnp.where(b < 2, 0, 1)
+        return dot_rows(a[left, :, pl.ds(pl.multiple_of(e * shard, LANE), shard)], bv[b])
+
+    def finish(b, acc):
+        out = pltpu.make_async_copy(acc, gsum.at[b], gsem)
+        out.start()
+        out.wait()
+
+    total = RowSum(p, sums, piece, finish, False)
+    g_cube, d_cube = CubeSum(p, cube_g, part_g, width), CubeSum(p, cube_d, part_d, width)
+    n, chips = total.blocks, p.chips
+    g_cube.stage(0)
+    total.run(0, n)
+    for s in range(1, p.bits):
+        g_cube.stage(s)
+    if not final:
+        g_cube.drain()
+        d_cube.stage(0)
+    total.run(n, 2 * n)
+    if final:
+        late[3].wait()
+        g_cube.drain()
+    for part, (lo, size) in enumerate(cols):
+        value = g_cube.result(part)
+        gffn[:, lo : lo + size] = gffn[:, lo : lo + size] + value if final else value
+    if not final:
+        for s in range(1, p.bits):
+            d_cube.stage(s)
+    else:
+        for copy in late[:3]:
+            copy.wait()
+        mix_load(1, 0).start()
+        fine = 48 if own % 48 == 0 else own
+
+        def norm_back(i, gains):
+            at = pl.ds(pl.multiple_of(i * fine, fine), fine)
+            g = gffn[at, :]
+            n_own = mid_v[at, :] * r_mid[at, :]
+            gains = gains + jnp.sum((g * n_own).reshape(fine // 8, 8, width), axis=0)
+            gn = g * gain_ffn[...]
+            back = r_mid[at, :] * (gn - n_own * jnp.mean(gn * n_own, axis=-1, keepdims=True))
+            grad = cot_v[at, :].astype(F32) + back
+            gmid[at, :] = grad
+            low = grad.astype(BF16)
+            gbr[at, :] = low
+            dots = jnp.mean(low.astype(F32) * (mid_v[at, :] - tok_v[at, :].astype(F32)), axis=-1, keepdims=True)
+            rd_out[at, :] = jnp.broadcast_to(dots, (fine, LANE))
+            return gains
+
+        gains = lax.fori_loop(0, own // fine, norm_back, jnp.zeros((8, width), F32))
+        gain_part[...] = jnp.sum(gains, axis=0, keepdims=True)
+
+        def across(kind, j, owner):
+            send, recv, to = ssem.at[kind, j], rsem.at[kind, owner], p.peer(j)
+            if kind == 0:
+                return remote(gm_out.at[j], gm_in.at[owner], send, recv, to)
+            if kind == 1:
+                return remote(rd_out, rd_in.at[owner], send, recv, to)
+            here = pl.ds(pl.multiple_of((p.m ^ j) * mine, LANE), mine)
+            return remote(gbr.at[:, here], gb_in.at[owner], send, recv, to)
+
+        for j in range(1, n_mp):
+            across(1, j, p.m).start()
+        turns = [(j, s) for j in (*range(1, n_mp), 0) for s in range(2)]
+        for at, (j, s) in enumerate(turns):
+            mix_load(j, s).wait()
+            if at + 1 < len(turns):
+                mix_load(*turns[at + 1]).start()
+            value = dot_trans(gbr[...], wmb[s]).astype(BF16)
+            if j:
+                gm_out[j, :, s * ch : (s + 1) * ch] = value
+                if s:
+                    across(0, j, p.m).start()
+            else:
+                gm_in[p.m, :, s * ch : (s + 1) * ch] = value
+        for j in range(1, n_mp):
+            across(2, j, p.m).start()
+        gb_in[p.m] = gbr[:, pl.ds(pl.multiple_of(p.m * mine, LANE), mine)]
+        rd_in[p.m] = rd_out[...]
+        down_load = load(down1, gffn, lsem.at[9])
+        d_cube.stage(0)
+    total.run(2 * n, 3 * n)
+    if final:
+        for s in range(1, p.bits):
+            d_cube.stage(s)
+    total.run(3 * n, total.steps)
+    if final:
+        for j in range(1, n_mp):
+            for kind in range(3):
+                across(kind, j, p.m ^ j).wait_recv()
+        back = [load(src, dst, lsem.at[10 + i]) for i, (src, dst) in enumerate(((gm_in, gm), (gb_in, gb), (rd_in, rowdot)))]
+        down_load.wait()
+        for part, (lo, size) in enumerate(cols):
+            at = slice(lo, lo + size)
+            mixed[:, at] = (mid_v[:, at] + gffn[:, at] + d_cube.result(part)).astype(BF16)
+        for j in range(1, n_mp):
+            for kind in range(3):
+                across(kind, j, p.m).wait_send()
+        for copy in back:
+            copy.wait()
+    else:
+        for part, (lo, size) in enumerate(cols):
+            down[:, lo : lo + size] = d_cube.result(part)
+    d_cube.drain()
+    total.drain()
+
+
+def ffn_part(n_dp, n_mp, cid, ffn_in, grad_out, w, *rest):
+    rows, width = ffn_in.shape
+    h, shard, own = w.shape[1] // 3, width // n_dp, rows // n_mp
+    mine = width // n_mp
+    final = bool(rest)
+    f_own = jax.ShapeDtypeStruct((own, width), F32)
+    gsum = jax.ShapeDtypeStruct((3, shard, h), F32)
+    scratch = [
+        pltpu.VMEM((2, rows, width), BF16),
+        pltpu.VMEM((3, width, h), BF16),
+        pltpu.VMEM((3, rows, h), BF16),
+        pltpu.VMEM((3, n_mp, own, h) if own % 16 else (1, 1, 16, LANE), BF16),
+        pltpu.SemaphoreType.DMA((13,)),
+        pltpu.SemaphoreType.DMA,
+        *RowSum.scratch(n_dp, 3, shard, h),
+        *CubeSum.scratch(n_mp, own, width),
+        *CubeSum.scratch(n_mp, own, width)[1:],
+    ]
+    if final:
+        piece = jax.ShapeDtypeStruct((n_mp, own, mine), BF16)
+        outs = (
+            gsum, jax.ShapeDtypeStruct((own, width), BF16), f_own, jax.ShapeDtypeStruct((1, width), F32),
+            piece, piece, jax.ShapeDtypeStruct((n_mp, own, LANE), F32),
+        )
+        scratch += [
+            pltpu.VMEM((own, width), F32),
+            pltpu.VMEM((own, width), F32),
+            pltpu.VMEM((own, width), BF16),
+            pltpu.VMEM((own, width), BF16),
+            pltpu.VMEM((2, mine // 2, width), BF16),
+            pltpu.VMEM((own, width), BF16),
+            *[pltpu.VMEM((n_mp, own, mine), BF16)] * 3,
+            pltpu.VMEM((own, LANE), F32),
+            pltpu.VMEM((n_mp, own, LANE), F32),
+            pltpu.SemaphoreType.DMA((2,)),
+            pltpu.SemaphoreType.DMA((3, n_mp)),
+            pltpu.SemaphoreType.DMA((3, n_mp)),
+        ]
+        in_specs = [ANY] * 6 + [VMEM, ANY, ANY, VMEM, ANY]
+    else:
+        outs = (gsum, f_own, f_own)
+        in_specs = [ANY] * 3
+    return pl.pallas_call(
+        functools.partial(ffn_kernel, n_dp, n_mp, final),
+        out_shape=outs,
+        in_specs=in_specs,
+        out_specs=(ANY, VMEM, VMEM, VMEM, ANY, ANY, ANY)[: len(outs)],
+        scratch_shapes=scratch,
+        compiler_params=pltpu.CompilerParams(collective_id=cid, has_side_effects=True, vmem_limit_bytes=VMEM_LIMIT),
+        name="ffn_last" if final else "ffn_first",
+    )(ffn_in, grad_out, w, *rest)
+
+
+def project_kernel(
+    n_dp, n_mp, normed, mixed, g_in, g_f, g_g, g_b, g_split, w, gmid, tok, r_in, gain_in, gain_ffn_part, dgain, dbound,
+    gw, gtok, small, a, bv, bq, wv, lsem, rsend, rrecv, gall, *refs,
+):
+    p = Place(n_dp, n_mp)
+    rows, width = normed.shape
+    mine = bv.shape[2]
+    half, ch, own = width // 2, mine // 2, rows // n_mp
+    shard = gw.shape[2]
+    sums, cube_refs, vec = refs[:5], refs[5:8], SmallSum(p, refs[8:10])
+    loads = [load(normed, a.at[0], lsem.at[0])]
+    loads += [load(src, bv.at[i], lsem.at[1 + i]) for i, src in enumerate((g_in, g_f, g_g, g_b))]
+    loads += [load(mixed, a.at[1], lsem.at[5])]
+    late = [load(w.at[:, i * mine : (i + 1) * mine], wv.at[i], lsem.at[6 + i]) for i in range(3)]
+    if own % 16:
+        late.append(load(g_split, bq, lsem.at[9]))
+    p.barrier(far=True)
+    for copy in loads:
+        copy.wait()
+
+    def piece(b, e):
+        left = jnp.where(b < 3, 0, 1)
+        return dot_rows(a[left, :, pl.ds(pl.multiple_of(e * shard, LANE), shard)], bv[b])
+
+    def out_copy(b, mask, owner):
+        return remote(gall.at[b, owner], gall.at[b, owner], rsend.at[b, mask], rrecv.at[b, owner], p.peer(mask))
+
+    def finish(b, acc):
+        gall[b, p.m] = acc[...].astype(BF16)
+        for mask in range(1, n_mp):
+            out_copy(b, mask, p.m).start()
+
+    cols = bounds(width, p.bits, LANE)
+
+    def partial(q, part):
+        lo, size = cols[part]
+        value = 0.0
+        for b in range(3):
+            left = bq[b, q] if own % 16 else bv[b, pl.ds(pl.multiple_of(q * own, 16), own), :]
+            value = value + dot_trans(left, wv[b, lo : lo + size, :])
+        return value
+
+    total = RowSum(p, sums, piece, finish, True)
+    cube = CubeSum(p, cube_refs, partial, width)
+    tick = p.chips
+    total.run(0, tick)
+    for copy in late:
+        copy.wait()
+    cube.stage(0)
+    total.run(tick, 2 * tick)
+    for s in range(1, p.bits):
+        cube.stage(s)
+    total.run(2 * tick, 3 * tick)
+    for part, (lo, size) in enumerate(cols):
+        gtok[:, lo : lo + size] = cube.result(part)
+    fine = 48 if own % 48 == 0 else own
+
+    def norm_back(i, gains):
+        at = pl.ds(pl.multiple_of(i * fine, fine), fine)
+        g = gtok[at, :]
+        n_own = tok[at, :].astype(F32) * r_in[at, :]
+        gains = gains + jnp.sum((g * n_own).reshape(fine // 8, 8, width), axis=0)
+        gn = g * gain_in[...]
+        gtok[at, :] = gmid[at, :] + r_in[at, :] * (gn - n_own * jnp.mean(gn * n_own, axis=-1, keepdims=True))
+        return gains
+
+    gains = lax.fori_loop(0, own // fine, norm_back, jnp.zeros((8, width), F32))
+    vec.buf[0] = jnp.zeros((4, width), F32)
+    vec.buf[0, 0:1] = jnp.sum(gains, axis=0, keepdims=True)
+    vec.buf[0, 1:2] = gain_ffn_part[...]
+    here = pl.ds(pl.multiple_of(p.m * ch, LANE), ch)
+    vec.buf[0, 2:3, here] = dgain[:, :ch]
+    vec.buf[0, 2:3, pl.ds(pl.multiple_of(half + p.m * ch, LANE), ch)] = dgain[:, ch:]
+    vec.buf[0, 3:4, here] = dbound[...]
+    vec.twins()
+    total.run(3 * tick, 4 * tick)
+    vec.cube()
+    total.run(4 * tick, 5 * tick)
+    vec.line()
+    total.run(5 * tick, total.steps)
+    for b in range(4):
+        for mask in range(1, n_mp):
+            out_copy(b, mask, p.m ^ mask).wait_recv()
+    out = load(gall, gw, lsem.at[10])
+    small[...] = vec.result()
+    out.wait()
+    for b in range(4):
+        for mask in range(1, n_mp):
+            out_copy(b, mask, p.m).wait_send()
+    cube.drain()
+    total.drain()
+
+
+def project_back(n_dp, n_mp, cid, normed, mixed, g_in, g_f, g_g, g_b, w, gmid, tok, r_in, gain_in, *vectors):
+    rows, width = normed.shape
+    mine, shard, own = g_in.shape[1], width // n_dp, rows // n_mp
+    if own % 16:
+        g_split = jnp.stack([g.reshape(n_mp, own, mine) for g in (g_in, g_f, g_g)])
+    else:
+        g_split = jnp.zeros((1, 1, 16, LANE), BF16)
+    return pl.pallas_call(
+        functools.partial(project_kernel, n_dp, n_mp),
+        out_shape=(
+            jax.ShapeDtypeStruct((4, n_mp, shard, mine), BF16),
+            jax.ShapeDtypeStruct((own, width), F32),
+            jax.ShapeDtypeStruct((4, width), F32),
+        ),
+        in_specs=[ANY] * 8 + [VMEM] * 7,
+        out_specs=(ANY, VMEM, VMEM),
+        scratch_shapes=[
+            pltpu.VMEM((2, rows, width), BF16),
+            pltpu.VMEM((4, rows, mine), BF16),
+            pltpu.VMEM(g_split.shape, BF16),
+            pltpu.VMEM((3, width, mine), BF16),
+            pltpu.SemaphoreType.DMA((11,)),
+            pltpu.SemaphoreType.DMA((4, n_mp)),
+            pltpu.SemaphoreType.DMA((4, n_mp)),
+            pltpu.VMEM((4, n_mp, shard, mine), BF16),
+            *RowSum.scratch(n_dp, 4, shard, mine),
+            *CubeSum.scratch(n_mp, own, width),
+            *SmallSum.scratch(n_dp, n_mp, (4, width)),
+        ],
+        compiler_params=pltpu.CompilerParams(collective_id=cid, has_side_effects=True, vmem_limit_bytes=VMEM_LIMIT),
+        name="project_back",
+    )(normed, mixed, g_in, g_f, g_g, g_b, g_split, w, gmid, tok, r_in, gain_in, *vectors)
+
+
 def per_device(n_dp, n_mp, tokens, segment_ids, cotangent, gain_in, w_in, w_forget, w_outgate, bound_logit, gain_mix,
                w_mix, gain_ffn, w_gate, w_up, w_down):
     m, d = lax.axis_index("mp"), lax.axis_index("dp")
@@ -233,10 +1202,9 @@
     mine = 2 * ch
     own = rows // n_mp
     ffn = w_gate.shape[1]
-    shard = w_in.shape[0]
-
-    def from_peer(x, j):
-        return lax.ppermute(x, "mp", [(q, q ^ j) for q in range(n_mp)])
+    padded = -(-ffn // LANE) * LANE
+    cut = -(-padded // 2 // LANE) * LANE
+    parts = ((0, cut), (cut, padded - cut))
 
     def cols(x, at, size):
         return lax.dynamic_slice_in_dim(x, at, size, 1)
@@ -244,41 +1212,26 @@
     def own_channels(x):
         return jnp.concatenate([cols(x, m * ch, ch), cols(x, half + m * ch, ch)], axis=1)
 
-    def gather_rows(x):
-        out = jnp.zeros((x.shape[0] * n_mp, x.shape[1]), x.dtype)
-        for j in range(n_mp):
-            part = x if j == 0 else from_peer(x, j)
-            out = lax.dynamic_update_slice_in_dim(out, part, (m ^ j) * x.shape[0], 0)
-        return out
-
-    def scatter_sum(x):
-        total = lax.dynamic_slice_in_dim(x, m * own, own, 0)
-        for j in range(1, n_mp):
-            part = lax.dynamic_slice_in_dim(x, (m ^ j) * own, own, 0).astype(BF16)
-            total = total + from_peer(part, j).astype(F32)
-        return total
-
-    mixer_cols = jnp.concatenate([own_channels(w_in), own_channels(w_forget), own_channels(w_outgate)], axis=1)
-    w_cat = lax.all_gather(mixer_cols, "dp", axis=0, tiled=True)
-    mix_cols = cols(w_mix, m * mine, mine)
-    w_mix_q = lax.all_gather(mix_cols, "dp", axis=0, tiled=True)
-    wg = lax.all_gather(w_gate, "dp", axis=0, tiled=True)
-    wu = lax.all_gather(w_up, "dp", axis=0, tiled=True)
-    wd = lax.all_gather(w_down, "dp", axis=1, tiled=True)
-
-    core = lax.rem(d, 2)
-    hw = width // 2
-    part = lax.dynamic_slice_in_dim(w_mix_q, core * hw, hw, 0)
-    half_mix = jnp.zeros((hw, width), BF16)
-    for j in range(n_mp):
-        piece = part if j == 0 else from_peer(part, j)
-        half_mix = lax.dynamic_update_slice_in_dim(half_mix, piece, (m ^ j) * mine, 1)
-    other_mix = lax.ppermute(half_mix, "dp", [(q, q ^ 1) for q in range(n_dp)])
-    wm = jnp.zeros((width, width), BF16)
-    wm = lax.dynamic_update_slice_in_dim(wm, half_mix, core * hw, 0)
-    wm = lax.dynamic_update_slice_in_dim(wm, other_mix, (1 - core) * hw, 0)
-
-    grad_out = gather_rows(cotangent)
+    def own_rows(x):
+        return lax.dynamic_slice_in_dim(x, m * own, own, 0)
+
+    def gather_dp(x):
+        return lax.all_gather(x, "dp", axis=0, tiled=True)
+
+    w_cat = gather_dp(
+        jnp.concatenate(
+            [own_channels(w_in), own_channels(w_forget), own_channels(w_outgate), cols(w_mix, m * mine, mine)], axis=1
+        )
+    )
+    fill = ((0, 0), (0, padded - ffn))
+    gate_p, up_p, down_p = jnp.pad(w_gate, fill), jnp.pad(w_up, fill), jnp.pad(w_down.T, fill)
+    w_ffn = []
+    for lo, size in parts:
+        at = slice(lo, lo + size)
+        piece = jnp.concatenate([gate_p[:, at], up_p[:, at], down_p[:, at]], axis=1)
+        w_ffn.append(gather_dp(piece))
+
+    grad_out = gather_mp(n_dp, n_mp, 1, cotangent).reshape(rows, width)
 
     stream = tokens.astype(F32)
     ident = segment_ids[0]
@@ -286,81 +1239,20 @@
     starts = jnp.where(ident != previous, 1.0, 0.0).astype(F32)[:, None]
     r_in = lax.rsqrt(jnp.mean(stream * stream, axis=-1, keepdims=True) + EPS)
     normed = (stream * r_in * gain_in).astype(BF16)
-    pin = dot(normed, w_cat[:, :mine])
-    pf = dot(normed, w_cat[:, mine : 2 * mine])
-    pg = dot(normed, w_cat[:, 2 * mine :])
     bl = lax.dynamic_slice_in_dim(bound_logit, m * ch, ch, 0)[None]
     gain = own_channels(gain_mix[None])
+    pin, pf, pg, st, phasor, r_mix, mixer_out, ffn_in, middle, r_mid, wm = mixer_forward(
+        n_dp, n_mp, 2, normed, w_cat, tokens, starts, bl, gain, gain_ffn[None]
+    )
+
+    g_one, gffn, down = ffn_part(n_dp, n_mp, 3, ffn_in, grad_out, w_ffn[0])
+    tok_own = own_rows(tokens)
+    g_two, mixed, gmid, gain_ffn_part, gm, gb, rowdot = ffn_part(
+        n_dp, n_mp, 4, ffn_in, grad_out, w_ffn[1], gffn, down, middle, r_mid, cotangent, tok_own, gain_ffn[None], wm
+    )
+
     lanes = ch // LANE
     scratch = [pltpu.VMEM((lanes, rows, LANE), F32)] * 4
-    st, phasor, rowsq = call_local(
-        scan_forward,
-        (
-            jax.ShapeDtypeStruct((rows, mine), F32),
-            jax.ShapeDtypeStruct((rows, mine), F32),
-            jax.ShapeDtypeStruct((rows, 1), F32),
-        ),
-        scratch,
-        pin, pf, starts, bl,
-        name="scan_forward",
-    )
-    rowsq = lax.psum(rowsq[:, 0], "mp")[:, None]
-    r_mix = lax.rsqrt(rowsq / width + EPS)
-    mixer_mine = (st * r_mix * gain * (pg * jax.nn.sigmoid(pg))).astype(BF16)
-    mixer_out = jnp.zeros((rows, width), BF16)
-    for j in range(n_mp):
-        piece = mixer_mine if j == 0 else from_peer(mixer_mine, j)
-        mixer_out = lax.dynamic_update_slice_in_dim(mixer_out, piece[:, :ch], (m ^ j) * ch, 1)
-        mixer_out = lax.dynamic_update_slice_in_dim(mixer_out, piece[:, ch:], half + (m ^ j) * ch, 1)
-    branch = dot(mixer_out, wm)
-    middle = stream + branch
-    r_ffn = lax.rsqrt(jnp.mean(middle * middle, axis=-1, keepdims=True) + EPS)
-    ffn_in = (middle * r_ffn * gain_ffn).astype(BF16)
-
-    gate_val = dot(ffn_in, wg)
-    up_val = dot(ffn_in, wu)
-    sig = jax.nn.sigmoid(gate_val)
-    hidden = (gate_val * sig * up_val).astype(BF16)
-    grad_hidden = dot_trans(grad_out, wd)
-    grad_gate = (grad_hidden * up_val * sig * (1.0 + gate_val * (1.0 - sig))).astype(BF16)
-    grad_up = (grad_hidden * gate_val * sig).astype(BF16)
-    grad_ffn = scatter_sum(dot_trans(grad_gate, wg) + dot_trans(grad_up, wu))
-    g_down = lax.psum_scatter(dot_rows(grad_out, hidden).astype(BF16), "dp", scatter_dimension=0, tiled=True)
-    g_gate_up = lax.psum_scatter(
-        jnp.concatenate([dot_rows(ffn_in, grad_gate), dot_rows(ffn_in, grad_up)], axis=1).astype(BF16),
-        "dp", scatter_dimension=0, tiled=True,
-    )
-    down = scatter_sum(dot(hidden, wd))
-    row_at = m * own
-
-    def own_rows(x):
-        return lax.dynamic_slice_in_dim(x, row_at, own, 0)
-
-    middle_own = own_rows(middle)
-    mixed = (middle_own + down).astype(BF16)
-
-    r_own = own_rows(r_ffn)
-    n_own = middle_own * r_own
-    gain_ffn_part = jnp.sum(grad_ffn * n_own, axis=0)
-    gn = grad_ffn * gain_ffn
-    grad_middle = cotangent.astype(F32) + r_own * (gn - n_own * jnp.mean(gn * n_own, axis=-1, keepdims=True))
-    grad_branch = grad_middle.astype(BF16)
-    rowdot_own = jnp.mean(grad_branch.astype(F32) * (middle_own - own_rows(stream)), axis=-1, keepdims=True)
-    grad_mixer_own = dot_trans(grad_branch, wm)
-
-    gm = jnp.zeros((rows, mine), F32)
-    gb_cols = jnp.zeros((rows, mine), BF16)
-    rowdot = jnp.zeros((rows, 1), F32)
-    for j in range(n_mp):
-        q = m ^ j
-        piece = jnp.concatenate([cols(grad_mixer_own, q * ch, ch), cols(grad_mixer_own, half + q * ch, ch)], axis=1)
-        gb = cols(grad_branch, q * mine, mine)
-        rd = rowdot_own
-        if j:
-            piece, gb, rd = from_peer(piece, j), from_peer(gb, j), from_peer(rd, j)
-        gm = lax.dynamic_update_slice_in_dim(gm, piece, q * own, 0)
-        gb_cols = lax.dynamic_update_slice_in_dim(gb_cols, gb, q * own, 0)
-        rowdot = lax.dynamic_update_slice_in_dim(rowdot, rd, q * own, 0)
     gin, gf, gg, dgain, dbound = call_local(
         scan_backward,
         (
@@ -371,57 +1263,37 @@
             jax.ShapeDtypeStruct((1, ch), F32),
         ),
         scratch,
-        gm, pin, pf, pg, st, phasor, r_mix, rowdot, bl, gain,
+        gm.reshape(rows, mine), pin, pf, pg, st, phasor, r_mix, rowdot.reshape(rows, LANE)[:, :1], bl, gain,
         name="scan_backward",
     )
-    g_cat = jnp.concatenate([gin, gf, gg], axis=1)
-    g_mix = lax.psum_scatter(
-        jnp.concatenate([dot_rows(normed, g_cat), dot_rows(mixer_out, gb_cols)], axis=1).astype(BF16),
-        "dp", scatter_dimension=0, tiled=True,
+    g_mixer, grad_tokens, small = project_back(
+        n_dp, n_mp, 5, normed, mixer_out, gin, gf, gg, gb.reshape(rows, mine), w_cat, gmid, tok_own, own_rows(r_in),
+        gain_in[None], gain_ffn_part, dgain, dbound,
     )
-    grad_normed = scatter_sum(dot_trans(g_cat, w_cat))
-    s_own, ri_own = own_rows(stream), own_rows(r_in)
-    n_in = s_own * ri_own
-    gain_in_part = jnp.sum(grad_normed * n_in, axis=0)
-    gn_in = grad_normed * gain_in
-    grad_tokens = grad_middle + ri_own * (gn_in - n_in * jnp.mean(gn_in * n_in, axis=-1, keepdims=True))
-
-    g_win = jnp.zeros((shard, width), F32)
-    g_wf, g_wo, g_wm = g_win, g_win, g_win
-    for j in range(n_mp):
-        q = m ^ j
-        piece = (g_mix if j == 0 else from_peer(g_mix, j)).astype(F32)
-
-        def put(total, lo):
-            total = lax.dynamic_update_slice_in_dim(total, piece[:, lo : lo + ch], q * ch, 1)
-            return lax.dynamic_update_slice_in_dim(total, piece[:, lo + ch : lo + mine], half + q * ch, 1)
-
-        g_win, g_wf, g_wo = put(g_win, 0), put(g_wf, mine), put(g_wo, 2 * mine)
-        g_wm = lax.dynamic_update_slice_in_dim(g_wm, piece[:, 3 * mine :], q * mine, 1)
-
-    gmix_full = jnp.zeros((width,), F32)
-    gmix_full = lax.dynamic_update_slice_in_dim(gmix_full, dgain[0, :ch], m * ch, 0)
-    gmix_full = lax.dynamic_update_slice_in_dim(gmix_full, dgain[0, ch:], half + m * ch, 0)
-    gb_full = lax.dynamic_update_slice_in_dim(jnp.zeros((half,), F32), dbound[0], m * ch, 0)
-    small = lax.psum(jnp.concatenate([gain_in_part, gain_ffn_part, gmix_full, gb_full]), ("dp", "mp"))
-
-    def part_of(lo, size):
-        return lax.dynamic_slice_in_dim(small, lo + d * (size // n_dp), size // n_dp, 0)
-
+
+    def part_of(row, size):
+        return lax.dynamic_slice_in_dim(small[row], d * (size // n_dp), size // n_dp, 0)
+
+    g_mixer = g_mixer.astype(F32)
+
+    def by_channel(g):
+        return jnp.concatenate([g[q, :, lo : lo + ch] for lo in (0, ch) for q in range(n_mp)], axis=1)
+
+    g_ffn = jnp.concatenate([g_one, g_two], axis=2)[:, :, :ffn]
     return (
         mixed,
         grad_tokens,
         part_of(0, width),
-        g_win,
-        g_wf,
-        g_wo,
-        part_of(3 * width, half),
-        part_of(2 * width, width),
-        g_wm,
-        part_of(width, width),
-        g_gate_up[:, :ffn].astype(F32),
-        g_gate_up[:, ffn:].astype(F32),
-        g_down.astype(F32).T,
+        by_channel(g_mixer[0]),
+        by_channel(g_mixer[1]),
+        by_channel(g_mixer[2]),
+        part_of(3, half),
+        part_of(2, width),
+        jnp.concatenate([g_mixer[3, q] for q in range(n_mp)], axis=1),
+        part_of(1, width),
+        g_ffn[0],
+        g_ffn[1],
+        g_ffn[2].T,
     )
 
 

time: 760 us -> 639 us (0.84)
  Pallas kernels: 20.4 us -> 536 us
  waiting for transfers between devices: 263 us -> 16.1 us
  matrix products: 150 us -> 0 us
  local copies, waits for them, and re-layouts: 128 us -> 46 us
  blocking collectives: 78.2 us -> 0 us
  starting transfers between devices: 39.1 us -> 0.12 us
  other arithmetic: 54.3 us -> 16.5 us
    pallas_call x0 -> x5, Pallas kernels: none -> 525 us  [the longest x2 279 us: ffn_part(): pl.pallas_call(functools.partial(ffn_kernel, n_dp, n_mp, final), out_shap...]
    ppermute x31 -> x0, waiting for transfers between devices: 228 us -> none  [the longest x30 228 us: from_peer(): return lax.ppermute(x, 'mp', [(q, q ^ j) for q in range(n_mp)])]
    dot_general x17 -> x0, matrix products: 150 us -> none  [the longest x7 58.4 us: dot(): return jnp.dot(left, right, preferred_element_type=F32)]
    psum x2 -> x0, blocking collectives: 78.2 us -> none  [the longest x1 68.3 us: per_device(): lax.psum(jnp.concatenate([gain_in_part, gain_ffn_part, gmix_full, gb_full...]
    dynamic_update_slice x58 -> x0, local copies, waits for them, and re-layouts: 47.8 us -> none  [the longest x11 12.9 us: put(): lax.dynamic_update_slice_in_dim(total, piece[:, lo + ch:lo + mine], half...]
    ppermute x31 -> x0, starting transfers between devices: 38.8 us -> none  [the longest x30 38.8 us: from_peer(): return lax.ppermute(x, 'mp', [(q, q ^ j) for q in range(n_mp)])]
    slice x37 -> x11, local copies, waits for them, and re-layouts: 35.6 us -> 2.34 us  [the longest x10 1.67 us: per_device(): piece = jnp.concatenate([gate_p[:, at], up_p[:, at], down_p[:, at]], axis=1)]
    concatenate x6 -> x3, other arithmetic: 22.3 us -> 3.6 us  [the longest x2 2.11 us: per_device(): piece = jnp.concatenate([gate_p[:, at], up_p[:, at], down_p[:, at]], axis=1)]
  transfers between devices with their start and end apart: 39 -> 3, of which waited for: 17 -> 2; matrix products, arithmetic and copies ran while one was open for 33% -> 3% of each run, Pallas kernels for 1% -> 47%
where the time goes in v2:
time: 639 us; the launch traced here: 630 us
  Pallas kernels  536 us (84%)
  local copies, waits for them, and re-layouts  46 us (7%)
  other arithmetic  16.5 us (3%)
  waiting for transfers between devices  16.1 us (3%)
  between operations  15.2 us (2%)
    pallas_call x2, Pallas kernels, ffn_part(): pl.pallas_call(functools.partial(ffn_kernel, n_dp, n_mp, final), out_shap...  279 us
    pallas_call x1, Pallas kernels, project_back(): pl.pallas_call(functools.partial(project_kernel, n_dp, n_mp), out_shape=(...  111 us
    pallas_call x1, Pallas kernels, mixer_forward(): pl.pallas_call(functools.partial(mixer_kernel, n_dp, n_mp), out_shape=(*(...  89.3 us
    pallas_call x1, Pallas kernels, gather_mp(): pl.pallas_call(functools.partial(gather_kernel, n_dp, n_mp), out_shape=ja...  46 us
    unnamed x88, local copies, waits for them, and re-layouts  25.8 us
    all_gather x3, waiting for transfers between devices, gather_dp(): return lax.all_gather(x, 'dp', axis=0, tiled=True)  16 us
  transfers between devices with their start and end apart: 3, of which 2 were waited for; matrix products, arithmetic and copies ran while one was open for 3% of the time, Pallas kernels for 47%

profile of v2, /device:TPU:8, one launch (start us, length us, event | category | flops | bytes accessed | tf_op | source)
XLA Modules:
  0.0 629.7 jit_solution(4819067517530772603)
XLA Ops:
  7.2 1.0 dynamic-slice_dynamic-update-slice_fusion.6
  8.2 0.9 dynamic-slice_dynamic-update-slice_fusion.5
  9.1 0.9 dynamic-slice_dynamic-update-slice_fusion.4
  10.1 0.9 dynamic-slice_dynamic-update-slice_fusion.3
  11.0 0.9 dynamic-slice_dynamic-update-slice_fusion.2
  11.9 0.9 dynamic-slice_dynamic-update-slice_fusion.1
  12.8 1.0 dynamic-slice_dynamic-update-slice_fusion
  13.8 1.0 copy-done.19
  15.9 1.1 pad_maximum_fusion.1
  17.2 0.8 slice-done.1
  18.1 1.0 pad_maximum_fusion.2
  20.9 46.0 %gather_mp.1 = bf16[4,240,2048]{2,1,0:T(8,128)(2,1)} custom-call(bf16[240,2048]{1,0:T(8,128)(2,1)} %refs_4_.1), custom_call_target="tpu_custom_call" | custom-call | tf_op jit(solution)/shard_map/gather_mp/pallas_call | solution.py:627
  66.9 3.0 fusion
  70.0 0.8 copy.38.r_in
  70.8 1.3 dynamic_slice.63
  72.1 0.8 fusion.29
  73.4 2.2 constant_dynamic-slice_fusion.4.refs_5_.tok
  75.7 0.8 compare_select_fusion.starts
  76.5 5.1 fusion.2.normed
  81.6 13.9 %all-gather.4.cloned.1.call-done.w = bf16[2048,2048]{1,0:T(8,128)(2,1)} async-done(((bf16[256,2048]{1,0:T(8,128)(2,1)}), bf16[2048,2048]{1,0:T(8,128)(2,1)}) %all-gather.4.cloned.1.call-update) | async-done | bytes 8388624 | tf_op jit(solution)/shard_map/all_gather | solution.py:1219
  95.6 89.3 %mixer_forward.1 = (f32[960,512]{1,0:T(8,128)}, f32[960,512]{1,0:T(8,128)}, f32[960,512]{1,0:T(8,128)}, f32[960,512]{1,0:T(8,128)}, f32[960,512]{1,0:T(8,128)}, ...) custom-call(bf16[960,2048]{1,0:T(8,128)(2,1)} %fusion.2.normed, ...), custom_call_target="tpu_custom_call" | custom-call | tf_op jit(solution)/shard_map/mixer_forward/pallas_call | solution.py:805
  184.9 2.1 all-gather.8.cloned.1.call-done.w
  186.9 157.8 %ffn_first.1 = (f32[3,256,768]{2,1,0:T(8,128)}, f32[240,2048]{1,0:T(8,128)}, f32[240,2048]{1,0:T(8,128)}) custom-call(bf16[960,2048]{1,0:T(8,128)(2,1)} %get-tuple-element.42.ffn_in, bf16[960,2048]{1,0:T(8,128)(2,1)} %bitcast.143, bf16[2048,2304]{1,0:T(8,128)(2,1)} %all-gather.8.cloned.1.call-done.w), custom_call_target="tpu_custom_call" | custom-call | tf_op jit(solution)/shard_map/ffn_first/pallas_call | solution.py:1058
  344.9 121.6 %ffn_last.1 = (f32[3,256,640]{2,1,0:T(8,128)}, bf16[240,2048]{1,0:T(8,128)(2,1)}, f32[240,2048]{1,0:T(8,128)}, f32[1,2048]{1,0:T(1,128)}, bf16[4,240,512]{2,1,0:...) custom-call(bf16[960,2048]{1,0:T(8,128)(2,1)} %get-tuple-element.42.ffn_in, ...), custom_call_target="tpu_custom_call" | custom-call | tf_op jit(solution)/shard_map/ffn_last/pallas_call | solution.py:1058
  466.5 1.2 copy-done.3
  467.7 1.0 copy-done.5
  468.7 10.3 %scan_backward.1 = (bf16[960,512]{1,0:T(8,128)(2,1)S(1)}, bf16[960,512]{1,0:T(8,128)(2,1)S(1)}, bf16[960,512]{1,0:T(8,128)(2,1)S(1)}, f32[1,512]{1,0:T(1,128)S(1)}, f32[1,256]{1,0:T(1,128)S(1)}) custom-call(bf16[960,512]{1,0:T(8,128)(2,1)S(1)} %bitcast.139, f32[960,512]{1,0:T(8,128)} %get-tuple-element.51.pin, f32[960,512]{1,0:T(8,128)} %get-tuple-element.52.pf, ...), custom_call_target="tpu_custom_call" | custom-call | tf_op jit(solution)/shard_map/scan_backward/pallas_call | solution.py:218
  479.1 0.9 copy-done
  480.0 0.9 copy-done.1
  481.0 0.9 copy-done.2
  483.6 110.7 %project_back.1 = (bf16[4,4,256,512]{3,2,1,0:T(8,128)(2,1)}, f32[240,2048]{1,0:T(8,128)}, f32[4,2048]{1,0:T(4,128)}) custom-call(bf16[960,2048]{1,0:T(8,128)(2,1)} %fusion.2.normed, bf16[960,2048]{1,0:T(8,128)(2,1)} %get-tuple-element.49.mixed, bf16[960,512]{1,0:T(8,128)(2,1)} %copy-done, bf16[960,512]{1,0:T(8,128)(2,1)} %copy-done.1, ...), custom_call_target="tpu_custom_call" | custom-call | tf_op jit(solution)/shard_map/project_back/pallas_call | solution.py:1169
  594.4 3.3 convert_element_type.11
  597.7 1.4 slice_bitcast_fusion.9
  599.1 2.0 slice_bitcast_fusion
  603.3 1.3 copy-done.24
  604.8 1.4 copy-done.18
  606.3 1.9 slice_bitcast_fusion.3
  608.1 1.5 copy.39
  609.7 1.1 fusion.26
  610.8 1.0 fusion.25
  611.8 1.1 fusion.24
  613.0 1.0 fusion.23
  614.1 1.2 constant_dynamic-slice_fusion.3
  615.9 1.8 fusion.3
  617.7 1.1 fusion.27
  618.8 1.5 pad_maximum_fusion
  620.3 0.9 copy.70
  621.7 1.3 copy.71
  (96 shorter events, 8.3 us)
Async XLA Ops:
  7.2 7.7 %copy-start.21 = (bf16[1408,256]{1,0:T(8,128)(2,1)S(1)}, bf16[1408,256]{1,0:T(8,128)(2,1)}, u32[]{:S(2)}) copy-start(bf16[1408,256]{1,0:T(8,128)(2,1)} %param.27) | copy-start | bytes 2162692
  7.2 88.4 %all-gather.4.cloned.1.call-start = ((), (), s32[]{:S(2)}) async-start(), calls=%async_computation | async-start | bytes 9437184 | tf_op jit(solution)/shard_map/all_gather | solution.py:1219
  13.8 1.0 copy-start.19
  14.8 1.0 slice-start
  14.8 1.1 slice-start.2
  14.9 172.1 %all-gather.8.cloned.1.call-start = ((), (), s32[]{:S(2)}) async-start(), calls=%async_computation.2 | async-start | bytes 10616832 | tf_op jit(solution)/shard_map/all_gather | solution.py:1219
  17.0 1.0 slice-start.1
  17.0 1.1 slice-start.3
  17.1 327.8 %all-gather.6.cloned.1.call-start = ((), (), s32[]{:S(2)}) async-start(), calls=%async_computation.1 | async-start | bytes 8847360 | tf_op jit(solution)/shard_map/all_gather | solution.py:1219
  17.2 2.0 copy-start.27
  69.9 6.7 %copy-start.22 = (f32[2048]{0:T(1024)S(1)}, f32[2048]{0:T(1024)}, u32[]{:S(2)}) copy-start(f32[2048]{0:T(1024)} %param.17) | copy-start | bytes 24580
  344.8 121.7 %copy-start.4 = (f32[960,1]{1,0:T(8,128)S(1)}, f32[960,1]{1,0:T(8,128)}, u32[]{:S(2)}) copy-start(f32[960,1]{1,0:T(8,128)} %get-tuple-element.56.r) | copy-start | bytes 11524
  344.8 121.7 %copy-start.6 = (f32[1,512]{1,0:T(1,128)S(1)}, f32[1,512]{1,0:T(1,128)}, u32[]{:S(2)}) copy-start(f32[1,512]{1,0:T(1,128)} %pad_maximum_fusion.3.gain) | copy-start | bytes 6148
  344.9 121.7 %copy-start.7 = (f32[256]{0:T(256)S(1)}, f32[256]{0:T(256)}, u32[]{:S(2)}) copy-start(f32[256]{0:T(256)} %dynamic_slice.63) | copy-start | bytes 3076
  466.5 1.2 copy-start.3
  467.7 1.0 copy-start.5
  479.1 0.9 copy-start
  480.0 0.9 copy-start.1
  481.0 0.9 copy-start.2
  481.9 0.6 copy-start.8
  482.5 0.6 copy-start.9
  599.1 2.0 copy-start.26
  601.1 1.4 copy-start.10
  601.9 2.7 copy-start.12
  602.0 1.3 copy-start.23
  603.3 1.3 copy-start.24
  604.6 1.5 copy-start.18
  609.7 4.3 copy-start.11
  611.8 7.0 %copy-start.13 = (f32[256,512]{1,0:T(8,128)S(1)}, f32[256,512]{1,0:T(8,128)}, u32[]{:S(2)}) copy-start(f32[256,512]{1,0:T(8,128)} %get-tuple-element.110) | copy-start | bytes 1572868
  611.8 7.0 %copy-start.14 = (f32[256,512]{1,0:T(8,128)S(1)}, f32[256,512]{1,0:T(8,128)}, u32[]{:S(2)}) copy-start(f32[256,512]{1,0:T(8,128)} %get-tuple-element.111) | copy-start | bytes 1572868
  611.8 7.0 %copy-start.15 = (f32[256,512]{1,0:T(8,128)S(1)}, f32[256,512]{1,0:T(8,128)}, u32[]{:S(2)}) copy-start(f32[256,512]{1,0:T(8,128)} %get-tuple-element.112) | copy-start | bytes 1572868
  611.8 7.0 %copy-start.16 = (f32[256,512]{1,0:T(8,128)S(1)}, f32[256,512]{1,0:T(8,128)}, u32[]{:S(2)}) copy-start(f32[256,512]{1,0:T(8,128)} %get-tuple-element.113) | copy-start | bytes 1572868
  614.1 6.3 copy-start.25
  618.8 1.5 copy-start.20
  618.8 2.9 copy-start.17
Sparse Core Ops, SparseCore 0:
  14.9 80.5 all-gather.3
  97.8 89.1 all-gather.7
  189.2 125.2 all-gather.5

commit v3 on v2

--- a/solution.py
+++ b/solution.py
@@ -612,60 +612,179 @@
         return total
 
 
-def gather_kernel(n_dp, n_mp, mine, whole, lsem, send, recv):
-    p = Place(n_dp, n_mp)
-    p.barrier(line=False, twin=False)
-    own = load(mine, whole.at[p.m], lsem)
-    for mask in range(1, n_mp):
-        remote(mine, whole.at[p.m], send.at[mask], recv.at[p.m], p.peer(mask)).start()
-    own.wait()
-    for mask in range(1, n_mp):
-        remote(mine, whole.at[p.m ^ mask], send.at[mask], recv.at[p.m ^ mask], p.peer(mask)).wait()
-
-
-def gather_mp(n_dp, n_mp, cid, x):
-    return pl.pallas_call(
-        functools.partial(gather_kernel, n_dp, n_mp),
-        out_shape=jax.ShapeDtypeStruct((n_mp, *x.shape), x.dtype),
-        in_specs=[ANY],
-        out_specs=ANY,
-        scratch_shapes=[
-            pltpu.SemaphoreType.DMA,
-            pltpu.SemaphoreType.DMA((n_mp,)),
-            pltpu.SemaphoreType.DMA((n_mp,)),
-        ],
-        compiler_params=pltpu.CompilerParams(collective_id=cid, has_side_effects=True),
-        name="gather_mp",
-    )(x)
+class RowGather:
+    @staticmethod
+    def scratch(n_dp, units):
+        return [pltpu.SemaphoreType.DMA((5, units, n_dp // 2))]
+
+    def __init__(self, place, refs, src, dst):
+        self.p, self.src, self.dst = place, src, dst
+        (self.sem,) = refs
+
+    def hop(self, u, e, side, own=False):
+        p = self.p
+        here = self.dst(u, e, p.c)
+        device = (p.chip(1), p.chip(-1), p.twin())[side]
+        recv = self.sem.at[4 if side == 2 else 3, u, e]
+        return remote(self.src(u) if own else here, here, self.sem.at[side, u, e], recv, device)
+
+    def start(self, u):
+        p = self.p
+
+        @pl.when(p.k < p.chips - 1)
+        def _():
+            self.hop(u, p.k, 0, True).start()
+
+        @pl.when(p.k > 0)
+        def _():
+            self.hop(u, p.k, 1, True).start()
+
+        self.hop(u, p.k, 2, True).start()
+
+    def forward(self, u, s):
+        p = self.p
+
+        @pl.when(p.k - s >= 0)
+        def _():
+            self.hop(u, p.k - s, 0).wait_recv()
+
+            @pl.when(p.k < p.chips - 1)
+            def _():
+                self.hop(u, p.k - s, 0).start()
+
+            self.hop(u, p.k - s, 2).start()
+
+        @pl.when(p.k + s < p.chips)
+        def _():
+            self.hop(u, p.k + s, 1).wait_recv()
+
+            @pl.when(p.k > 0)
+            def _():
+                self.hop(u, p.k + s, 1).start()
+
+            self.hop(u, p.k + s, 2).start()
+
+    def finish(self, u):
+        p = self.p
+        for e in range(p.chips):
+            there = self.dst(u, e, 1 - p.c)
+            remote(there, there, self.sem.at[2, u, e], self.sem.at[4, u, e], p.twin()).wait_recv()
+
+    def drain(self, u):
+        p = self.p
+        for e in range(p.chips):
+
+            @pl.when((e <= p.k) & (p.k < p.chips - 1))
+            def _():
+                self.hop(u, e, 0).wait_send()
+
+            @pl.when((e >= p.k) & (p.k > 0))
+            def _():
+                self.hop(u, e, 1).wait_send()
+
+            self.hop(u, e, 2).wait_send()
 
 
 def mixer_kernel(
-    n_dp, n_mp, normed, w, tokens, starts, bl, gain, gain_ffn,
-    pin_o, pf_o, pg_o, st_o, phasor_o, r_o, mix_o, ffn_o, mid_o, rmid_o, wm_o,
-    x, wv, pin, pf, pg, st, phasor, rowsq, a_re, a_im, b_re, b_im, mix, wm, tok, ffn_v, mid_v, rs_out, rs_in,
-    lsem, osem, rs_sem, wtwin, *gsems,
+    n_dp, n_mp, w_in, w_forget, w_outgate, w_mix, w_gate, w_up, w_down, cot, tokens, ident, bound, gain_mix, gain_in, gain_ffn,
+    normed_o, rin_o, pin_o, pf_o, pg_o, st_o, phasor_o, r_o, mix_o, ffn_o, mid_o, rmid_o, wm_o, wcat_o, one_o, one_d, cot_o,
+    x, wv, wq, pin, pf, pg, st, phasor, rowsq, rin, starts, bl, gain, a_re, a_im, b_re, b_im, mix, wm, tok, ffn_v, mid_v, rs_out, rs_in,
+    lsem, osem, rs_sem, wtwin, csem, *gsems,
 ):
     p = Place(n_dp, n_mp)
-    rows, width = normed.shape
+    rows, width = tokens.shape
     mine = pin.shape[1]
     half, ch = width // 2, mine // 2
     own = rows // n_mp
     hw = width // 2
+    shard, h = w_in.shape[0], one_o.shape[2]
     row_parts = bounds(hw, p.bits, 16)
 
     def mix_view(q, part):
         lo, size = row_parts[part]
         return wm.at[pl.ds(pl.multiple_of(p.c * hw + lo, 16), size), pl.ds(pl.multiple_of(q * mine, LANE), mine)]
 
-    loads = [load(normed, x, lsem.at[0])]
-    loads += [load(w.at[:, i * mine : (i + 1) * mine], wv.at[i], lsem.at[1 + i]) for i in range(3)]
+    def rows_at(e, c):
+        return pl.ds(pl.multiple_of((2 * e + c) * shard, 16), shard)
+
+    def lanes_at(at, size):
+        return pl.ds(pl.multiple_of(at, LANE), size)
+
+    def unit_src(u):
+        if u < 4:
+            return unit_dst(u, p.k, p.c)
+        return (w_gate.at[:, :h], w_up.at[:, :h], w_down.at[:h])[u - 4]
+
+    def unit_dst(u, e, c):
+        if u == 6:
+            return one_d.at[:, lanes_at((2 * e + c) * shard, shard)]
+        return (wv.at[u] if u < 3 else wq if u == 3 else one_o.at[u - 4]).at[rows_at(e, c)]
+
+    mine_at = rows_at(p.k, p.c)
+    keep = {3: [load(w_mix.at[:, lanes_at(p.m * mine, mine)], wq.at[mine_at], lsem.at[1])]}
+    for u, w in enumerate((w_in, w_forget, w_outgate)):
+        keep[u] = [
+            load(w.at[:, lanes_at(side * half + p.m * ch, ch)], wv.at[u, mine_at, side * ch : (side + 1) * ch], lsem.at[2 + 2 * u + side])
+            for side in range(2)
+        ]
+    tok_load = load(tokens, tok, lsem.at[0])
+    vectors = [
+        load(bound.at[:, lanes_at(p.m * ch, ch)], bl, lsem.at[10]),
+        *[
+            load(gain_mix.at[:, lanes_at(side * half + p.m * ch, ch)], gain.at[:, side * ch : (side + 1) * ch], lsem.at[11 + side])
+            for side in range(2)
+        ],
+    ]
+    first_own = [load(unit_src(u), unit_dst(u, p.k, p.c), lsem.at[9 + u]) for u in range(4, 7)]
+    cot_own = load(cot, cot_o.at[p.m], lsem.at[8])
+    p.barrier()
+    z = RowGather(p, gsems[:1], unit_src, unit_dst)
+    gsems = gsems[1:]
+    order = (3, 0, 1, 2)
+    for u in order:
+        for copy in keep[u]:
+            copy.wait()
+        z.start(u)
+
+    def cot_copy(mask, owner):
+        return remote(cot, cot_o.at[owner], csem.at[0, mask], csem.at[1, owner], p.peer(mask))
+
+    for mask in range(1, n_mp):
+        cot_copy(mask, p.m).start()
+    tok_load.wait()
+    fine = 48
+
+    def norm_in(i, _):
+        at = pl.ds(pl.multiple_of(i * fine, 16), fine)
+        v = tok[at, :].astype(F32)
+        r = lax.rsqrt(jnp.mean(v * v, axis=-1, keepdims=True) + EPS)
+        rin[at, :] = r
+        x[at, :] = (v * r * gain_in[...]).astype(BF16)
+        return 0
+
+    lax.fori_loop(0, rows // fine, norm_in, 0)
+    eighth = jnp.full((8, LANE), 0.125, F32)
+    ids = lax.dot_general(
+        jnp.broadcast_to(ident[...].astype(F32), (8, rows)), eighth, (((0,), (0,)), ((), ())),
+        precision=lax.Precision.HIGHEST, preferred_element_type=F32,
+    )[:, :1]
+    before = jnp.concatenate([ids[:1] - 1.0, ids[:-1]], axis=0)
+    starts[...] = jnp.where(jnp.abs(ids - before) > 0.5, 1.0, 0.0)
+    for copy in vectors:
+        copy.wait()
+    outs = [load(x, normed_o, osem.at[0]), load(rin, rin_o, osem.at[1])]
+    for s in range(1, p.chips - 1):
+        for u in order:
+            z.forward(u, s)
+    for u in range(4, 7):
+        z.start(u)
+    z.forward(3, p.chips - 1)
+    z.finish(3)
     own_mix = load(
-        w.at[pl.ds(pl.multiple_of(p.c * hw, 16), hw), 3 * mine : 4 * mine],
+        wq.at[pl.ds(pl.multiple_of(p.c * hw, 16), hw)],
         wm.at[pl.ds(pl.multiple_of(p.c * hw, 16), hw), pl.ds(pl.multiple_of(p.m * mine, LANE), mine)],
-        lsem.at[4],
+        lsem.at[9],
     )
-    tok_load = load(tokens, tok, lsem.at[5])
-    p.barrier(line=False)
     gw = CubeGather(p, gsems[0:2], mix_view)
 
     def to_twin(part, sub):
@@ -684,23 +803,28 @@
     gw.stage(0)
     for part in range(p.bits):
         to_twin(part, 0).start()
-    for copy in loads:
-        copy.wait()
     step = 240
 
-    def project(i, _):
-        at = pl.ds(pl.multiple_of(i * step, 16), step)
-        pin[at, :] = dot(x[at, :], wv[0])
-        pf[at, :] = dot(x[at, :], wv[1])
-        pg[at, :] = dot(x[at, :], wv[2])
-        return 0
-
-    lax.fori_loop(0, rows // step, project, 0)
+    def project(u, out):
+        z.forward(u, p.chips - 1)
+        z.finish(u)
+
+        def body(i, _):
+            at = pl.ds(pl.multiple_of(i * step, 16), step)
+            out[at, :] = dot(x[at, :], wv[u])
+            return 0
+
+        lax.fori_loop(0, rows // step, body, 0)
+
+    project(0, pin)
+    project(1, pf)
+    project(2, pg)
+    outs += [load(wv.at[u], wcat_o.at[u], osem.at[2 + u]) for u in range(3)]
     for s in range(1, p.bits):
         gw.stage(s)
     scan_forward(pin, pf, starts, bl, st, phasor, rowsq, a_re, a_im, b_re, b_im)
-    outs = [
-        load(src, dst, osem.at[i])
+    outs += [
+        load(src, dst, osem.at[5 + i])
         for i, (src, dst) in enumerate(((pin, pin_o), (pf, pf_o), (pg, pg_o), (st, st_o), (phasor, phasor_o)))
     ]
     ones = jnp.ones((8, mine), F32)
@@ -713,17 +837,20 @@
 
     for mask in range(1, n_mp):
         rs_copy(mask).start()
+    gw.last()
+    for part in range(p.bits):
+        for sub in range(1, n_mp):
+            to_twin(part, sub).start()
+    z.forward(4, 1)
     total = rs_out[...]
     for mask in range(1, n_mp):
         rs_copy(mask).wait_recv()
         total = total + rs_in[mask]
     inv = lax.rsqrt(total / width + EPS)
-    eighth = jnp.full((8, LANE), 0.125, F32)
     rowsq[...] = lax.dot_general(
         inv, eighth, (((0,), (0,)), ((), ())), precision=lax.Precision.HIGHEST, preferred_element_type=F32
     )[:, :1]
-    outs.append(load(rowsq, r_o, osem.at[5]))
-    fine = 48
+    outs.append(load(rowsq, r_o, osem.at[10]))
     re_at = pl.ds(pl.multiple_of(p.m * ch, LANE), ch)
     im_at = pl.ds(pl.multiple_of(half + p.m * ch, LANE), ch)
 
@@ -749,18 +876,15 @@
             at = 2 + 2 * (2 * n + side)
             gathers.append(CubeGather(p, gsems[at : at + 2], view))
             gathers[-1].stage(0)
-    gw.last()
-    for part in range(p.bits):
-        for sub in range(1, n_mp):
-            to_twin(part, sub).start()
+    z.forward(5, 1)
     for s in range(1, p.bits):
         for g in gathers:
             g.stage(s)
-    tok_load.wait()
+    z.forward(6, 1)
     for part in range(p.bits):
         for sub in range(n_mp):
             from_twin(part, sub).wait_recv()
-    outs.append(load(wm, wm_o, osem.at[6]))
+    outs.append(load(wm, wm_o, osem.at[11]))
     for n in range(spans):
         gathers[2 * n].last()
         gathers[2 * n + 1].last()
@@ -780,12 +904,28 @@
             return 0
 
         lax.fori_loop(n * span // step, (n + 1) * span // step, mix_rows, 0)
-        rows_at = slice(n * span, (n + 1) * span)
-        outs.append(load(ffn_v.at[rows_at], ffn_o.at[rows_at], osem.at[7 + 2 * n]))
-        outs.append(load(mix.at[rows_at], mix_o.at[rows_at], osem.at[8 + 2 * n]))
-    outs.append(load(mid_v, mid_o, osem.at[7 + 2 * spans]))
+        at = slice(n * span, (n + 1) * span)
+        outs.append(load(ffn_v.at[at], ffn_o.at[at], osem.at[12 + 2 * n]))
+        outs.append(load(mix.at[at], mix_o.at[at], osem.at[13 + 2 * n]))
+        if n == 0:
+            z.forward(4, 2)
+    outs.append(load(mid_v, mid_o, osem.at[12 + 2 * spans]))
+    z.forward(5, 2)
+    z.forward(6, 2)
+    for s in range(3, p.chips):
+        for u in range(4, 7):
+            z.forward(u, s)
+    for u in range(4, 7):
+        z.finish(u)
+    for mask in range(1, n_mp):
+        cot_copy(mask, p.m ^ mask).wait_recv()
+    cot_own.wait()
+    for copy in first_own:
+        copy.wait()
     for copy in outs:
         copy.wait()
+    for u in range(7):
+        z.drain(u)
     gw.drain()
     for g in gathers:
         g.drain()
@@ -794,32 +934,38 @@
             to_twin(part, sub).wait_send()
     for mask in range(1, n_mp):
         rs_copy(mask).wait_send()
-
-
-def mixer_forward(n_dp, n_mp, cid, normed, w, tokens, starts, bl, gain, gain_ffn):
-    rows, width = normed.shape
-    mine = w.shape[1] // 4
+        cot_copy(mask, p.m).wait_send()
+
+
+def mixer_forward(n_dp, n_mp, cid, h, *args):
+    rows, width = args[8].shape
+    mine = width // n_mp
     own, lanes = rows // n_mp, mine // 2 // LANE
     bits = n_mp.bit_length() - 1
     full, part, lane = (rows, width), (rows, mine), (lanes, rows, LANE)
+
+    def f32(*shape):
+        return jax.ShapeDtypeStruct(shape, F32)
+
+    def bf16(*shape):
+        return jax.ShapeDtypeStruct(shape, BF16)
+
     return pl.pallas_call(
         functools.partial(mixer_kernel, n_dp, n_mp),
         out_shape=(
-            *(jax.ShapeDtypeStruct(part, F32),) * 5,
-            jax.ShapeDtypeStruct((rows, 1), F32),
-            jax.ShapeDtypeStruct(full, BF16),
-            jax.ShapeDtypeStruct(full, BF16),
-            jax.ShapeDtypeStruct((own, width), F32),
-            jax.ShapeDtypeStruct((own, 1), F32),
-            jax.ShapeDtypeStruct((width, width), BF16),
+            bf16(*full), f32(rows, 1), *(f32(*part),) * 5, f32(rows, 1), bf16(*full), bf16(*full), f32(own, width), f32(own, 1),
+            bf16(width, width), bf16(3, width, mine), bf16(2, width, h), bf16(h, width), bf16(n_mp, own, width),
         ),
-        in_specs=[ANY] * 3 + [VMEM] * 4,
-        out_specs=(ANY,) * 9 + (VMEM, ANY),
+        in_specs=[ANY] * 9 + [VMEM] + [ANY] * 2 + [VMEM] * 2,
+        out_specs=(ANY,) * 11 + (VMEM,) + (ANY,) * 5,
         scratch_shapes=[
             pltpu.VMEM(full, BF16),
             pltpu.VMEM((3, width, mine), BF16),
+            pltpu.VMEM((width, mine), BF16),
             *[pltpu.VMEM(part, F32)] * 5,
-            pltpu.VMEM((rows, 1), F32),
+            *[pltpu.VMEM((rows, 1), F32)] * 3,
+            pltpu.VMEM((1, mine // 2), F32),
+            pltpu.VMEM((1, mine), F32),
             *[pltpu.VMEM(lane, F32)] * 4,
             pltpu.VMEM(full, BF16),
             pltpu.VMEM((width, width), BF16),
@@ -828,18 +974,20 @@
             pltpu.VMEM((own, width), F32),
             pltpu.VMEM((8, rows), F32),
             pltpu.VMEM((n_mp, 8, rows), F32),
-            pltpu.SemaphoreType.DMA((6,)),
-            pltpu.SemaphoreType.DMA((12,)),
+            pltpu.SemaphoreType.DMA((17,)),
+            pltpu.SemaphoreType.DMA((17,)),
             pltpu.SemaphoreType.DMA((2, n_mp)),
             pltpu.SemaphoreType.DMA((2, bits, n_mp)),
+            pltpu.SemaphoreType.DMA((2, n_mp)),
+            *RowGather.scratch(n_dp, 7),
             *CubeGather.scratch(n_mp) * 5,
         ],
         compiler_params=pltpu.CompilerParams(collective_id=cid, has_side_effects=True, vmem_limit_bytes=VMEM_LIMIT),
         name="mixer_forward",
-    )(normed, w, tokens, starts, bl, gain, gain_ffn)
-
-
-def ffn_kernel(n_dp, n_mp, final, ffn_in, grad_out, w, *refs):
+    )(*args)
+
+
+def ffn_kernel(n_dp, n_mp, final, ffn_in, grad_out, w, w_d, *refs):
     p = Place(n_dp, n_mp)
     rows, width = ffn_in.shape
     own = rows // n_mp
@@ -847,17 +995,17 @@
         gffn1, down1, middle, r_mid, cot, tok, gain_ffn, w_mix, gsum, mixed, gmid, gain_part, gm, gb, rowdot = refs[:15]
         refs = refs[15:]
     else:
-        gsum, gffn, down = refs[:3]
-        refs = refs[3:]
-    a, wv, bv, bq, lsem, gsem = refs[:6]
-    sums, cube_g = refs[6:11], refs[11:14]
-    cube_d = (cube_g[0], *refs[14:16])
-    refs = refs[16:]
+        w_gate, w_up, w_down, gsum, gffn, down, next_w, next_d = refs[:8]
+        refs = refs[8:]
+    a, wv, wd, bv, bq, lsem, gsem = refs[:7]
+    sums, cube_g = refs[7:12], refs[12:15]
+    cube_d = (cube_g[0], *refs[15:17])
+    refs = refs[17:]
     h = bv.shape[2]
     shard = gsum.shape[1]
     loads = [load(ffn_in, a.at[0], lsem.at[0])]
-    loads += [load(w.at[:, b * h : (b + 1) * h], wv.at[b], lsem.at[1 + b]) for b in range(3)]
-    loads += [load(grad_out, a.at[1], lsem.at[4])]
+    loads += [load(w.at[b], wv.at[b], lsem.at[1 + b]) for b in range(2)]
+    loads += [load(grad_out, a.at[1], lsem.at[3]), load(w_d, wd, lsem.at[4])]
     if final:
         gffn, mid_v, cot_v, tok_v, wmb, gbr, gm_out, gm_in, gb_in, rd_out, rd_in, wsem, ssem, rsem = refs
         late = [load(src, dst, lsem.at[5 + i]) for i, (src, dst) in enumerate(((middle, mid_v), (cot, cot_v), (tok, tok_v), (gffn1, gffn)))]
@@ -871,6 +1019,18 @@
             )
 
     p.barrier()
+    if not final:
+        h_next = next_d.shape[0]
+        srcs = (w_gate.at[:, h:], w_up.at[:, h:], w_down.at[h:])
+
+        def next_dst(u, e, c):
+            at = pl.ds(pl.multiple_of((2 * e + c) * shard, LANE), shard)
+            return next_d.at[:, at] if u == 2 else next_w.at[u, at]
+
+        z = RowGather(p, refs, lambda u: srcs[u], next_dst)
+        own_next = [load(srcs[u], next_dst(u, p.k, p.c), lsem.at[5 + u]) for u in range(3)]
+        for u in range(3):
+            z.start(u)
     for copy in loads:
         copy.wait()
     step = 240
@@ -881,7 +1041,7 @@
         up = dot(a[0, at, :], wv[1])
         sig = sigmoid(gate)
         silu = gate * sig
-        grad = dot(a[1, at, :], wv[2])
+        grad = dot_trans(a[1, at, :], wd[...])
         values = (grad * up * sig * (1.0 + gate * (1.0 - sig)), grad * silu, silu * up)
         for b in range(3):
             bv[b, at, :] = values[b].astype(BF16)
@@ -903,7 +1063,7 @@
 
     def part_d(q, part):
         lo, size = cols[part]
-        return dot_trans(rows_of(2, q), wv[2, lo : lo + size, :])
+        return dot(rows_of(2, q), wd[:, lo : lo + size])
 
     def piece(b, e):
         left = jnp.where(b < 2, 0, 1)
@@ -917,15 +1077,25 @@
     total = RowSum(p, sums, piece, finish, False)
     g_cube, d_cube = CubeSum(p, cube_g, part_g, width), CubeSum(p, cube_d, part_d, width)
     n, chips = total.blocks, p.chips
-    g_cube.stage(0)
-    total.run(0, n)
-    for s in range(1, p.bits):
-        g_cube.stage(s)
     if not final:
+        z.forward(0, 1)
+        total.run(0, n)
+        z.forward(1, 1)
+        g_cube.stage(0)
+        z.forward(2, 1)
+        for i in range(3):
+            total.run(n + i, n + i + 1)
+            z.forward(i, 2)
+        for s in range(1, p.bits):
+            g_cube.stage(s)
         g_cube.drain()
         d_cube.stage(0)
-    total.run(n, 2 * n)
-    if final:
+    else:
+        total.run(0, n)
+        g_cube.stage(0)
+        total.run(n, 2 * n)
+        for s in range(1, p.bits):
+            g_cube.stage(s)
         late[3].wait()
         g_cube.drain()
     for part, (lo, size) in enumerate(cols):
@@ -987,11 +1157,20 @@
         rd_in[p.m] = rd_out[...]
         down_load = load(down1, gffn, lsem.at[9])
         d_cube.stage(0)
-    total.run(2 * n, 3 * n)
     if final:
+        total.run(2 * n, 3 * n)
         for s in range(1, p.bits):
             d_cube.stage(s)
-    total.run(3 * n, total.steps)
+        total.run(3 * n, total.steps)
+    else:
+        for i in range(2 * n, total.steps):
+            total.run(i, i + 1)
+            if i // n + 1 < p.chips:
+                z.forward(i % n, i // n + 1)
+        for u in range(3):
+            z.finish(u)
+            own_next[u].wait()
+            z.drain(u)
     if final:
         for j in range(1, n_mp):
             for kind in range(3):
@@ -1013,16 +1192,17 @@
     total.drain()
 
 
-def ffn_part(n_dp, n_mp, cid, ffn_in, grad_out, w, *rest):
+def ffn_part(n_dp, n_mp, cid, final, ffn_in, grad_out, w, w_d, *rest):
     rows, width = ffn_in.shape
-    h, shard, own = w.shape[1] // 3, width // n_dp, rows // n_mp
+    h = w.shape[2]
+    shard, own = width // n_dp, rows // n_mp
     mine = width // n_mp
-    final = bool(rest)
     f_own = jax.ShapeDtypeStruct((own, width), F32)
     gsum = jax.ShapeDtypeStruct((3, shard, h), F32)
     scratch = [
         pltpu.VMEM((2, rows, width), BF16),
-        pltpu.VMEM((3, width, h), BF16),
+        pltpu.VMEM((2, width, h), BF16),
+        pltpu.VMEM((h, width), BF16),
         pltpu.VMEM((3, rows, h), BF16),
         pltpu.VMEM((3, n_mp, own, h) if own % 16 else (1, 1, 16, LANE), BF16),
         pltpu.SemaphoreType.DMA((13,)),
@@ -1051,19 +1231,26 @@
             pltpu.SemaphoreType.DMA((3, n_mp)),
             pltpu.SemaphoreType.DMA((3, n_mp)),
         ]
-        in_specs = [ANY] * 6 + [VMEM, ANY, ANY, VMEM, ANY]
+        in_specs = [ANY] * 7 + [VMEM, ANY, ANY, VMEM, ANY]
+        out_specs = (ANY, VMEM, VMEM, VMEM, ANY, ANY, ANY)
     else:
-        outs = (gsum, f_own, f_own)
-        in_specs = [ANY] * 3
+        h_next = rest[2].shape[0] - h
+        outs = (
+            gsum, f_own, f_own,
+            jax.ShapeDtypeStruct((2, width, h_next), BF16), jax.ShapeDtypeStruct((h_next, width), BF16),
+        )
+        scratch += RowGather.scratch(n_dp, 3)
+        in_specs = [ANY] * 7
+        out_specs = (ANY, VMEM, VMEM, ANY, ANY)
     return pl.pallas_call(
         functools.partial(ffn_kernel, n_dp, n_mp, final),
         out_shape=outs,
         in_specs=in_specs,
-        out_specs=(ANY, VMEM, VMEM, VMEM, ANY, ANY, ANY)[: len(outs)],
+        out_specs=out_specs,
         scratch_shapes=scratch,
         compiler_params=pltpu.CompilerParams(collective_id=cid, has_side_effects=True, vmem_limit_bytes=VMEM_LIMIT),
         name="ffn_last" if final else "ffn_first",
-    )(ffn_in, grad_out, w, *rest)
+    )(ffn_in, grad_out, w, w_d, *rest)
 
 
 def project_kernel(
@@ -1079,7 +1266,7 @@
     loads = [load(normed, a.at[0], lsem.at[0])]
     loads += [load(src, bv.at[i], lsem.at[1 + i]) for i, src in enumerate((g_in, g_f, g_g, g_b))]
     loads += [load(mixed, a.at[1], lsem.at[5])]
-    late = [load(w.at[:, i * mine : (i + 1) * mine], wv.at[i], lsem.at[6 + i]) for i in range(3)]
+    late = [load(w.at[i], wv.at[i], lsem.at[6 + i]) for i in range(3)]
     if own % 16:
         late.append(load(g_split, bq, lsem.at[9]))
     p.barrier(far=True)
@@ -1193,6 +1380,89 @@
     )(normed, mixed, g_in, g_f, g_g, g_b, g_split, w, gmid, tok, r_in, gain_in, *vectors)
 
 
+def result_kernel(
+    n_mp, gmix, one, two, mixed, gtok, small,
+    o_mixed, o_tok, o_gin, o_win, o_wf, o_wo, o_bound, o_gmix, o_wm, o_gffn, o_gate, o_up, o_down,
+    gm, gw, gffn, down, mixed_v, tok_v, sem, osem,
+):
+    d = lax.axis_index("dp")
+    shard, mine = gmix.shape[2:]
+    ch, half = mine // 2, n_mp * mine // 2
+    h, h2 = one.shape[2], two.shape[2]
+    mixer = [load(gmix.at[b], gm.at[b], sem.at[b]) for b in range(4)]
+    through = [load(mixed, mixed_v, sem.at[4]), load(gtok, tok_v, sem.at[5])]
+    ffn = [
+        (load(one.at[i], gffn.at[i, :, :h], sem.at[6 + 2 * i]), load(two.at[i], gffn.at[i, :, h:], sem.at[7 + 2 * i]))
+        for i in range(3)
+    ]
+    outs = []
+    for b, out in enumerate((o_win, o_wf, o_wo, o_wm)):
+        mixer[b].wait()
+        for q in range(n_mp):
+            value = gm[b, q].astype(F32)
+            if b < 3:
+                gw[b, :, q * ch : (q + 1) * ch] = value[:, :ch]
+                gw[b, :, half + q * ch : half + (q + 1) * ch] = value[:, ch:]
+            else:
+                gw[b, :, q * mine : (q + 1) * mine] = value
+        outs.append(load(gw.at[b], out, osem.at[b]))
+    for i, (copy, src, out) in enumerate(zip(through, (mixed_v, tok_v), (o_mixed, o_tok))):
+        copy.wait()
+        outs.append(load(src, out, osem.at[4 + i]))
+    for i, out in enumerate((o_gate, o_up)):
+        for copy in ffn[i]:
+            copy.wait()
+        outs.append(load(gffn.at[i], out, osem.at[6 + i]))
+    at = pl.ds(pl.multiple_of(d * shard, LANE), shard)
+    for row, out in enumerate((o_gin, o_gffn, o_gmix)):
+        out[...] = small[row : row + 1, at]
+    size = shard // 2
+    if size % LANE == 0:
+        o_bound[...] = small[3:4, pl.ds(pl.multiple_of(d * size, LANE), size)]
+    else:
+        pair = small[3:4, pl.ds(pl.multiple_of(lax.div(d, 2) * 2 * size, LANE), 2 * size)]
+        o_bound[...] = jnp.where(lax.rem(d, 2) == 0, pair[:, :size], pair[:, size:])
+    for copy in ffn[2]:
+        copy.wait()
+    for lo in range(0, h + h2, LANE):
+        down[lo : lo + LANE, :] = gffn[2, :, lo : lo + LANE].T
+    outs.append(load(down, o_down, osem.at[8]))
+    for copy in outs:
+        copy.wait()
+
+
+def results(n_dp, n_mp, gmix, one, two, mixed, gtok, small):
+    shard, mine = gmix.shape[2:]
+    width, ffn = n_mp * mine, one.shape[2] + two.shape[2]
+    own = mixed.shape[0]
+
+    def f32(*shape):
+        return jax.ShapeDtypeStruct(shape, F32)
+
+    row = f32(1, shard)
+    return pl.pallas_call(
+        functools.partial(result_kernel, n_mp),
+        out_shape=(
+            jax.ShapeDtypeStruct((own, width), BF16), f32(own, width), row, *(f32(shard, width),) * 3, f32(1, shard // 2), row,
+            f32(shard, width), row, f32(shard, ffn), f32(shard, ffn), f32(ffn, shard),
+        ),
+        in_specs=[ANY] * 5 + [VMEM],
+        out_specs=(ANY, ANY, VMEM, ANY, ANY, ANY, VMEM, VMEM, ANY, VMEM, ANY, ANY, ANY),
+        scratch_shapes=[
+            pltpu.VMEM((4, n_mp, shard, mine), BF16),
+            pltpu.VMEM((4, shard, width), F32),
+            pltpu.VMEM((3, shard, ffn), F32),
+            pltpu.VMEM((ffn, shard), F32),
+            pltpu.VMEM((own, width), BF16),
+            pltpu.VMEM((own, width), F32),
+            pltpu.SemaphoreType.DMA((12,)),
+            pltpu.SemaphoreType.DMA((9,)),
+        ],
+        compiler_params=pltpu.CompilerParams(vmem_limit_bytes=VMEM_LIMIT),
+        name="results",
+    )(gmix, one, two, mixed, gtok, small)
+
+
 def per_device(n_dp, n_mp, tokens, segment_ids, cotangent, gain_in, w_in, w_forget, w_outgate, bound_logit, gain_mix,
                w_mix, gain_ffn, w_gate, w_up, w_down):
     m, d = lax.axis_index("mp"), lax.axis_index("dp")
@@ -1204,53 +1474,29 @@
     ffn = w_gate.shape[1]
     padded = -(-ffn // LANE) * LANE
     cut = -(-padded // 2 // LANE) * LANE
-    parts = ((0, cut), (cut, padded - cut))
-
-    def cols(x, at, size):
-        return lax.dynamic_slice_in_dim(x, at, size, 1)
-
-    def own_channels(x):
-        return jnp.concatenate([cols(x, m * ch, ch), cols(x, half + m * ch, ch)], axis=1)
+    if padded != ffn:
+        fill = ((0, 0), (0, padded - ffn))
+        w_gate, w_up, w_down = jnp.pad(w_gate, fill), jnp.pad(w_up, fill), jnp.pad(w_down, fill[::-1])
 
     def own_rows(x):
         return lax.dynamic_slice_in_dim(x, m * own, own, 0)
 
-    def gather_dp(x):
-        return lax.all_gather(x, "dp", axis=0, tiled=True)
-
-    w_cat = gather_dp(
-        jnp.concatenate(
-            [own_channels(w_in), own_channels(w_forget), own_channels(w_outgate), cols(w_mix, m * mine, mine)], axis=1
-        )
+    normed, r_in, pin, pf, pg, st, phasor, r_mix, mixer_out, ffn_in, middle, r_mid, wm, w_cat, w_one, d_one, grad_out = mixer_forward(
+        n_dp, n_mp, 2, cut, w_in, w_forget, w_outgate, w_mix, w_gate, w_up, w_down, cotangent, tokens, segment_ids,
+        bound_logit[None], gain_mix[None], gain_in[None], gain_ffn[None],
     )
-    fill = ((0, 0), (0, padded - ffn))
-    gate_p, up_p, down_p = jnp.pad(w_gate, fill), jnp.pad(w_up, fill), jnp.pad(w_down.T, fill)
-    w_ffn = []
-    for lo, size in parts:
-        at = slice(lo, lo + size)
-        piece = jnp.concatenate([gate_p[:, at], up_p[:, at], down_p[:, at]], axis=1)
-        w_ffn.append(gather_dp(piece))
-
-    grad_out = gather_mp(n_dp, n_mp, 1, cotangent).reshape(rows, width)
-
-    stream = tokens.astype(F32)
-    ident = segment_ids[0]
-    previous = jnp.concatenate([ident[:1] - 1, ident[:-1]])
-    starts = jnp.where(ident != previous, 1.0, 0.0).astype(F32)[:, None]
-    r_in = lax.rsqrt(jnp.mean(stream * stream, axis=-1, keepdims=True) + EPS)
-    normed = (stream * r_in * gain_in).astype(BF16)
-    bl = lax.dynamic_slice_in_dim(bound_logit, m * ch, ch, 0)[None]
-    gain = own_channels(gain_mix[None])
-    pin, pf, pg, st, phasor, r_mix, mixer_out, ffn_in, middle, r_mid, wm = mixer_forward(
-        n_dp, n_mp, 2, normed, w_cat, tokens, starts, bl, gain, gain_ffn[None]
+    grad_out = grad_out.reshape(rows, width)
+
+    g_one, gffn, down, w_two, d_two = ffn_part(
+        n_dp, n_mp, 3, False, ffn_in, grad_out, w_one, d_one, w_gate, w_up, w_down
     )
-
-    g_one, gffn, down = ffn_part(n_dp, n_mp, 3, ffn_in, grad_out, w_ffn[0])
     tok_own = own_rows(tokens)
     g_two, mixed, gmid, gain_ffn_part, gm, gb, rowdot = ffn_part(
-        n_dp, n_mp, 4, ffn_in, grad_out, w_ffn[1], gffn, down, middle, r_mid, cotangent, tok_own, gain_ffn[None], wm
+        n_dp, n_mp, 4, True, ffn_in, grad_out, w_two, d_two, gffn, down, middle, r_mid, cotangent, tok_own, gain_ffn[None], wm
     )
 
+    bl = lax.dynamic_slice_in_dim(bound_logit, m * ch, ch, 0)[None]
+    gain = jnp.concatenate([lax.dynamic_slice_in_dim(gain_mix, at + m * ch, ch, 0) for at in (0, half)])[None]
     lanes = ch // LANE
     scratch = [pltpu.VMEM((lanes, rows, LANE), F32)] * 4
     gin, gf, gg, dgain, dbound = call_local(
@@ -1271,30 +1517,11 @@
         gain_in[None], gain_ffn_part, dgain, dbound,
     )
 
-    def part_of(row, size):
-        return lax.dynamic_slice_in_dim(small[row], d * (size // n_dp), size // n_dp, 0)
-
-    g_mixer = g_mixer.astype(F32)
-
-    def by_channel(g):
-        return jnp.concatenate([g[q, :, lo : lo + ch] for lo in (0, ch) for q in range(n_mp)], axis=1)
-
-    g_ffn = jnp.concatenate([g_one, g_two], axis=2)[:, :, :ffn]
-    return (
-        mixed,
-        grad_tokens,
-        part_of(0, width),
-        by_channel(g_mixer[0]),
-        by_channel(g_mixer[1]),
-        by_channel(g_mixer[2]),
-        part_of(3, half),
-        part_of(2, width),
-        jnp.concatenate([g_mixer[3, q] for q in range(n_mp)], axis=1),
-        part_of(1, width),
-        g_ffn[0],
-        g_ffn[1],
-        g_ffn[2].T,
-    )
+    out = results(n_dp, n_mp, g_mixer, g_one, g_two, mixed, grad_tokens, small)
+    out = [v[0] if v.shape[0] == 1 else v for v in out]
+    if padded != ffn:
+        out[10:] = [out[10][:, :ffn], out[11][:, :ffn], out[12][:ffn]]
+    return tuple(out)
 
 
 def solution(mesh):

time: 639 us -> 558 us (0.87)
  local copies, waits for them, and re-layouts: 46 us -> 12.1 us
  other arithmetic: 16.5 us -> 0.01 us
  waiting for transfers between devices: 16.1 us -> 0 us
  between operations: 15.2 us -> 1.17 us
    pallas_call x2, Pallas kernels: 279 us -> 248 us  [ffn_part(): pl.pallas_call(functools.partial(ffn_kernel, n_dp, n_mp, final), out_shap...]
    pallas_call x2, Pallas kernels: 135 us -> 162 us  [the longest x1 150 us: mixer_forward(): pl.pallas_call(functools.partial(mixer_kernel, n_dp, n_mp), out_shape=(bf...]
    unnamed x88 -> x16, local copies, waits for them, and re-layouts: 25.8 us -> 6.2 us
    all_gather x3 -> x0, waiting for transfers between devices: 16 us -> none  [gather_dp(): return lax.all_gather(x, 'dp', axis=0, tiled=True)]
    convert_element_type x2 -> x0, other arithmetic: 8.44 us -> none  [the longest x1 5.11 us: per_device(): normed = (stream * r_in * gain_in).astype(BF16)]
  transfers between devices with their start and end apart: 3 -> 0, of which waited for: 2 -> 0; matrix products, arithmetic and copies ran while one was open for 3% -> 0% of each run, Pallas kernels for 47% -> 0%
where the time goes in v3:
time: 558 us; the launch traced here: 550 us
  Pallas kernels  536 us (96%)
  local copies, waits for them, and re-layouts  12.1 us (2%)
    pallas_call x2, Pallas kernels, ffn_part(): pl.pallas_call(functools.partial(ffn_kernel, n_dp, n_mp, final), out_shap...  248 us
    pallas_call x1, Pallas kernels, mixer_forward(): pl.pallas_call(functools.partial(mixer_kernel, n_dp, n_mp), out_shape=(bf...  150 us
    pallas_call x1, Pallas kernels, project_back(): pl.pallas_call(functools.partial(project_kernel, n_dp, n_mp), out_shape=(...  116 us
    pallas_call x1, Pallas kernels, results(): pl.pallas_call(functools.partial(result_kernel, n_mp), out_shape=(jax.Sha...  12 us

profile of v3, /device:TPU:8, one launch (start us, length us, event | category | flops | bytes accessed | tf_op | source)
XLA Modules:
  0.0 549.7 jit_solution(2006911970273571247)
XLA Ops:
  0.6 149.9 %mixer_forward.1 = (bf16[960,2048]{1,0:T(8,128)(2,1)}, f32[960,1]{1,0:T(8,128)}, f32[960,512]{1,0:T(8,128)}, f32[960,512]{1,0:T(8,128)}, f32[960,512]{1,0:T(8,12...) custom-call(bf16[256,2048]{1,0:T(8,128)(2,1)} %w_in.1, ...), custom_call_target="tpu_custom_call" | custom-call | tf_op jit(solution)/shard_map/mixer_forward/pallas_call | solution.py:953
  150.5 124.7 %ffn_first.1 = (f32[3,256,768]{2,1,0:T(8,128)}, f32[240,2048]{1,0:T(8,128)}, f32[240,2048]{1,0:T(8,128)}, bf16[2,2048,640]{2,1,0:T(8,128)(2,1)}, bf16[640,2048]{1,0:T(8,128)(2,1)}) custom-call(bf16[960,2048]{1,0:T(8,128)(2,1)} %get-tuple-element.65.ffn_in, bf16[960,2048]{1,0:T(8,128)(2,1)} %bitcast.19, bf16[2,2048,768]{2,1,0:T(8,128)(2,1)} %get-tuple-element.67.w, ...), custom_call_target="tpu_custom_call" | custom-call | tf_op jit(solution)/shard_map/ffn_first/pallas_call | solution.py:1245
  275.2 2.3 constant_dynamic-slice_fusion.1.refs_5_.tok
  277.5 0.0 copy-start.4
  277.5 123.0 %ffn_last.1 = (f32[3,256,640]{2,1,0:T(8,128)}, bf16[240,2048]{1,0:T(8,128)(2,1)}, f32[240,2048]{1,0:T(8,128)}, f32[1,2048]{1,0:T(1,128)}, bf16[4,240,512]{2,1,0:...) custom-call(bf16[960,2048]{1,0:T(8,128)(2,1)} %get-tuple-element.65.ffn_in, ...), custom_call_target="tpu_custom_call" | custom-call | tf_op jit(solution)/shard_map/ffn_last/pallas_call | solution.py:1245
  400.5 0.8 fusion
  401.3 0.8 dynamic_slice.16
  402.1 0.0 copy-done.4
  402.1 0.0 copy-start
  402.1 1.2 copy-done
  403.3 0.0 copy-start.5
  403.3 1.0 copy-done.5
  404.3 10.4 %scan_backward.1 = (bf16[960,512]{1,0:T(8,128)(2,1)S(1)}, bf16[960,512]{1,0:T(8,128)(2,1)S(1)}, bf16[960,512]{1,0:T(8,128)(2,1)S(1)}, f32[1,512]{1,0:T(1,128)S(1)}, f32[1,256]{1,0:T(1,128)S(1)}) custom-call(bf16[960,512]{1,0:T(8,128)(2,1)S(1)} %bitcast.15, f32[960,512]{1,0:T(8,128)} %get-tuple-element.77.pin, f32[960,512]{1,0:T(8,128)} %get-tuple-element.78.pf, ...), custom_call_target="tpu_custom_call" | custom-call | tf_op jit(solution)/shard_map/scan_backward/pallas_call | solution.py:218
  414.7 0.0 copy-start.1
  414.7 0.9 copy-done.1
  415.6 0.0 copy-start.2
  415.6 0.9 copy-done.2
  416.6 0.0 copy-start.3
  416.6 0.9 copy-done.3
  417.5 0.0 copy-start.6
  417.5 0.6 copy-done.6
  418.1 0.0 copy-start.7
  418.1 0.6 copy-done.7
  418.6 1.6 constant_dynamic-slice_fusion.r_in
  420.2 0.6 broadcast_in_dim.29.g_split
  420.8 116.4 %project_back.1 = (bf16[4,4,256,512]{3,2,1,0:T(8,128)(2,1)}, f32[240,2048]{1,0:T(8,128)}, f32[4,2048]{1,0:T(4,128)}) custom-call(bf16[960,2048]{1,0:T(8,128)(2,1)} %get-tuple-element.63.normed, bf16[960,2048]{1,0:T(8,128)(2,1)} %get-tuple-element.64.mixed, bf16[960,512]{1,0:T(8,128)(2,1)} %copy-done.1, bf16[960,512]{1,0:T(8,128)(2,1)} %copy-done.2, ...), custom_call_target="tpu_custom_call" | custom-call | tf_op jit(solution)/shard_map/project_back/pallas_call | solution.py:1356
  537.2 12.0 %results.1 = (bf16[240,2048]{1,0:T(8,128)(2,1)}, f32[240,2048]{1,0:T(8,128)}, f32[1,256]{1,0:T(1,128)}, f32[256,2048]{1,0:T(8,128)}, f32[256,2048]{1,0:T(8,128)}...) custom-call(bf16[4,4,256,512]{3,2,1,0:T(8,128)(2,1)} %get-tuple-elem, ...), custom_call_target="tpu_custom_call" | custom-call | tf_op jit(solution)/shard_map/results/pallas_call | solution.py:1443
  (1 shorter events, 0.0 us)
Async XLA Ops:
  277.5 124.6 %copy-start.4 = (f32[960,1]{1,0:T(8,128)S(1)}, f32[960,1]{1,0:T(8,128)}, u32[]{:S(2)}) copy-start(f32[960,1]{1,0:T(8,128)} %get-tuple-element.82.r) | copy-start | bytes 11524
  402.1 1.2 copy-start
  403.3 1.0 copy-start.5
  414.7 0.9 copy-start.1
  415.6 0.9 copy-start.2
  416.6 0.9 copy-start.3
  417.5 0.6 copy-start.6
  418.1 0.6 copy-start.7

commit v4 on v3

--- a/solution.py
+++ b/solution.py
@@ -110,7 +110,7 @@
 
 
 def scan_backward(
-    gm, pin, pf, pg, st, phasor, r, rowdot, bl, gain, gin, gf, gg, dgain, dbound, a_re, a_im, b_re, b_im
+    gm, pin, pf, pg, st, phasor, r, rowdot, bl, gain, gin, gf, gg, dgain, dbound, a_re, a_im, b_re, b_im, between=(),
 ):
     rows, half = pin.shape[0], pin.shape[1] // 2
     width = 2 * half
@@ -121,7 +121,7 @@
 
     def prepare(i, total):
         at = pl.ds(pl.multiple_of(i * step, 16), step)
-        g, gate = gm[at, :], pg[at, :]
+        g, gate = gm[at, :].astype(F32), pg[at, :]
         sig = sigmoid(gate)
         silu = gate * sig
         n = st[at, :] * r[at, :]
@@ -140,6 +140,8 @@
 
     total = lax.fori_loop(0, rows // step, prepare, jnp.zeros((8, width), F32))
     dgain[...] = jnp.sum(total, axis=0, keepdims=True)
+    for task in between[:1]:
+        task()
     zero, one = jnp.zeros((CHUNKS, LANE), F32), jnp.ones((CHUNKS, LANE), F32)
 
     def local(i, carry):
@@ -159,6 +161,8 @@
         return tuple(out)
 
     last = lax.fori_loop(0, span, local, (one, zero, zero, zero) * lanes, unroll=2)
+    for task in between[1:]:
+        task()
     carries = []
     for j in range(lanes):
         p_re, p_im, s_re, s_im = last[4 * j : 4 * j + 4]
@@ -321,16 +325,19 @@
         self.piece, self.finish = piece, finish
         self.blocks, self.skew = self.summed.shape[0], skew
         chips = place.chips
-        self.steps = (self.blocks + chips - 1) * chips if skew else self.blocks * chips
+        self.steps = chips - 1 + (self.blocks + chips - 2) * chips if skew else self.blocks * chips
 
     def order(self, i):
         chips = self.p.chips
         ok = (i >= 0) & (i < self.steps)
         i = jnp.clip(i, 0, self.steps - 1)
         if self.skew:
-            t = lax.rem(i, chips)
-            b = lax.div(i, chips) - t
-            return t, jnp.clip(b, 0, self.blocks - 1), (b >= 0) & (b < self.blocks) & ok
+            early = i < chips - 1
+            j = jnp.maximum(i - (chips - 1), 0)
+            t = jnp.where(early, i, lax.rem(j, chips))
+            b = jnp.where(early, 0, 1 + lax.div(j, chips) - t)
+            ok = ok & (early | ((b >= 0) & (b < self.blocks) & ((b > 0) | (t == chips - 1))))
+            return t, jnp.clip(b, 0, self.blocks - 1), ok
         return lax.div(i, self.blocks), lax.rem(i, self.blocks), ok
 
     def targets(self, i):
@@ -419,12 +426,19 @@
 
             self.send(b, down, False)
 
-    def run(self, lo, hi):
-        if lo == 0:
-            self.give(0)
+    def run(self, lo, hi, fresh=False, ahead=True):
+        if lo == 0 or fresh:
+            self.give(lo)
 
         def body(i, _):
-            self.give(i + 1)
+            if ahead:
+                self.give(i + 1)
+            else:
+
+                @pl.when(i + 1 < hi)
+                def _():
+                    self.give(i + 1)
+
             self.work(i)
             return 0
 
@@ -453,13 +467,13 @@
 
 class CubeSum:
     @staticmethod
-    def scratch(n_mp, rows, width):
+    def scratch(n_mp, rows, width, whole=True):
         bits = n_mp.bit_length() - 1
         most = max(size for _, size in bounds(width, bits, LANE))
+        slots = n_mp - 1 if whole else n_mp - 2
         return [
-            pltpu.VMEM((bits, n_mp - 1, rows, most), BF16),
-            pltpu.VMEM((bits, n_mp - 1, rows, most), BF16),
-            pltpu.SemaphoreType.DMA((2, bits, n_mp - 1)),
+            *[pltpu.VMEM((bits, slots, rows, most), BF16)] * 2,
+            pltpu.SemaphoreType.DMA((2, bits, slots)),
         ]
 
     def __init__(self, place, refs, partial, width):
@@ -486,29 +500,43 @@
             self.p.peer(self.masks[part, s][0]),
         )
 
-    def arrived(self, part, s, sub):
-        self.copy(part, s, sub).wait_recv()
-        return self.inbox[part, self.slots[part, s, sub], :, : self.cols[part][1]].astype(F32)
-
-    def stage(self, s):
+    def pieces(self, part, mask, stages):
+        for r in stages:
+            self.copy(part, r, mask).wait_recv()
+        base, total = self.cols[part]
+        for lo in range(0, total, 4 * LANE):
+            size = min(4 * LANE, total - lo)
+            value = self.partial(self.p.m ^ mask, base + lo, size)
+            for r in stages:
+                value = value + self.inbox[part, self.slots[part, r, mask], :, lo : lo + size].astype(F32)
+            yield lo, size, value
+
+    def stage(self, s, only=None):
         for part in range(self.p.bits):
             bit, subs = self.masks[part, s]
             for sub in subs:
-                value = self.partial(self.p.m ^ (bit | sub), part)
-                for r in range(s):
-                    value = value + self.arrived(part, r, bit | sub)
-                self.out[part, self.slots[part, s, sub], :, : self.cols[part][1]] = value.astype(BF16)
+                if only not in (None, bit | sub):
+                    continue
+                for lo, size, value in self.pieces(part, bit | sub, range(s)):
+                    self.out[part, self.slots[part, s, sub], :, lo : lo + size] = value.astype(BF16)
                 self.copy(part, s, sub).start()
 
-    def result(self, part):
-        value = self.partial(self.p.m, part)
-        for s in range(self.p.bits):
-            value = value + self.arrived(part, s, 0)
-        return value
-
-    def drain(self):
+    def results(self, stages=None):
+        for part in range(self.p.bits):
+            base = self.cols[part][0]
+            for lo, size, value in self.pieces(part, 0, range(self.p.bits if stages is None else stages)):
+                yield slice(base + lo, base + lo + size), value
+
+    def parting(self):
+        s = self.p.bits - 1
+        for part in range(self.p.bits):
+            for lo, size, value in self.pieces(part, self.masks[part, s][0], range(s)):
+                yield part, slice(lo, lo + size), value
+
+    def drain(self, stages=None):
         for part, s, sub in self.slots:
-            self.copy(part, s, sub).wait_send()
+            if stages is None or s < stages:
+                self.copy(part, s, sub).wait_send()
 
 
 class CubeGather:
@@ -688,8 +716,8 @@
 def mixer_kernel(
     n_dp, n_mp, w_in, w_forget, w_outgate, w_mix, w_gate, w_up, w_down, cot, tokens, ident, bound, gain_mix, gain_in, gain_ffn,
     normed_o, rin_o, pin_o, pf_o, pg_o, st_o, phasor_o, r_o, mix_o, ffn_o, mid_o, rmid_o, wm_o, wcat_o, one_o, one_d, cot_o,
-    x, wv, wq, pin, pf, pg, st, phasor, rowsq, rin, starts, bl, gain, a_re, a_im, b_re, b_im, mix, wm, tok, ffn_v, mid_v, rs_out, rs_in,
-    lsem, osem, rs_sem, wtwin, csem, *gsems,
+    x, wv, wq, pin, pf, pg, st, phasor, rowsq, rin, starts, bl, gain, a_re, a_im, b_re, b_im, mix, wm, tok, ffn_v, mid_v, cot_v, rs_out, rs_in,
+    lsem, osem, rs_sem, wtwin, *gsems,
 ):
     p = Place(n_dp, n_mp)
     rows, width = tokens.shape
@@ -736,21 +764,28 @@
         ],
     ]
     first_own = [load(unit_src(u), unit_dst(u, p.k, p.c), lsem.at[9 + u]) for u in range(4, 7)]
-    cot_own = load(cot, cot_o.at[p.m], lsem.at[8])
+    cot_own = load(cot, cot_v.at[p.m], lsem.at[8])
     p.barrier()
     z = RowGather(p, gsems[:1], unit_src, unit_dst)
     gsems = gsems[1:]
     order = (3, 0, 1, 2)
-    for u in order:
+
+    def start(u):
         for copy in keep[u]:
             copy.wait()
         z.start(u)
 
-    def cot_copy(mask, owner):
-        return remote(cot, cot_o.at[owner], csem.at[0, mask], csem.at[1, owner], p.peer(mask))
-
-    for mask in range(1, n_mp):
-        cot_copy(mask, p.m).start()
+    start(3)
+    start(0)
+    cot_parts = bounds(width, p.bits, LANE)
+
+    def cot_view(q, part):
+        lo, size = cot_parts[part]
+        return cot_v.at[q, :, lo : lo + size]
+
+    cot_own.wait()
+    gc = CubeGather(p, gsems[10:12], cot_view)
+    gc.stage(0)
     tok_load.wait()
     fine = 48
 
@@ -772,19 +807,7 @@
     starts[...] = jnp.where(jnp.abs(ids - before) > 0.5, 1.0, 0.0)
     for copy in vectors:
         copy.wait()
-    outs = [load(x, normed_o, osem.at[0]), load(rin, rin_o, osem.at[1])]
-    for s in range(1, p.chips - 1):
-        for u in order:
-            z.forward(u, s)
-    for u in range(4, 7):
-        z.start(u)
-    z.forward(3, p.chips - 1)
-    z.finish(3)
-    own_mix = load(
-        wq.at[pl.ds(pl.multiple_of(p.c * hw, 16), hw)],
-        wm.at[pl.ds(pl.multiple_of(p.c * hw, 16), hw), pl.ds(pl.multiple_of(p.m * mine, LANE), mine)],
-        lsem.at[9],
-    )
+    outs = [load(x, normed_o, osem.at[0]), load(rin.at[pl.ds(pl.multiple_of(p.m * own, 8), own)], rin_o, osem.at[1])]
     gw = CubeGather(p, gsems[0:2], mix_view)
 
     def to_twin(part, sub):
@@ -799,10 +822,6 @@
         ]
         return remote(ref, ref, wtwin.at[0, part, sub], wtwin.at[1, part, sub], p.twin())
 
-    own_mix.wait()
-    gw.stage(0)
-    for part in range(p.bits):
-        to_twin(part, 0).start()
     step = 240
 
     def project(u, out):
@@ -816,16 +835,35 @@
 
         lax.fori_loop(0, rows // step, body, 0)
 
-    project(0, pin)
+    core_rows = pl.ds(pl.multiple_of(p.c * hw, 16), hw)
+    for tau in range(1, p.chips + 2):
+        for i, u in enumerate(order):
+            if 1 <= tau - i <= p.chips - 2:
+                z.forward(u, tau - i)
+        if tau + 1 < len(order):
+            start(order[tau + 1])
+        if tau == p.chips - 1:
+            for s in range(1, p.bits):
+                gc.stage(s)
+            z.forward(3, p.chips - 1)
+            z.finish(3)
+            own_mix = load(wq.at[core_rows], wm.at[core_rows, lanes_at(p.m * mine, mine)], lsem.at[9])
+            own_mix.wait()
+            gw.stage(0)
+            for part in range(p.bits):
+                to_twin(part, 0).start()
+        if tau == p.chips:
+            project(0, pin)
+    for u in range(4, 7):
+        z.start(u)
     project(1, pf)
-    project(2, pg)
-    outs += [load(wv.at[u], wcat_o.at[u], osem.at[2 + u]) for u in range(3)]
     for s in range(1, p.bits):
         gw.stage(s)
     scan_forward(pin, pf, starts, bl, st, phasor, rowsq, a_re, a_im, b_re, b_im)
     outs += [
         load(src, dst, osem.at[5 + i])
         for i, (src, dst) in enumerate(((pin, pin_o), (pf, pf_o), (pg, pg_o), (st, st_o), (phasor, phasor_o)))
+        if i != 2
     ]
     ones = jnp.ones((8, mine), F32)
     rs_out[...] = lax.dot_general(
@@ -837,6 +875,9 @@
 
     for mask in range(1, n_mp):
         rs_copy(mask).start()
+    project(2, pg)
+    outs += [load(wv.at[u], wcat_o.at[u], osem.at[2 + u]) for u in range(3)]
+    outs.append(load(pg, pg_o, osem.at[7]))
     gw.last()
     for part in range(p.bits):
         for sub in range(1, n_mp):
@@ -881,6 +922,8 @@
         for g in gathers:
             g.stage(s)
     z.forward(6, 1)
+    gc.last()
+    outs.append(load(cot_v, cot_o, osem.at[17]))
     for part in range(p.bits):
         for sub in range(n_mp):
             from_twin(part, sub).wait_recv()
@@ -917,9 +960,6 @@
             z.forward(u, s)
     for u in range(4, 7):
         z.finish(u)
-    for mask in range(1, n_mp):
-        cot_copy(mask, p.m ^ mask).wait_recv()
-    cot_own.wait()
     for copy in first_own:
         copy.wait()
     for copy in outs:
@@ -927,6 +967,7 @@
     for u in range(7):
         z.drain(u)
     gw.drain()
+    gc.drain()
     for g in gathers:
         g.drain()
     for part in range(p.bits):
@@ -934,7 +975,6 @@
             to_twin(part, sub).wait_send()
     for mask in range(1, n_mp):
         rs_copy(mask).wait_send()
-        cot_copy(mask, p.m).wait_send()
 
 
 def mixer_forward(n_dp, n_mp, cid, h, *args):
@@ -953,7 +993,7 @@
     return pl.pallas_call(
         functools.partial(mixer_kernel, n_dp, n_mp),
         out_shape=(
-            bf16(*full), f32(rows, 1), *(f32(*part),) * 5, f32(rows, 1), bf16(*full), bf16(*full), f32(own, width), f32(own, 1),
+            bf16(*full), f32(own, 1), *(f32(*part),) * 5, f32(rows, 1), bf16(*full), bf16(*full), f32(own, width), f32(own, 1),
             bf16(width, width), bf16(3, width, mine), bf16(2, width, h), bf16(h, width), bf16(n_mp, own, width),
         ),
         in_specs=[ANY] * 9 + [VMEM] + [ANY] * 2 + [VMEM] * 2,
@@ -972,252 +1012,360 @@
             pltpu.VMEM(full, BF16),
             pltpu.VMEM(full, BF16),
             pltpu.VMEM((own, width), F32),
+            pltpu.VMEM((n_mp, own, width), BF16),
             pltpu.VMEM((8, rows), F32),
             pltpu.VMEM((n_mp, 8, rows), F32),
             pltpu.SemaphoreType.DMA((17,)),
-            pltpu.SemaphoreType.DMA((17,)),
+            pltpu.SemaphoreType.DMA((18,)),
             pltpu.SemaphoreType.DMA((2, n_mp)),
             pltpu.SemaphoreType.DMA((2, bits, n_mp)),
-            pltpu.SemaphoreType.DMA((2, n_mp)),
             *RowGather.scratch(n_dp, 7),
-            *CubeGather.scratch(n_mp) * 5,
+            *CubeGather.scratch(n_mp) * 6,
         ],
         compiler_params=pltpu.CompilerParams(collective_id=cid, has_side_effects=True, vmem_limit_bytes=VMEM_LIMIT),
         name="mixer_forward",
     )(*args)
 
 
-def ffn_kernel(n_dp, n_mp, final, ffn_in, grad_out, w, w_d, *refs):
+STEP = 240
+
+
+def ffn_rows(at, own, a, w_gate, w_up, w_down, put):
+    gate = dot(a[0, at, :], w_gate)
+    up = dot(a[0, at, :], w_up)
+    sig = sigmoid(gate)
+    silu = gate * sig
+    grad = dot_trans(a[1, at, :], w_down)
+    put(0, (grad * up * sig * (1.0 + gate * (1.0 - sig))).astype(BF16))
+    put(1, (grad * silu).astype(BF16))
+    put(2, (silu * up).astype(BF16))
+
+
+class FfnSums:
+    def __init__(self, p, a, wv, wd, h, bv, bq, gsum, gsem, sums, cube_g, cube_d):
+        rows, width = a.shape[1:]
+        own, shard = rows // p.n_mp, gsum.shape[1]
+        def rows_of(b, q):
+            return bq[b, q] if own % 16 else bv[b, pl.ds(pl.multiple_of(q * own, 16), own), :]
+
+        def part_g(q, lo, size):
+            at = slice(lo, lo + size)
+            return dot_trans(rows_of(0, q), wv[0, at, :h]) + dot_trans(rows_of(1, q), wv[1, at, :h])
+
+        def part_d(q, lo, size):
+            return dot(rows_of(2, q), wd[:h, lo : lo + size])
+
+        def piece(b, e):
+            left = jnp.where(b < 2, 0, 1)
+            return dot_rows(a[left, :, pl.ds(pl.multiple_of(e * shard, LANE), shard)], bv[b])
+
+        def finish(b, acc):
+            out = pltpu.make_async_copy(acc, gsum.at[b], gsem)
+            out.start()
+            out.wait()
+
+        self.total = RowSum(p, sums, piece, finish, False)
+        self.g_cube, self.d_cube = CubeSum(p, cube_g, part_g, width), CubeSum(p, cube_d, part_d, width)
+
+
+def first_kernel(
+    n_dp, n_mp, ffn_in, grad_out, w, w_d, w_gate, w_up, w_down, gsum, gffn, down, next_w, next_d, next_b, next_q,
+    a, wv, wd, wv2, wd2, bv, bq, stage, stage_q, result, lsem, gsem, bsem, *refs,
+):
     p = Place(n_dp, n_mp)
     rows, width = ffn_in.shape
-    own = rows // n_mp
-    if final:
-        gffn1, down1, middle, r_mid, cot, tok, gain_ffn, w_mix, gsum, mixed, gmid, gain_part, gm, gb, rowdot = refs[:15]
-        refs = refs[15:]
-    else:
-        w_gate, w_up, w_down, gsum, gffn, down, next_w, next_d = refs[:8]
-        refs = refs[8:]
-    a, wv, wd, bv, bq, lsem, gsem = refs[:7]
-    sums, cube_g = refs[7:12], refs[12:15]
-    cube_d = (cube_g[0], *refs[15:17])
-    refs = refs[17:]
-    h = bv.shape[2]
-    shard = gsum.shape[1]
-    loads = [load(ffn_in, a.at[0], lsem.at[0])]
-    loads += [load(w.at[b], wv.at[b], lsem.at[1 + b]) for b in range(2)]
-    loads += [load(grad_out, a.at[1], lsem.at[3]), load(w_d, wd, lsem.at[4])]
-    if final:
-        gffn, mid_v, cot_v, tok_v, wmb, gbr, gm_out, gm_in, gb_in, rd_out, rd_in, wsem, ssem, rsem = refs
-        late = [load(src, dst, lsem.at[5 + i]) for i, (src, dst) in enumerate(((middle, mid_v), (cot, cot_v), (tok, tok_v), (gffn1, gffn)))]
-        mine = gm.shape[2]
-        half, ch = width // 2, mine // 2
-
-        def mix_load(j, s):
-            q = p.m ^ j
-            return pltpu.make_async_copy(
-                w_mix.at[pl.ds(pl.multiple_of(s * half + q * ch, LANE), ch)], wmb.at[s], wsem.at[s]
-            )
-
+    own, h, h_next, shard = rows // n_mp, bv.shape[2], next_d.shape[0], gsum.shape[1]
+    sums, cube_g, cube_d, zsem = refs[:5], refs[5:8], refs[8:11], refs[11:12]
+    loads = [load(ffn_in, a.at[0], lsem.at[0]), load(w, wv, lsem.at[1]), load(grad_out, a.at[1], lsem.at[2]), load(w_d, wd, lsem.at[3])]
     p.barrier()
-    if not final:
-        h_next = next_d.shape[0]
-        srcs = (w_gate.at[:, h:], w_up.at[:, h:], w_down.at[h:])
-
-        def next_dst(u, e, c):
-            at = pl.ds(pl.multiple_of((2 * e + c) * shard, LANE), shard)
-            return next_d.at[:, at] if u == 2 else next_w.at[u, at]
-
-        z = RowGather(p, refs, lambda u: srcs[u], next_dst)
-        own_next = [load(srcs[u], next_dst(u, p.k, p.c), lsem.at[5 + u]) for u in range(3)]
-        for u in range(3):
-            z.start(u)
+    srcs = (w_gate.at[:, h:], w_up.at[:, h:], w_down.at[h:])
+
+    def next_dst(u, e, c):
+        at = pl.ds(pl.multiple_of((2 * e + c) * shard, LANE), shard)
+        return next_d.at[:, at] if u == 2 else next_w.at[u, at]
+
+    z = RowGather(p, zsem, lambda u: srcs[u], next_dst)
+    own_next = [load(srcs[u], next_dst(u, p.k, p.c), lsem.at[5 + u]) for u in range(3)]
+    for u in range(3):
+        z.start(u)
     for copy in loads:
         copy.wait()
-    step = 240
-
-    def forward(i, _):
-        at = pl.ds(pl.multiple_of(i * step, 16), step)
-        gate = dot(a[0, at, :], wv[0])
-        up = dot(a[0, at, :], wv[1])
-        sig = sigmoid(gate)
-        silu = gate * sig
-        grad = dot_trans(a[1, at, :], wd[...])
-        values = (grad * up * sig * (1.0 + gate * (1.0 - sig)), grad * silu, silu * up)
-        for b in range(3):
-            bv[b, at, :] = values[b].astype(BF16)
+
+    f = FfnSums(p, a, wv, wd, h, bv, bq, gsum, gsem, sums, cube_g, cube_d)
+    total, g_cube, d_cube = f.total, f.g_cube, f.d_cube
+    n, chunks = total.blocks, rows // STEP
+    for j in (*range(1, chunks), 0):
+        i = lax.div(p.m * chunks, n_mp) ^ j
+        at = pl.ds(pl.multiple_of(i * STEP, 16), STEP)
+
+        def put(b, value):
+            bv[b, at, :] = value
             if own % 16:
-                for j in range(step // own):
-                    bq[b, i * (step // own) + j] = values[b][j * own : (j + 1) * own].astype(BF16)
-        return 0
-
-    lax.fori_loop(0, rows // step, forward, 0)
-    cols = bounds(width, p.bits, LANE)
-
-    def rows_of(b, q):
-        return bq[b, q] if own % 16 else bv[b, pl.ds(pl.multiple_of(q * own, 16), own), :]
-
-    def part_g(q, part):
-        lo, size = cols[part]
-        at = slice(lo, lo + size)
-        return dot_trans(rows_of(0, q), wv[0, at, :]) + dot_trans(rows_of(1, q), wv[1, at, :])
-
-    def part_d(q, part):
-        lo, size = cols[part]
-        return dot(rows_of(2, q), wd[:, lo : lo + size])
-
-    def piece(b, e):
-        left = jnp.where(b < 2, 0, 1)
-        return dot_rows(a[left, :, pl.ds(pl.multiple_of(e * shard, LANE), shard)], bv[b])
-
-    def finish(b, acc):
-        out = pltpu.make_async_copy(acc, gsum.at[b], gsem)
-        out.start()
-        out.wait()
-
-    total = RowSum(p, sums, piece, finish, False)
-    g_cube, d_cube = CubeSum(p, cube_g, part_g, width), CubeSum(p, cube_d, part_d, width)
-    n, chips = total.blocks, p.chips
-    if not final:
-        z.forward(0, 1)
-        total.run(0, n)
-        z.forward(1, 1)
+                wide = value.astype(F32)
+                for q in range(STEP // own):
+                    bq[b, i * (STEP // own) + q] = wide[q * own : (q + 1) * own].astype(BF16)
+
+        ffn_rows(at, own, a, wv[0], wv[1], wd[...], put)
+        if own == STEP and j:
+            g_cube.stage(0, j)
+    if own != STEP:
         g_cube.stage(0)
-        z.forward(2, 1)
-        for i in range(3):
-            total.run(n + i, n + i + 1)
-            z.forward(i, 2)
-        for s in range(1, p.bits):
-            g_cube.stage(s)
-        g_cube.drain()
-        d_cube.stage(0)
-    else:
-        total.run(0, n)
-        g_cube.stage(0)
-        total.run(n, 2 * n)
-        for s in range(1, p.bits):
-            g_cube.stage(s)
-        late[3].wait()
-        g_cube.drain()
-    for part, (lo, size) in enumerate(cols):
-        value = g_cube.result(part)
-        gffn[:, lo : lo + size] = gffn[:, lo : lo + size] + value if final else value
-    if not final:
-        for s in range(1, p.bits):
-            d_cube.stage(s)
-    else:
-        for copy in late[:3]:
+    z.forward(0, 1)
+    total.run(0, n)
+    z.forward(1, 1)
+    d_cube.stage(0)
+    z.forward(2, 1)
+    for i in range(3):
+        total.run(n + i, n + i + 1)
+        z.forward(i, 2)
+        if i == 1:
+            for s in range(1, p.bits):
+                g_cube.stage(s)
+    last = total.steps - n
+    for i in range(2 * n, last):
+        total.run(i, i + 1)
+        z.forward(i % n, i // n + 1)
+    for s in range(1, p.bits):
+        d_cube.stage(s)
+    for u in range(3):
+        z.finish(u)
+        own_next[u].wait()
+    loads = [load(next_w, wv2, lsem.at[8]), load(next_d, wd2, lsem.at[9])]
+    for copy in loads:
+        copy.wait()
+    sent = []
+    for i in range(chunks):
+        slot = i % 2
+        for copy in sent[i - 2 : i - 1] and sent[i - 2]:
             copy.wait()
-        mix_load(1, 0).start()
-        fine = 48 if own % 48 == 0 else own
-
-        def norm_back(i, gains):
-            at = pl.ds(pl.multiple_of(i * fine, fine), fine)
-            g = gffn[at, :]
-            n_own = mid_v[at, :] * r_mid[at, :]
-            gains = gains + jnp.sum((g * n_own).reshape(fine // 8, 8, width), axis=0)
-            gn = g * gain_ffn[...]
-            back = r_mid[at, :] * (gn - n_own * jnp.mean(gn * n_own, axis=-1, keepdims=True))
-            grad = cot_v[at, :].astype(F32) + back
-            gmid[at, :] = grad
-            low = grad.astype(BF16)
-            gbr[at, :] = low
-            dots = jnp.mean(low.astype(F32) * (mid_v[at, :] - tok_v[at, :].astype(F32)), axis=-1, keepdims=True)
-            rd_out[at, :] = jnp.broadcast_to(dots, (fine, LANE))
-            return gains
-
-        gains = lax.fori_loop(0, own // fine, norm_back, jnp.zeros((8, width), F32))
-        gain_part[...] = jnp.sum(gains, axis=0, keepdims=True)
-
-        def across(kind, j, owner):
-            send, recv, to = ssem.at[kind, j], rsem.at[kind, owner], p.peer(j)
-            if kind == 0:
-                return remote(gm_out.at[j], gm_in.at[owner], send, recv, to)
-            if kind == 1:
-                return remote(rd_out, rd_in.at[owner], send, recv, to)
-            here = pl.ds(pl.multiple_of((p.m ^ j) * mine, LANE), mine)
-            return remote(gbr.at[:, here], gb_in.at[owner], send, recv, to)
-
-        for j in range(1, n_mp):
-            across(1, j, p.m).start()
-        turns = [(j, s) for j in (*range(1, n_mp), 0) for s in range(2)]
-        for at, (j, s) in enumerate(turns):
-            mix_load(j, s).wait()
-            if at + 1 < len(turns):
-                mix_load(*turns[at + 1]).start()
-            value = dot_trans(gbr[...], wmb[s]).astype(BF16)
-            if j:
-                gm_out[j, :, s * ch : (s + 1) * ch] = value
-                if s:
-                    across(0, j, p.m).start()
-            else:
-                gm_in[p.m, :, s * ch : (s + 1) * ch] = value
-        for j in range(1, n_mp):
-            across(2, j, p.m).start()
-        gb_in[p.m] = gbr[:, pl.ds(pl.multiple_of(p.m * mine, LANE), mine)]
-        rd_in[p.m] = rd_out[...]
-        down_load = load(down1, gffn, lsem.at[9])
-        d_cube.stage(0)
-    if final:
-        total.run(2 * n, 3 * n)
-        for s in range(1, p.bits):
-            d_cube.stage(s)
-        total.run(3 * n, total.steps)
-    else:
-        for i in range(2 * n, total.steps):
-            total.run(i, i + 1)
-            if i // n + 1 < p.chips:
-                z.forward(i % n, i // n + 1)
-        for u in range(3):
-            z.finish(u)
-            own_next[u].wait()
-            z.drain(u)
-    if final:
-        for j in range(1, n_mp):
-            for kind in range(3):
-                across(kind, j, p.m ^ j).wait_recv()
-        back = [load(src, dst, lsem.at[10 + i]) for i, (src, dst) in enumerate(((gm_in, gm), (gb_in, gb), (rd_in, rowdot)))]
-        down_load.wait()
-        for part, (lo, size) in enumerate(cols):
-            at = slice(lo, lo + size)
-            mixed[:, at] = (mid_v[:, at] + gffn[:, at] + d_cube.result(part)).astype(BF16)
-        for j in range(1, n_mp):
-            for kind in range(3):
-                across(kind, j, p.m).wait_send()
-        for copy in back:
+
+        def put(b, value, slot=slot):
+            stage[slot, b] = value
+            if own % 16:
+                wide = value.astype(F32)
+                for j in range(STEP // own):
+                    stage_q[slot, b, j] = wide[j * own : (j + 1) * own].astype(BF16)
+
+        ffn_rows(
+            slice(i * STEP, (i + 1) * STEP), own, a, wv2[0], wv2[1], wd2[...], put
+        )
+        copies = [load(stage.at[slot], next_b.at[:, i * STEP : (i + 1) * STEP], bsem.at[0, i])]
+        if own % 16:
+            per = STEP // own
+            copies.append(load(stage_q.at[slot], next_q.at[:, i * per : (i + 1) * per], bsem.at[1, i]))
+        sent.append(copies)
+    total.run(last, total.steps)
+    for at, value in g_cube.results():
+        result[:, at] = value
+    load(result, gffn, lsem.at[10]).wait()
+    for at, value in d_cube.results():
+        result[:, at] = value
+    load(result, down, lsem.at[4]).wait()
+    for copies in sent[-2:]:
+        for copy in copies:
             copy.wait()
-    else:
-        for part, (lo, size) in enumerate(cols):
-            down[:, lo : lo + size] = d_cube.result(part)
+    g_cube.drain()
     d_cube.drain()
     total.drain()
-
-
-def ffn_part(n_dp, n_mp, cid, final, ffn_in, grad_out, w, w_d, *rest):
+    for u in range(3):
+        z.drain(u)
+
+
+def last_kernel(
+    n_dp, n_mp, ffn_in, grad_out, w, w_d, b_in, q_in, gffn1, down1, middle, r_mid, cot, tok, gain_ffn, w_mix,
+    gsum, base, parting, gmid, gain_part, gm, gb, rowdot,
+    a, wv, wd, bv, bq, gffn, mid_v, cot_v, tok_v, wmb, gbr, gm_out, gm_in, gb_in, rd_col, rd_out, rd_in,
+    lsem, gsem, wsem, ssem, rsem, *refs,
+):
+    p = Place(n_dp, n_mp)
     rows, width = ffn_in.shape
-    h = w.shape[2]
-    shard, own = width // n_dp, rows // n_mp
-    mine = width // n_mp
+    own, h = rows // n_mp, bv.shape[2]
+    mine = gm.shape[2]
+    half, ch = width // 2, mine // 2
+    sums, cube_g, cube_d = refs[:5], refs[5:8], refs[8:11]
+    loads_w = [load(b_in, bv, lsem.at[1]), load(w, wv, lsem.at[3])]
+    if own % 16:
+        loads_w.append(load(q_in, bq, lsem.at[5]))
+    loads = [load(ffn_in, a.at[0], lsem.at[0]), load(grad_out, a.at[1], lsem.at[2])]
+    loads_d = [load(w_d, wd, lsem.at[4])]
+    late = [
+        load(src, dst, lsem.at[6 + i])
+        for i, (src, dst) in enumerate(((middle, mid_v), (cot, cot_v), (tok.at[p.m], tok_v), (gffn1, gffn)))
+    ]
+
+    def mix_load(j, s):
+        q = p.m ^ j
+        return pltpu.make_async_copy(
+            w_mix.at[pl.ds(pl.multiple_of(s * half + q * ch, LANE), ch)], wmb.at[s], wsem.at[s]
+        )
+
+    p.barrier()
+    mix_load(1, 0).start()
+    f = FfnSums(p, a, wv, wd, h, bv, bq, gsum, gsem, sums, cube_g, cube_d)
+    total, g_cube, d_cube = f.total, f.g_cube, f.d_cube
+    n = total.blocks
+    for copy in loads_w:
+        copy.wait()
+    g_cube.stage(0)
+    for copy in loads:
+        copy.wait()
+    total.run(0, n + 1)
+    for s in range(1, p.bits):
+        g_cube.stage(s)
+    total.run(n + 1, n + 2)
+    for copy in loads_d:
+        copy.wait()
+    d_cube.stage(0)
+    total.run(n + 2, 2 * n)
+    for copy in late:
+        copy.wait()
+    for at, value in g_cube.results():
+        gffn[:, at] += value
+    fine = 16 if own % 16 == 0 else own
+
+    def norm_back(i, gains):
+        at = pl.ds(pl.multiple_of(i * fine, fine), fine)
+        g = gffn[at, :]
+        n_own = mid_v[at, :] * r_mid[at, :]
+        gains = gains + jnp.sum((g * n_own).reshape(fine // 8, 8, width), axis=0)
+        gn = g * gain_ffn[...]
+        back = r_mid[at, :] * (gn - n_own * jnp.mean(gn * n_own, axis=-1, keepdims=True))
+        grad = cot_v[at, :].astype(F32) + back
+        gffn[at, :] = grad
+        low = grad.astype(BF16)
+        gbr[at, :] = low
+        dots = jnp.mean(low.astype(F32) * (mid_v[at, :] - tok_v[at, :].astype(F32)), axis=-1, keepdims=True)
+        rd_col[at, :] = jnp.broadcast_to(dots, (fine, LANE))
+        return gains
+
+    gains = lax.fori_loop(0, own // fine, norm_back, jnp.zeros((8, width), F32))
+    gmid_out = load(gffn, gmid, lsem.at[15])
+    gain_part[...] = jnp.sum(gains, axis=0, keepdims=True)
+    rd_out[...] = lax.dot_general(
+        jnp.full((8, LANE), 1.0 / LANE, F32), rd_col[...], (((1,), (1,)), ((), ())),
+        precision=lax.Precision.HIGHEST, preferred_element_type=F32,
+    )
+
+    def across(kind, j, owner):
+        send, recv, to = ssem.at[kind, j], rsem.at[kind, owner], p.peer(j)
+        if kind == 0:
+            return remote(gm_out.at[j], gm_in.at[owner], send, recv, to)
+        if kind == 1:
+            return remote(rd_out, rd_in.at[owner], send, recv, to)
+        here = pl.ds(pl.multiple_of((p.m ^ j) * mine, LANE), mine)
+        return remote(gbr.at[:, here], gb_in.at[owner], send, recv, to)
+
+    for j in range(1, n_mp):
+        across(1, j, p.m).start()
+    turns = [(j, s) for j in (*range(1, n_mp), 0) for s in range(2)]
+    for at, (j, s) in enumerate(turns):
+        mix_load(j, s).wait()
+        if at + 1 < len(turns):
+            mix_load(*turns[at + 1]).start()
+        value = dot_trans(gbr[...], wmb[s]).astype(BF16)
+        if j:
+            gm_out[j, :, s * ch : (s + 1) * ch] = value
+            if s:
+                across(0, j, p.m).start()
+        else:
+            gm_in[p.m, :, s * ch : (s + 1) * ch] = value
+    for j in range(1, n_mp):
+        across(2, j, p.m).start()
+    gb_in[p.m] = gbr[:, pl.ds(pl.multiple_of(p.m * mine, LANE), mine)]
+    rd_in[p.m] = rd_out[...]
+    gmid_out.wait()
+    down_load = load(down1, gffn, lsem.at[10])
+    total.run(2 * n, total.steps - n)
+    for s in range(1, p.bits - 1):
+        d_cube.stage(s)
+    for part, at, value in d_cube.parting():
+        parting[part, :, at] = value.astype(BF16)
+    down_load.wait()
+    for at, value in d_cube.results(p.bits - 1):
+        gffn[:, at] += mid_v[:, at] + value
+    back = [load(gffn, base, lsem.at[14])]
+    total.run(total.steps - n, total.steps)
+    for j in range(1, n_mp):
+        for kind in range(3):
+            across(kind, j, p.m ^ j).wait_recv()
+    back.extend(load(src, dst, lsem.at[11 + i]) for i, (src, dst) in enumerate(((gm_in, gm), (gb_in, gb), (rd_in, rowdot))))
+    for j in range(1, n_mp):
+        for kind in range(3):
+            across(kind, j, p.m).wait_send()
+    for copy in back:
+        copy.wait()
+    g_cube.drain()
+    d_cube.drain(p.bits - 1)
+    total.drain()
+
+
+def split_shape(n_mp, own, h):
+    return (3, n_mp, own, h) if own % 16 else (1, 1, 16, LANE)
+
+
+def parting_shape(n_mp, own, width):
+    bits = n_mp.bit_length() - 1
+    return (bits, own, max(size for _, size in bounds(width, bits, LANE)))
+
+
+def ffn_first(n_dp, n_mp, cid, *args):
+    (rows, width), h = args[0].shape, args[2].shape[2]
+    shard, own, h_next = width // n_dp, rows // n_mp, args[6].shape[0] - h
     f_own = jax.ShapeDtypeStruct((own, width), F32)
-    gsum = jax.ShapeDtypeStruct((3, shard, h), F32)
-    scratch = [
-        pltpu.VMEM((2, rows, width), BF16),
-        pltpu.VMEM((2, width, h), BF16),
-        pltpu.VMEM((h, width), BF16),
-        pltpu.VMEM((3, rows, h), BF16),
-        pltpu.VMEM((3, n_mp, own, h) if own % 16 else (1, 1, 16, LANE), BF16),
-        pltpu.SemaphoreType.DMA((13,)),
-        pltpu.SemaphoreType.DMA,
-        *RowSum.scratch(n_dp, 3, shard, h),
-        *CubeSum.scratch(n_mp, own, width),
-        *CubeSum.scratch(n_mp, own, width)[1:],
-    ]
-    if final:
-        piece = jax.ShapeDtypeStruct((n_mp, own, mine), BF16)
-        outs = (
-            gsum, jax.ShapeDtypeStruct((own, width), BF16), f_own, jax.ShapeDtypeStruct((1, width), F32),
-            piece, piece, jax.ShapeDtypeStruct((n_mp, own, LANE), F32),
-        )
-        scratch += [
+    per = STEP // own if own % 16 else 1
+    return pl.pallas_call(
+        functools.partial(first_kernel, n_dp, n_mp),
+        out_shape=(
+            jax.ShapeDtypeStruct((3, shard, h), F32), f_own, f_own,
+            jax.ShapeDtypeStruct((2, width, h_next), BF16), jax.ShapeDtypeStruct((h_next, width), BF16),
+            jax.ShapeDtypeStruct((3, rows, h_next), BF16), jax.ShapeDtypeStruct(split_shape(n_mp, own, h_next), BF16),
+        ),
+        in_specs=[ANY] * 7,
+        out_specs=(ANY,) * 7,
+        scratch_shapes=[
+            pltpu.VMEM((2, rows, width), BF16),
+            pltpu.VMEM((2, width, h), BF16),
+            pltpu.VMEM((h, width), BF16),
+            pltpu.VMEM((2, width, h_next), BF16),
+            pltpu.VMEM((h_next, width), BF16),
+            pltpu.VMEM((3, rows, h), BF16),
+            pltpu.VMEM(split_shape(n_mp, own, h), BF16),
+            pltpu.VMEM((2, 3, STEP, h_next), BF16),
+            pltpu.VMEM((2, 3, per, own, h_next) if own % 16 else (1, 1, 1, 16, LANE), BF16),
+            pltpu.VMEM((own, width), F32),
+            pltpu.SemaphoreType.DMA((11,)),
+            pltpu.SemaphoreType.DMA,
+            pltpu.SemaphoreType.DMA((2, rows // STEP)),
+            *RowSum.scratch(n_dp, 3, shard, h),
+            *CubeSum.scratch(n_mp, own, width),
+            *CubeSum.scratch(n_mp, own, width),
+            *RowGather.scratch(n_dp, 3),
+        ],
+        compiler_params=pltpu.CompilerParams(collective_id=cid, has_side_effects=True, vmem_limit_bytes=VMEM_LIMIT),
+        name="ffn_first",
+    )(*args)
+
+
+def ffn_last(n_dp, n_mp, cid, *args):
+    (rows, width), h = args[0].shape, args[2].shape[2]
+    shard, own, mine = width // n_dp, rows // n_mp, width // n_mp
+    piece = jax.ShapeDtypeStruct((n_mp, own, mine), BF16)
+    return pl.pallas_call(
+        functools.partial(last_kernel, n_dp, n_mp),
+        out_shape=(
+            jax.ShapeDtypeStruct((3, shard, h), F32), jax.ShapeDtypeStruct((own, width), F32),
+            jax.ShapeDtypeStruct(parting_shape(n_mp, own, width), BF16),
+            jax.ShapeDtypeStruct((own, width), F32), jax.ShapeDtypeStruct((1, width), F32),
+            piece, piece, jax.ShapeDtypeStruct((n_mp, 8, own), F32),
+        ),
+        in_specs=[ANY] * 9 + [VMEM, ANY, ANY, VMEM, ANY],
+        out_specs=(ANY, ANY, VMEM, ANY, VMEM, ANY, ANY, ANY),
+        scratch_shapes=[
+            pltpu.VMEM((2, rows, width), BF16),
+            pltpu.VMEM((2, width, h), BF16),
+            pltpu.VMEM((h, width), BF16),
+            pltpu.VMEM((3, rows, h), BF16),
+            pltpu.VMEM(split_shape(n_mp, own, h), BF16),
             pltpu.VMEM((own, width), F32),
             pltpu.VMEM((own, width), F32),
             pltpu.VMEM((own, width), BF16),
@@ -1226,36 +1374,26 @@
             pltpu.VMEM((own, width), BF16),
             *[pltpu.VMEM((n_mp, own, mine), BF16)] * 3,
             pltpu.VMEM((own, LANE), F32),
-            pltpu.VMEM((n_mp, own, LANE), F32),
+            pltpu.VMEM((8, own), F32),
+            pltpu.VMEM((n_mp, 8, own), F32),
+            pltpu.SemaphoreType.DMA((16,)),
+            pltpu.SemaphoreType.DMA,
             pltpu.SemaphoreType.DMA((2,)),
             pltpu.SemaphoreType.DMA((3, n_mp)),
             pltpu.SemaphoreType.DMA((3, n_mp)),
-        ]
-        in_specs = [ANY] * 7 + [VMEM, ANY, ANY, VMEM, ANY]
-        out_specs = (ANY, VMEM, VMEM, VMEM, ANY, ANY, ANY)
-    else:
-        h_next = rest[2].shape[0] - h
-        outs = (
-            gsum, f_own, f_own,
-            jax.ShapeDtypeStruct((2, width, h_next), BF16), jax.ShapeDtypeStruct((h_next, width), BF16),
-        )
-        scratch += RowGather.scratch(n_dp, 3)
-        in_specs = [ANY] * 7
-        out_specs = (ANY, VMEM, VMEM, ANY, ANY)
-    return pl.pallas_call(
-        functools.partial(ffn_kernel, n_dp, n_mp, final),
-        out_shape=outs,
-        in_specs=in_specs,
-        out_specs=out_specs,
-        scratch_shapes=scratch,
+            *RowSum.scratch(n_dp, 3, shard, h),
+            *CubeSum.scratch(n_mp, own, width),
+            *CubeSum.scratch(n_mp, own, width, False),
+        ],
         compiler_params=pltpu.CompilerParams(collective_id=cid, has_side_effects=True, vmem_limit_bytes=VMEM_LIMIT),
-        name="ffn_last" if final else "ffn_first",
-    )(ffn_in, grad_out, w, w_d, *rest)
+        name="ffn_last",
+    )(*args)
 
 
 def project_kernel(
-    n_dp, n_mp, normed, mixed, g_in, g_f, g_g, g_b, g_split, w, gmid, tok, r_in, gain_in, gain_ffn_part, dgain, dbound,
-    gw, gtok, small, a, bv, bq, wv, lsem, rsend, rrecv, gall, *refs,
+    n_dp, n_mp, normed, mixed, gm, g_b, pin, pf, pg, st, phasor, r_mix, rowdot, bound, gain_mix, w, gmid, tok, r_in, gain_in,
+    gain_ffn_part, base, parting, gw, gtok, small, done,
+    a, bv, bq, gall, dgain, dbound, tok_v, base_v, last_v, lsem, rsend, rrecv, dsem, *refs,
 ):
     p = Place(n_dp, n_mp)
     rows, width = normed.shape
@@ -1263,121 +1401,197 @@
     half, ch, own = width // 2, mine // 2, rows // n_mp
     shard = gw.shape[2]
     sums, cube_refs, vec = refs[:5], refs[5:8], SmallSum(p, refs[8:10])
-    loads = [load(normed, a.at[0], lsem.at[0])]
-    loads += [load(src, bv.at[i], lsem.at[1 + i]) for i, src in enumerate((g_in, g_f, g_g, g_b))]
-    loads += [load(mixed, a.at[1], lsem.at[5])]
-    late = [load(w.at[i], wv.at[i], lsem.at[6 + i]) for i in range(3)]
-    if own % 16:
-        late.append(load(g_split, bq, lsem.at[9]))
+    loads = [load(mixed, a.at[0], lsem.at[0]), load(g_b, bv.at[0], lsem.at[1])]
+    late = [load(normed, a.at[1], lsem.at[12])]
+    late.append(load(tok.at[p.m], tok_v, lsem.at[16]))
+    early_d = [load(parting, last_v.at[0], lsem.at[19])]
+    late_d = load(base, base_v, lsem.at[20])
     p.barrier(far=True)
     for copy in loads:
         copy.wait()
 
+    down_cols = bounds(width, p.bits, LANE)
+
+    def last_stage(part):
+        size = down_cols[part][1]
+        to = p.peer(1 << ((part + p.bits - 1) % p.bits))
+        return remote(last_v.at[0, part, :, :size], last_v.at[1, part, :, :size], dsem.at[0, part], dsem.at[1, part], to)
+
+    for copy in early_d:
+        copy.wait()
+    for part in range(p.bits):
+        last_stage(part).start()
+
     def piece(b, e):
-        left = jnp.where(b < 3, 0, 1)
+        left = jnp.where(b == 0, 0, 1)
         return dot_rows(a[left, :, pl.ds(pl.multiple_of(e * shard, LANE), shard)], bv[b])
 
-    def out_copy(b, mask, owner):
-        return remote(gall.at[b, owner], gall.at[b, owner], rsend.at[b, mask], rrecv.at[b, owner], p.peer(mask))
+    out_cols = bounds(mine, p.bits, LANE)
+
+    def spread(b):
+        def view(q, part):
+            lo, size = out_cols[part]
+            return gall.at[b, q, :, lo : lo + size]
+
+        return CubeGather(p, (rsend.at[b], rrecv.at[b]), view)
 
     def finish(b, acc):
         gall[b, p.m] = acc[...].astype(BF16)
-        for mask in range(1, n_mp):
-            out_copy(b, mask, p.m).start()
-
-    cols = bounds(width, p.bits, LANE)
-
-    def partial(q, part):
-        lo, size = cols[part]
+        spread(b).stage(0)
+        for s in range(1, p.bits):
+
+            @pl.when(b >= s)
+            def _():
+                spread(b - s).stage(s)
+
+    def partial(q, lo, size):
         value = 0.0
         for b in range(3):
-            left = bq[b, q] if own % 16 else bv[b, pl.ds(pl.multiple_of(q * own, 16), own), :]
-            value = value + dot_trans(left, wv[b, lo : lo + size, :])
+            left = bq[b, q] if own % 16 else bv[1 + b, pl.ds(pl.multiple_of(q * own, 16), own), :]
+            value = value + dot_trans(left, held[0][b, lo : lo + size, :])
         return value
 
+    held = []
     total = RowSum(p, sums, piece, finish, True)
     cube = CubeSum(p, cube_refs, partial, width)
-    tick = p.chips
-    total.run(0, tick)
-    for copy in late:
-        copy.wait()
-    cube.stage(0)
-    total.run(tick, 2 * tick)
-    for s in range(1, p.bits):
-        cube.stage(s)
-    total.run(2 * tick, 3 * tick)
-    for part, (lo, size) in enumerate(cols):
-        gtok[:, lo : lo + size] = cube.result(part)
-    fine = 48 if own % 48 == 0 else own
-
-    def norm_back(i, gains):
-        at = pl.ds(pl.multiple_of(i * fine, fine), fine)
-        g = gtok[at, :]
-        n_own = tok[at, :].astype(F32) * r_in[at, :]
-        gains = gains + jnp.sum((g * n_own).reshape(fine // 8, 8, width), axis=0)
-        gn = g * gain_in[...]
-        gtok[at, :] = gmid[at, :] + r_in[at, :] * (gn - n_own * jnp.mean(gn * n_own, axis=-1, keepdims=True))
-        return gains
-
-    gains = lax.fori_loop(0, own // fine, norm_back, jnp.zeros((8, width), F32))
-    vec.buf[0] = jnp.zeros((4, width), F32)
-    vec.buf[0, 0:1] = jnp.sum(gains, axis=0, keepdims=True)
-    vec.buf[0, 1:2] = gain_ffn_part[...]
-    here = pl.ds(pl.multiple_of(p.m * ch, LANE), ch)
-    vec.buf[0, 2:3, here] = dgain[:, :ch]
-    vec.buf[0, 2:3, pl.ds(pl.multiple_of(half + p.m * ch, LANE), ch)] = dgain[:, ch:]
-    vec.buf[0, 3:4, here] = dbound[...]
-    vec.twins()
-    total.run(3 * tick, 4 * tick)
-    vec.cube()
-    total.run(4 * tick, 5 * tick)
-    vec.line()
-    total.run(5 * tick, total.steps)
-    for b in range(4):
-        for mask in range(1, n_mp):
-            out_copy(b, mask, p.m ^ mask).wait_recv()
-    out = load(gall, gw, lsem.at[10])
-    small[...] = vec.result()
-    out.wait()
-    for b in range(4):
-        for mask in range(1, n_mp):
-            out_copy(b, mask, p.m).wait_send()
-    cube.drain()
-    total.drain()
-
-
-def project_back(n_dp, n_mp, cid, normed, mixed, g_in, g_f, g_g, g_b, w, gmid, tok, r_in, gain_in, *vectors):
-    rows, width = normed.shape
-    mine, shard, own = g_in.shape[1], width // n_dp, rows // n_mp
-    if own % 16:
-        g_split = jnp.stack([g.reshape(n_mp, own, mine) for g in (g_in, g_f, g_g)])
-    else:
-        g_split = jnp.zeros((1, 1, 16, LANE), BF16)
+    tick, early = p.chips, p.chips - 1
+    def recurrence(gm_v, pin_v, pf_v, pg_v, st_v, ph_v, r_v, rd_v, bl, gain, a_re, a_im, b_re, b_im):
+        scans = [
+            load(src, dst, lsem.at[2 + i])
+            for i, (src, dst) in enumerate(
+                ((gm, gm_v), (pg, pg_v), (st, st_v), (pf, pf_v), (phasor, ph_v), (pin, pin_v), (r_mix, r_v))
+            )
+        ]
+        scans.append(load(bound.at[:, pl.ds(pl.multiple_of(p.m * ch, LANE), ch)], bl, lsem.at[9]))
+        for side in range(2):
+            at = pl.ds(pl.multiple_of(side * half + p.m * ch, LANE), ch)
+            scans.append(load(gain_mix.at[:, at], gain.at[:, side * ch : (side + 1) * ch], lsem.at[10 + side]))
+        eighth = jnp.full((8, LANE), 0.125, F32)
+        for q in range(n_mp):
+            rd_v[q * own : (q + 1) * own, :] = lax.dot_general(
+                rowdot[q], eighth, (((0,), (0,)), ((), ())), precision=lax.Precision.HIGHEST, preferred_element_type=F32
+            )[:, :1]
+        total.run(0, 1, ahead=False)
+        for copy in scans:
+            copy.wait()
+        scan_backward(
+            gm_v, pin_v, pf_v, pg_v, st_v, ph_v, r_v, rd_v, bl, gain, bv.at[1], bv.at[2], bv.at[3], dgain, dbound,
+            a_re, a_im, b_re, b_im,
+            between=(lambda: total.run(1, 2, True, False), lambda: total.run(2, early, True, False)),
+        )
+
+    part, column = (rows, mine), pltpu.VMEM((rows, 1), F32)
+    pl.run_scoped(
+        recurrence,
+        pltpu.VMEM(part, BF16), *[pltpu.VMEM(part, F32)] * 5, column, column, pltpu.VMEM((1, ch), F32), pltpu.VMEM((1, mine), F32),
+        *[pltpu.VMEM((ch // LANE, rows, LANE), F32)] * 4,
+    )
+
+    def sums_over_devices(wv):
+        held.append(wv)
+        late.extend(load(w.at[i], wv.at[i], lsem.at[13 + i]) for i in range(3))
+        for copy in late:
+            copy.wait()
+        if own % 16:
+            for b in range(3):
+                wide = bv[1 + b].astype(F32)
+                for q in range(n_mp):
+                    bq[b, q] = wide[q * own : (q + 1) * own].astype(BF16)
+        total.run(early, early + tick, True)
+        cube.stage(0)
+        total.run(early + tick, early + 2 * tick)
+        late_d.wait()
+        done_out = []
+        for part, (lo, size) in enumerate(down_cols):
+            last_stage(part).wait()
+            value = base_v[:, lo : lo + size] + last_v[1, part, :, :size].astype(F32)
+            last_v[1, part, :, :size] = value.astype(BF16)
+            done_out.append(load(last_v.at[1, part, :, :size], done.at[:, lo : lo + size], dsem.at[2, part]))
+        gmid_load = load(gmid, base_v, lsem.at[17])
+        total.run(early + 2 * tick, early + 3 * tick)
+        for s in range(1, p.bits):
+            cube.stage(s)
+        total.run(early + 3 * tick, early + 4 * tick)
+        for at, value in cube.results():
+            gtok[:, at] = value
+        gmid_load.wait()
+        fine = 16 if own % 16 == 0 else own
+
+        def norm_back(i, gains):
+            at = pl.ds(pl.multiple_of(i * fine, fine), fine)
+            g = gtok[at, :]
+            n_own = tok_v[at, :].astype(F32) * r_in[at, :]
+            gains = gains + jnp.sum((g * n_own).reshape(fine // 8, 8, width), axis=0)
+            gn = g * gain_in[...]
+            gtok[at, :] = base_v[at, :] + r_in[at, :] * (gn - n_own * jnp.mean(gn * n_own, axis=-1, keepdims=True))
+            return gains
+
+        gains = lax.fori_loop(0, own // fine, norm_back, jnp.zeros((8, width), F32))
+        vec.buf[0] = jnp.zeros((4, width), F32)
+        vec.buf[0, 0:1] = jnp.sum(gains, axis=0, keepdims=True)
+        vec.buf[0, 1:2] = gain_ffn_part[...]
+        here = pl.ds(pl.multiple_of(p.m * ch, LANE), ch)
+        vec.buf[0, 2:3, here] = dgain[:, :ch]
+        vec.buf[0, 2:3, pl.ds(pl.multiple_of(half + p.m * ch, LANE), ch)] = dgain[:, ch:]
+        vec.buf[0, 3:4, here] = dbound[...]
+        vec.twins()
+        total.run(early + 4 * tick, early + 5 * tick)
+        vec.cube()
+        total.run(early + 5 * tick, total.steps)
+        for b in range(total.blocks):
+            for s in range(max(1, total.blocks - b), p.bits):
+                spread(b).stage(s)
+        vec.line()
+        for b in range(total.blocks):
+            spread(b).last()
+        out = load(gall, gw, lsem.at[18])
+        small[...] = vec.result()
+        for copy in done_out:
+            copy.wait()
+        out.wait()
+        for b in range(total.blocks):
+            spread(b).drain()
+        cube.drain()
+        total.drain()
+
+
+    pl.run_scoped(sums_over_devices, pltpu.VMEM((3, width, mine), BF16))
+
+
+def project_back(n_dp, n_mp, cid, *args):
+    rows, width = args[0].shape
+    mine, shard, own = width // n_mp, width // n_dp, rows // n_mp
+    ch = mine // 2
     return pl.pallas_call(
         functools.partial(project_kernel, n_dp, n_mp),
         out_shape=(
             jax.ShapeDtypeStruct((4, n_mp, shard, mine), BF16),
             jax.ShapeDtypeStruct((own, width), F32),
             jax.ShapeDtypeStruct((4, width), F32),
+            jax.ShapeDtypeStruct((own, width), BF16),
         ),
-        in_specs=[ANY] * 8 + [VMEM] * 7,
-        out_specs=(ANY, VMEM, VMEM),
+        in_specs=[ANY] * 10 + [VMEM] + [ANY] * 5 + [VMEM] * 3 + [ANY] * 2,
+        out_specs=(ANY, VMEM, VMEM, ANY),
         scratch_shapes=[
             pltpu.VMEM((2, rows, width), BF16),
             pltpu.VMEM((4, rows, mine), BF16),
-            pltpu.VMEM(g_split.shape, BF16),
-            pltpu.VMEM((3, width, mine), BF16),
-            pltpu.SemaphoreType.DMA((11,)),
-            pltpu.SemaphoreType.DMA((4, n_mp)),
-            pltpu.SemaphoreType.DMA((4, n_mp)),
+            pltpu.VMEM((3, n_mp, own, mine) if own % 16 else (1, 1, 16, LANE), BF16),
             pltpu.VMEM((4, n_mp, shard, mine), BF16),
+            pltpu.VMEM((1, mine), F32),
+            pltpu.VMEM((1, ch), F32),
+            pltpu.VMEM((own, width), BF16),
+            pltpu.VMEM((own, width), F32),
+            pltpu.VMEM((2, *parting_shape(n_mp, own, width)), BF16),
+            pltpu.SemaphoreType.DMA((21,)),
+            *[pltpu.SemaphoreType.DMA((4, n_mp.bit_length() - 1, n_mp))] * 2,
+            pltpu.SemaphoreType.DMA((3, n_mp)),
             *RowSum.scratch(n_dp, 4, shard, mine),
             *CubeSum.scratch(n_mp, own, width),
             *SmallSum.scratch(n_dp, n_mp, (4, width)),
         ],
         compiler_params=pltpu.CompilerParams(collective_id=cid, has_side_effects=True, vmem_limit_bytes=VMEM_LIMIT),
         name="project_back",
-    )(normed, mixed, g_in, g_f, g_g, g_b, g_split, w, gmid, tok, r_in, gain_in, *vectors)
+    )(*args)
 
 
 def result_kernel(
@@ -1396,11 +1610,11 @@
         for i in range(3)
     ]
     outs = []
-    for b, out in enumerate((o_win, o_wf, o_wo, o_wm)):
+    for b, out in enumerate((o_wm, o_win, o_wf, o_wo)):
         mixer[b].wait()
         for q in range(n_mp):
             value = gm[b, q].astype(F32)
-            if b < 3:
+            if b:
                 gw[b, :, q * ch : (q + 1) * ch] = value[:, :ch]
                 gw[b, :, half + q * ch : half + (q + 1) * ch] = value[:, ch:]
             else:
@@ -1473,13 +1687,10 @@
     own = rows // n_mp
     ffn = w_gate.shape[1]
     padded = -(-ffn // LANE) * LANE
-    cut = -(-padded // 2 // LANE) * LANE
+    cut = padded // 2 // LANE * LANE
     if padded != ffn:
         fill = ((0, 0), (0, padded - ffn))
         w_gate, w_up, w_down = jnp.pad(w_gate, fill), jnp.pad(w_up, fill), jnp.pad(w_down, fill[::-1])
-
-    def own_rows(x):
-        return lax.dynamic_slice_in_dim(x, m * own, own, 0)
 
     normed, r_in, pin, pf, pg, st, phasor, r_mix, mixer_out, ffn_in, middle, r_mid, wm, w_cat, w_one, d_one, grad_out = mixer_forward(
         n_dp, n_mp, 2, cut, w_in, w_forget, w_outgate, w_mix, w_gate, w_up, w_down, cotangent, tokens, segment_ids,
@@ -1487,34 +1698,17 @@
     )
     grad_out = grad_out.reshape(rows, width)
 
-    g_one, gffn, down, w_two, d_two = ffn_part(
-        n_dp, n_mp, 3, False, ffn_in, grad_out, w_one, d_one, w_gate, w_up, w_down
+    g_one, gffn, down, w_two, d_two, b_two, q_two = ffn_first(
+        n_dp, n_mp, 3, ffn_in, grad_out, w_one, d_one, w_gate, w_up, w_down
     )
-    tok_own = own_rows(tokens)
-    g_two, mixed, gmid, gain_ffn_part, gm, gb, rowdot = ffn_part(
-        n_dp, n_mp, 4, True, ffn_in, grad_out, w_two, d_two, gffn, down, middle, r_mid, cotangent, tok_own, gain_ffn[None], wm
+    tok_own = tokens.reshape(n_mp, own, width)
+    g_two, base, parting, gmid, gain_ffn_part, gm, gb, rowdot = ffn_last(
+        n_dp, n_mp, 4, ffn_in, grad_out, w_two, d_two, b_two, q_two, gffn, down, middle, r_mid, cotangent, tok_own,
+        gain_ffn[None], wm,
     )
-
-    bl = lax.dynamic_slice_in_dim(bound_logit, m * ch, ch, 0)[None]
-    gain = jnp.concatenate([lax.dynamic_slice_in_dim(gain_mix, at + m * ch, ch, 0) for at in (0, half)])[None]
-    lanes = ch // LANE
-    scratch = [pltpu.VMEM((lanes, rows, LANE), F32)] * 4
-    gin, gf, gg, dgain, dbound = call_local(
-        scan_backward,
-        (
-            jax.ShapeDtypeStruct((rows, mine), BF16),
-            jax.ShapeDtypeStruct((rows, mine), BF16),
-            jax.ShapeDtypeStruct((rows, mine), BF16),
-            jax.ShapeDtypeStruct((1, mine), F32),
-            jax.ShapeDtypeStruct((1, ch), F32),
-        ),
-        scratch,
-        gm.reshape(rows, mine), pin, pf, pg, st, phasor, r_mix, rowdot.reshape(rows, LANE)[:, :1], bl, gain,
-        name="scan_backward",
-    )
-    g_mixer, grad_tokens, small = project_back(
-        n_dp, n_mp, 5, normed, mixer_out, gin, gf, gg, gb.reshape(rows, mine), w_cat, gmid, tok_own, own_rows(r_in),
-        gain_in[None], gain_ffn_part, dgain, dbound,
+    g_mixer, grad_tokens, small, mixed = project_back(
+        n_dp, n_mp, 5, normed, mixer_out, gm.reshape(rows, 2 * ch), gb.reshape(rows, 2 * ch), pin, pf, pg, st, phasor, r_mix, rowdot,
+        bound_logit[None], gain_mix[None], w_cat, gmid, tok_own, r_in, gain_in[None], gain_ffn_part, base, parting,
     )
 
     out = results(n_dp, n_mp, g_mixer, g_one, g_two, mixed, grad_tokens, small)

time: 558 us -> 478 us (0.86)
  Pallas kernels: 536 us -> 468 us
  local copies, waits for them, and re-layouts: 12.1 us -> 0 us
    pallas_call x3 -> x2, Pallas kernels: 258 us -> 207 us  [the longest x1 108 us: ffn_first(): pl.pallas_call(functools.partial(first_kernel, n_dp, n_mp), out_shape=(ja...]
    pallas_call x1, Pallas kernels: 116 us -> 106 us  [project_back(): pl.pallas_call(functools.partial(project_kernel, n_dp, n_mp), out_shape=(...]
    pallas_call x1, Pallas kernels: 150 us -> 143 us  [mixer_forward(): pl.pallas_call(functools.partial(mixer_kernel, n_dp, n_mp), out_shape=(bf...]
    unnamed x16 -> x0, local copies, waits for them, and re-layouts: 6.2 us -> none
where the time goes in v4:
time: 478 us; the launch traced here: 469 us
  Pallas kernels  468 us (98%)
    pallas_call x1, Pallas kernels, mixer_forward(): pl.pallas_call(functools.partial(mixer_kernel, n_dp, n_mp), out_shape=(bf...  143 us
    pallas_call x1, Pallas kernels, ffn_first(): pl.pallas_call(functools.partial(first_kernel, n_dp, n_mp), out_shape=(ja...  108 us
    pallas_call x1, Pallas kernels, project_back(): pl.pallas_call(functools.partial(project_kernel, n_dp, n_mp), out_shape=(...  106 us
    pallas_call x1, Pallas kernels, ffn_last(): pl.pallas_call(functools.partial(last_kernel, n_dp, n_mp), out_shape=(jax...  98.8 us
    pallas_call x1, Pallas kernels, results(): pl.pallas_call(functools.partial(result_kernel, n_mp), out_shape=(jax.Sha...  12 us

profile of v4, /device:TPU:8, one launch (start us, length us, event | category | flops | bytes accessed | tf_op | source)
XLA Modules:
  0.0 469.3 jit_solution(8749104917027161644)
XLA Ops:
  0.6 143.0 %mixer_forward.1 = (bf16[960,2048]{1,0:T(8,128)(2,1)}, f32[240,1]{1,0:T(8,128)}, f32[960,512]{1,0:T(8,128)}, f32[960,512]{1,0:T(8,128)}, f32[960,512]{1,0:T(8,12...) custom-call(bf16[256,2048]{1,0:T(8,128)(2,1)} %w_in.1, ...), custom_call_target="tpu_custom_call" | custom-call | tf_op jit(solution)/shard_map/mixer_forward/pallas_call | solution.py:993
  143.6 108.4 %ffn_first.1 = (f32[3,256,640]{2,1,0:T(8,128)}, f32[240,2048]{1,0:T(8,128)}, f32[240,2048]{1,0:T(8,128)}, bf16[2,2048,768]{2,1,0:T(8,128)(2,1)}, bf16[768,2048]{...) custom-call(bf16[960,2048]{1,0:T(8,128)(2,1)} %get-tuple-element.64.ffn_in, ...), custom_call_target="tpu_custom_call" | custom-call | tf_op jit(solution)/shard_map/ffn_first/pallas_call | solution.py:1316
  252.0 98.8 %ffn_last.1 = (f32[3,256,768]{2,1,0:T(8,128)}, f32[240,2048]{1,0:T(8,128)}, bf16[2,240,1024]{2,1,0:T(8,128)(2,1)}, f32[240,2048]{1,0:T(8,128)}, f32[1,2048]{1,0:...) custom-call(bf16[960,2048]{1,0:T(8,128)(2,1)} %get-tuple-element.64.ffn_in, ...), custom_call_target="tpu_custom_call" | custom-call | tf_op jit(solution)/shard_map/ffn_last/pallas_call | solution.py:1353
  350.8 106.1 %project_back.1 = (bf16[4,4,256,512]{3,2,1,0:T(8,128)(2,1)}, f32[240,2048]{1,0:T(8,128)}, f32[4,2048]{1,0:T(4,128)}, bf16[240,2048]{1,0:T(8,128)(2,1)}) custom-call(bf16[960,2048]{1,0:T(8,128)(2,1)} %get-tuple-element.62.normed, bf16[960,2048]{1,0:T(8,128)(2,1)} %get-tuple-element.63.mixed, bf16[960,512]{1,0:T(8,128)(2,1)} %bitcast.16, ...), custom_call_target="tpu_custom_call" | custom-call | tf_op jit(solution)/shard_map/project_back/pallas_call | solution.py:1565
  456.8 12.0 %results.1 = (bf16[240,2048]{1,0:T(8,128)(2,1)}, f32[240,2048]{1,0:T(8,128)}, f32[1,256]{1,0:T(1,128)}, f32[256,2048]{1,0:T(8,128)}, f32[256,2048]{1,0:T(8,128)}...) custom-call(bf16[4,4,256,512]{3,2,1,0:T(8,128)(2,1)} %get-tuple-elem, ...), custom_call_target="tpu_custom_call" | custom-call | tf_op jit(solution)/shard_map/results/pallas_call | solution.py:1657

commit v5 on v4

--- a/solution.py
+++ b/solution.py
@@ -784,7 +784,7 @@
         return cot_v.at[q, :, lo : lo + size]
 
     cot_own.wait()
-    gc = CubeGather(p, gsems[10:12], cot_view)
+    gc = CubeGather(p, gsems[18:20], cot_view)
     gc.stage(0)
     tok_load.wait()
     fine = 48
@@ -903,7 +903,7 @@
         mix[at, im_at] = value[:, ch:]
         return 0
 
-    spans = 2
+    spans = 4
     span = rows // spans
     gathers = []
     for n in range(spans):
@@ -923,7 +923,7 @@
             g.stage(s)
     z.forward(6, 1)
     gc.last()
-    outs.append(load(cot_v, cot_o, osem.at[17]))
+    outs.append(load(cot_v, cot_o, osem.at[21]))
     for part in range(p.bits):
         for sub in range(n_mp):
             from_twin(part, sub).wait_recv()
@@ -950,11 +950,9 @@
         at = slice(n * span, (n + 1) * span)
         outs.append(load(ffn_v.at[at], ffn_o.at[at], osem.at[12 + 2 * n]))
         outs.append(load(mix.at[at], mix_o.at[at], osem.at[13 + 2 * n]))
-        if n == 0:
-            z.forward(4, 2)
+        if n < 3:
+            z.forward(4 + n, 2)
     outs.append(load(mid_v, mid_o, osem.at[12 + 2 * spans]))
-    z.forward(5, 2)
-    z.forward(6, 2)
     for s in range(3, p.chips):
         for u in range(4, 7):
             z.forward(u, s)
@@ -1016,11 +1014,11 @@
             pltpu.VMEM((8, rows), F32),
             pltpu.VMEM((n_mp, 8, rows), F32),
             pltpu.SemaphoreType.DMA((17,)),
-            pltpu.SemaphoreType.DMA((18,)),
+            pltpu.SemaphoreType.DMA((22,)),
             pltpu.SemaphoreType.DMA((2, n_mp)),
             pltpu.SemaphoreType.DMA((2, bits, n_mp)),
             *RowGather.scratch(n_dp, 7),
-            *CubeGather.scratch(n_mp) * 6,
+            *CubeGather.scratch(n_mp) * 10,
         ],
         compiler_params=pltpu.CompilerParams(collective_id=cid, has_side_effects=True, vmem_limit_bytes=VMEM_LIMIT),
         name="mixer_forward",
@@ -1497,8 +1495,8 @@
                 wide = bv[1 + b].astype(F32)
                 for q in range(n_mp):
                     bq[b, q] = wide[q * own : (q + 1) * own].astype(BF16)
+        cube.stage(0)
         total.run(early, early + tick, True)
-        cube.stage(0)
         total.run(early + tick, early + 2 * tick)
         late_d.wait()
         done_out = []
@@ -1512,6 +1510,7 @@
         for s in range(1, p.bits):
             cube.stage(s)
         total.run(early + 3 * tick, early + 4 * tick)
+        total.run(early + 4 * tick, early + 5 * tick)
         for at, value in cube.results():
             gtok[:, at] = value
         gmid_load.wait()
@@ -1535,9 +1534,8 @@
         vec.buf[0, 2:3, pl.ds(pl.multiple_of(half + p.m * ch, LANE), ch)] = dgain[:, ch:]
         vec.buf[0, 3:4, here] = dbound[...]
         vec.twins()
-        total.run(early + 4 * tick, early + 5 * tick)
+        total.run(early + 5 * tick, total.steps)
         vec.cube()
-        total.run(early + 5 * tick, total.steps)
         for b in range(total.blocks):
             for s in range(max(1, total.blocks - b), p.bits):
                 spread(b).stage(s)

time: 478 us -> 473 us (0.990)
    pallas_call x1, Pallas kernels: 143 us -> 138 us  [mixer_forward(): pl.pallas_call(functools.partial(mixer_kernel, n_dp, n_mp), out_shape=(bf...]
where the time goes in v5:
time: 473 us; the launch traced here: 465 us
  Pallas kernels  464 us (98%)
    pallas_call x1, Pallas kernels, mixer_forward(): pl.pallas_call(functools.partial(mixer_kernel, n_dp, n_mp), out_shape=(bf...  138 us
    pallas_call x1, Pallas kernels, ffn_first(): pl.pallas_call(functools.partial(first_kernel, n_dp, n_mp), out_shape=(ja...  112 us
    pallas_call x1, Pallas kernels, project_back(): pl.pallas_call(functools.partial(project_kernel, n_dp, n_mp), out_shape=(...  105 us
    pallas_call x1, Pallas kernels, ffn_last(): pl.pallas_call(functools.partial(last_kernel, n_dp, n_mp), out_shape=(jax...  97.3 us
    pallas_call x1, Pallas kernels, results(): pl.pallas_call(functools.partial(result_kernel, n_mp), out_shape=(jax.Sha...  12 us

profile of v5, /device:TPU:8, one launch (start us, length us, event | category | flops | bytes accessed | tf_op | source)
XLA Modules:
  0.0 464.6 jit_solution(10534276158191036934)
XLA Ops:
  0.6 138.0 %mixer_forward.1 = (bf16[960,2048]{1,0:T(8,128)(2,1)}, f32[240,1]{1,0:T(8,128)}, f32[960,512]{1,0:T(8,128)}, f32[960,512]{1,0:T(8,128)}, f32[960,512]{1,0:T(8,12...) custom-call(bf16[256,2048]{1,0:T(8,128)(2,1)} %w_in.1, ...), custom_call_target="tpu_custom_call" | custom-call | tf_op jit(solution)/shard_map/mixer_forward/pallas_call | solution.py:991
  138.6 111.7 %ffn_first.1 = (f32[3,256,640]{2,1,0:T(8,128)}, f32[240,2048]{1,0:T(8,128)}, f32[240,2048]{1,0:T(8,128)}, bf16[2,2048,768]{2,1,0:T(8,128)(2,1)}, bf16[768,2048]{...) custom-call(bf16[960,2048]{1,0:T(8,128)(2,1)} %get-tuple-element.64.ffn_in, ...), custom_call_target="tpu_custom_call" | custom-call | tf_op jit(solution)/shard_map/ffn_first/pallas_call | solution.py:1314
  250.3 97.3 %ffn_last.1 = (f32[3,256,768]{2,1,0:T(8,128)}, f32[240,2048]{1,0:T(8,128)}, bf16[2,240,1024]{2,1,0:T(8,128)(2,1)}, f32[240,2048]{1,0:T(8,128)}, f32[1,2048]{1,0:...) custom-call(bf16[960,2048]{1,0:T(8,128)(2,1)} %get-tuple-element.64.ffn_in, ...), custom_call_target="tpu_custom_call" | custom-call | tf_op jit(solution)/shard_map/ffn_last/pallas_call | solution.py:1351
  347.6 104.7 %project_back.1 = (bf16[4,4,256,512]{3,2,1,0:T(8,128)(2,1)}, f32[240,2048]{1,0:T(8,128)}, f32[4,2048]{1,0:T(4,128)}, bf16[240,2048]{1,0:T(8,128)(2,1)}) custom-call(bf16[960,2048]{1,0:T(8,128)(2,1)} %get-tuple-element.62.normed, bf16[960,2048]{1,0:T(8,128)(2,1)} %get-tuple-element.63.mixed, bf16[960,512]{1,0:T(8,128)(2,1)} %bitcast.16, ...), custom_call_target="tpu_custom_call" | custom-call | tf_op jit(solution)/shard_map/project_back/pallas_call | solution.py:1563
  452.4 12.0 %results.1 = (bf16[240,2048]{1,0:T(8,128)(2,1)}, f32[240,2048]{1,0:T(8,128)}, f32[1,256]{1,0:T(1,128)}, f32[256,2048]{1,0:T(8,128)}, f32[256,2048]{1,0:T(8,128)}...) custom-call(bf16[4,4,256,512]{3,2,1,0:T(8,128)(2,1)} %get-tuple-elem, ...), custom_call_target="tpu_custom_call" | custom-call | tf_op jit(solution)/shard_map/results/pallas_call | solution.py:1655
